TPU v7x, 32 devices: a whole 2x2x4 slice. The times are simulated.
32 devices in a mesh: grp: 4 (over y, x), dev: 8 (over z, core).
Axes of the slice: x: 2, y: 2, z: 4, core: 2. Of those that a mesh axis runs over, the one named last changes fastest.
Arguments:
- displacement: float32 [3, 16, 32, 32], P(None, 'dev')
- external_force: float32 [3, 16, 32, 32], P(None, 'dev'), may hold values from -6 to 6
- element_sample: int32 [16, 32, 32], P('dev'), may hold values from 0 to 31, as said below
- lame_field: bfloat16 [32, 32, 1024], P('grp', 'dev'), may hold values from 0.5 to 2
- shear_field: bfloat16 [32, 32, 1024], P('grp', 'dev'), may hold values from 0.29882812 to 3
- plastic_steps: int32 [32], replicated, may hold values from 1 to 4
- owner_slot: int32 [32], replicated, may hold values from 0 to 7, as said below
Outputs:
- displacement_next: float32 [3, 16, 32, 32], P(None, 'dev')
- sample_response: float32 [32, 8], P(('grp', 'dev'))
- micro_strain: float32 [6, 32, 32, 1024], P(None, 'grp', 'dev')
Inputs may be any that keep to these rules, and one draw needn't show every extreme that they name: `element_sample`: every value from 0 to 31 is taken by at least one element. `owner_slot`: within each aligned block of 8 RVEs a permutation of 0 to 7; slot s of a block belongs to the block's owner s.
All inputs are finite; a program needn't handle non-finite values.
Results may differ from a plain program's by a relative error of at most 0.0009.
Values may be sent and summed in bfloat16 or wider, within the bound.
No kernel may reach another device: no remote copies, remote signals or barrier semaphores. Data moves between devices by JAX's collectives and lax.ppermute only.
A program may use at most 64 MiB of HBM per device.

v0:
```python
import jax
import jax.numpy as jnp
from jax import lax
from jax.sharding import PartitionSpec as P

VOX = 32
CG_STEPS = 3


shear_ref = 1.65
lame_ref = 1.25
green_ratio = (lame_ref + shear_ref) / (lame_ref + 2.0 * shear_ref)
relax_rate = 0.35
flow_scale = 4.0
spring_rate = 0.2
highest = lax.Precision.HIGHEST


def shifted_2(block, axis, distance):
    devices = range(lax.axis_size(axis))
    route = [(i - distance, i) for i in devices if i - distance in devices]
    return lax.ppermute(block, axis, route)


def wave_at(count, index):
    angle = 2.0 * jnp.pi / count * index.astype(jnp.float32)
    return jnp.where(index % (count // 2) == 0, 0.0, jnp.sin(angle))


def inverse_square(first, second, third):
    square = first * first + second * second + third * third
    live = square > 0.0
    return jnp.where(live, 1.0 / jnp.where(live, square, 1.0), 0.0)


def green_parts(parts, first, second, third, inverse):
    xx, yy, zz, yz, xz, xy = parts
    along_first = xx * first + xy * second + xz * third
    along_second = xy * first + yy * second + yz * third
    along_third = xz * first + yz * second + zz * third
    inner = first * along_first + second * along_second + third * along_third
    scaled = green_ratio * inner * inverse
    push_first = (along_first - scaled * first) * inverse / shear_ref
    push_second = (along_second - scaled * second) * inverse / shear_ref
    push_third = (along_third - scaled * third) * inverse / shear_ref
    return (
        first * push_first,
        second * push_second,
        third * push_third,
        0.5 * (second * push_third + third * push_second),
        0.5 * (first * push_third + third * push_first),
        0.5 * (first * push_second + second * push_first),
    )


def measure(stress):
    return (
        stress[0] * stress[0]
        + stress[1] * stress[1]
        + stress[2] * stress[2]
        + 2.0 * (stress[3] * stress[3] + stress[4] * stress[4] + stress[5] * stress[5])
    )


def material(strain, lame, shear, steps, bound):
    trace = strain[0] + strain[1] + strain[2]
    third_trace = trace / 3.0
    deviator = jnp.concatenate([strain[:3] - third_trace, strain[3:]])

    def relax(count, plastic):
        ratio = measure(2.0 * shear * (deviator - plastic)) / flow_scale
        moved = plastic + relax_rate * (deviator - plastic) * (ratio / (1.0 + ratio))
        return jnp.where(count < steps, moved, plastic)

    plastic = lax.fori_loop(0, bound, relax, jnp.zeros_like(deviator))
    elastic = strain - plastic
    stress = jnp.concatenate([2.0 * shear * elastic[:3] + lame * trace, 2.0 * shear * elastic[3:]])
    ratio = measure(2.0 * shear * (deviator - plastic)) / flow_scale
    return (stress, ratio)


def dft_tables(count):
    index = jnp.arange(count, dtype=jnp.int32)
    phase = index[:, None] * index[None, :] % count
    angle = 2.0 * jnp.pi / count * phase.astype(jnp.float32)
    return (jnp.cos(angle), jnp.sin(angle))


def last_axis(field, matrix):
    return jnp.einsum("...n,kn->...k", field, matrix, precision=highest)


def inner_axis(field, matrix):
    return jnp.einsum("...nm,kn->...km", field, matrix, precision=highest)


def forward(real, imag, table, contract):
    cosine, sine = table
    return (
        contract(real, cosine) + contract(imag, sine),
        contract(imag, cosine) - contract(real, sine),
    )


def backward(real, imag, table, contract):
    cosine, sine = table
    count = cosine.shape[0]
    return (
        (contract(real, cosine) - contract(imag, sine)) / count,
        (contract(imag, cosine) + contract(real, sine)) / count,
    )


def plane_forward(field, table):
    cube = field.reshape(field.shape[:-1] + (VOX, VOX))
    cosine, sine = table
    real = last_axis(cube, cosine)
    imag = -last_axis(cube, sine)
    real, imag = forward(real, imag, table, inner_axis)
    return jnp.stack([real, imag]).reshape((2,) + field.shape)


def plane_backward(spectrum, table):
    cube = spectrum.reshape(spectrum.shape[:-1] + (VOX, VOX))
    real, imag = backward(cube[0], cube[1], table, inner_axis)
    cosine, sine = table
    result = (last_axis(real, cosine) - last_axis(imag, sine)) / VOX
    return result.reshape(spectrum.shape[1:])


def spectral_green(stacked, first, second, third, inverse):
    parts = tuple((stacked[:, part] for part in range(6)))
    return jnp.stack(green_parts(parts, first, second, third, inverse), axis=1)


def cube_micro(item, table, first, second, third, inverse):
    lame_low, shear_low, count, load = item
    lame = lame_low.astype(jnp.float32)
    shear = shear_low.astype(jnp.float32)
    strain = jnp.broadcast_to(load[:, None, None], (6,) + lame.shape)
    stress, ratio = material(strain, lame, shear, count, count)
    spectrum = plane_forward(stress, table)
    real, imag = forward(spectrum[0], spectrum[1], table, inner_axis)
    pushed = spectral_green(jnp.stack([real, imag]), first, second, third, inverse)
    real, imag = backward(pushed[0], pushed[1], table, inner_axis)
    strain = strain - plane_backward(jnp.stack([real, imag]), table)
    stress, ratio = material(strain, lame, shear, count, count)
    response = (
        jnp.concatenate(
            [
                jnp.sum(stress, axis=(1, 2)),
                jnp.sum(lame)[None],
                jnp.sum(shear / (1.0 + ratio))[None],
            ]
        )
        / VOX**3
    )
    return (strain, response)


def shifted(field, axis, upward):
    extent = field.shape[axis]
    zero = jnp.zeros_like(lax.slice_in_dim(field, 0, 1, axis=axis))
    if upward:
        return jnp.concatenate([lax.slice_in_dim(field, 1, extent, axis=axis), zero], axis=axis)
    return jnp.concatenate([zero, lax.slice_in_dim(field, 0, extent - 1, axis=axis)], axis=axis)


def average_next(field, axis):
    return 0.5 * (field + shifted(field, axis, True))


def differ_next(field, axis):
    return shifted(field, axis, True) - field


def average_back(field, axis):
    return 0.5 * (field + shifted(field, axis, False))


def differ_back(field, axis):
    return shifted(field, axis, False) - field


def assemble(slope_x, slope_y, slope_z):
    return jnp.stack(
        [
            slope_x[0],
            slope_y[1],
            slope_z[2],
            0.5 * (slope_y[2] + slope_z[1]),
            0.5 * (slope_x[2] + slope_z[0]),
            0.5 * (slope_x[1] + slope_y[0]),
        ]
    )


def strain_local(field):
    following = shifted_2(field[:, :1], "dev", -1)
    extended = jnp.concatenate([field, following], axis=1)
    smooth_z = average_next(extended, 3)
    both = average_next(smooth_z, 2)
    slope_x = both[:, 1:] - both[:, :-1]
    along_y = differ_next(smooth_z, 2)
    slope_y = 0.5 * (along_y[:, :-1] + along_y[:, 1:])
    along_z = average_next(differ_next(extended, 3), 2)
    slope_z = 0.5 * (along_z[:, :-1] + along_z[:, 1:])
    return assemble(slope_x, slope_y, slope_z)


def force_local(stress):
    xx, yy, zz, yz, xz, xy = stress
    along_x = jnp.stack([xx, xy, xz])
    along_y = jnp.stack([xy, yy, yz])
    along_z = jnp.stack([xz, yz, zz])
    first = average_back(average_back(along_x, 3), 2)
    rest = differ_back(average_back(along_y, 3), 2) + average_back(differ_back(along_z, 3), 2)
    previous = shifted_2(jnp.stack([first[:, -1:], rest[:, -1:]]), "dev", 1)
    first_ext = jnp.concatenate([previous[0], first], axis=1)
    rest_ext = jnp.concatenate([previous[1], rest], axis=1)
    return first_ext[:, :-1] - first_ext[:, 1:] + 0.5 * (rest_ext[:, 1:] + rest_ext[:, :-1])


def stiffness(field, lame_cells, shear_cells):
    strain = strain_local(field)
    trace = strain[0] + strain[1] + strain[2]
    stress = jnp.concatenate(
        [2.0 * shear_cells * strain[:3] + lame_cells * trace, 2.0 * shear_cells * strain[3:]]
    )
    return force_local(stress) + spring_rate * field


def shards(
    displacement, external_force, element_sample, lame_field, shear_field, plastic_steps, owner_slot
):
    samples = plastic_steps.shape[0]
    group_size = lame_field.shape[0]
    devices = lax.axis_size("dev")
    rank = lax.axis_index("dev")
    group = lax.axis_index("grp")
    local_count = group_size // devices
    table = dft_tables(VOX)
    element_strain = strain_local(displacement)
    flat_sample = element_sample.reshape(-1)
    indicator = (flat_sample[:, None] == jnp.arange(samples, dtype=jnp.int32)[None, :]).astype(
        jnp.float32
    )
    sums = jnp.dot(element_strain.reshape(6, -1), indicator, precision=highest)
    counts = jnp.sum(indicator, axis=0)
    sums, counts = lax.psum((sums, counts), "dev")
    loads = sums / counts
    start = group * group_size
    group_steps = lax.dynamic_slice_in_dim(plastic_steps, start, group_size)
    group_slots = lax.dynamic_slice_in_dim(owner_slot, start, group_size)
    group_loads = lax.dynamic_slice_in_dim(loads, start, group_size, axis=1)
    order = jnp.argsort(group_slots)
    own_slots = rank * local_count + jnp.arange(local_count, dtype=jnp.int32)
    lame_own, shear_own = (
        lax.all_to_all(lame_field, "dev", split_axis=0, concat_axis=1, tiled=True),
        lax.all_to_all(shear_field, "dev", split_axis=0, concat_axis=1, tiled=True),
    )
    own_steps = lax.dynamic_slice_in_dim(group_steps, rank * local_count, local_count)
    own_loads = lax.dynamic_slice_in_dim(group_loads, rank * local_count, local_count, axis=1)
    column = jnp.arange(VOX * VOX, dtype=jnp.int32)
    first = wave_at(VOX, jnp.arange(VOX, dtype=jnp.int32))[:, None]
    second = wave_at(VOX, column // VOX)[None, :]
    third = wave_at(VOX, column % VOX)[None, :]
    inverse = inverse_square(first, second, third)

    def solve_one(item):
        return cube_micro(item, table, first, second, third, inverse)

    strains, local_rows = lax.map(solve_one, (lame_own, shear_own, own_steps, own_loads.T))
    moved = lax.all_to_all(strains, "dev", split_axis=2, concat_axis=0, tiled=True)
    gathered = lax.all_gather(local_rows, ("grp", "dev"), axis=0, tiled=True)
    micro_strain = jnp.transpose(moved, (1, 0, 2, 3))
    own_rows = jnp.take(gathered, start + jnp.take(order, own_slots), axis=0)
    element_table = jnp.dot(indicator, gathered, precision=highest)
    fields = element_table.T.reshape((8,) + displacement.shape[1:])
    element_stress = fields[:6]
    lame_cells = fields[6]
    shear_cells = fields[7]
    residual = external_force - force_local(element_stress) - spring_rate * displacement

    def squared(field):
        return lax.psum(jnp.sum(field * field), "dev")

    update = jnp.zeros_like(displacement)
    remainder = residual
    direction = residual
    norm_now = squared(remainder)
    for turn in range(CG_STEPS):
        image = stiffness(direction, lame_cells, shear_cells)
        alpha = norm_now / lax.psum(jnp.sum(direction * image), "dev")
        update = update + alpha * direction
        remainder = remainder - alpha * image
        if turn + 1 < CG_STEPS:
            norm_next = squared(remainder)
            direction = remainder + norm_next / norm_now * direction
            norm_now = norm_next
    return (displacement + update, own_rows, micro_strain)


def solution(mesh):
    in_specs = (
        P(None, "dev", None, None),
        P(None, "dev", None, None),
        P("dev", None, None),
        P("grp", "dev", None),
        P("grp", "dev", None),
        P(),
        P(),
    )
    out_specs = (P(None, "dev", None, None), P(("grp", "dev"), None), P(None, "grp", "dev", None))
    return jax.shard_map(shards, mesh=mesh, in_specs=in_specs, out_specs=out_specs, check_vma=False)
```

profile of v0, /device:TPU:5, one launch (start us, length us, event | category | flops | bytes accessed | tf_op | source)
XLA Modules:
  0.0 335.3 jit_solution(13572445268814090399)
XLA Ops:
  1.4 2.6 collective-permute-start
  4.0 5.0 %all-to-all-start = ((bf16[8,4,1024]{2,1,0:T(4,128)(2,1)}), bf16[8,4,1024]{2,1,0:T(4,128)(2,1)S(1)}, u32[]{:S(2)}, u32[]{:S(2)}) async-start(bf16[8,4,1024]{2,1,0:T(4,128)(2,1)} %param.15), calls=%async_computation | async-start | bytes 131072 | tf_op jit(solution)/shard_map/all_to_all | solution.py:260
  15.6 25.2 %all-reduce.37 = (f32[6,32]{0,1:T(8,128)S(1)}, f32[32]{0:T(128)S(1)}) all-reduce(f32[6,32]{0,1:T(8,128)S(1)} %fusion.62, f32[32]{0:T(128)S(1)} %convert_reduce_fusion), channel_id=1, replica_groups=mesh['grp'=4,'dev'=8] {'dev'}, use_global_device_ids=true, to_apply=%region_0.1 | all-reduce | flops 224 | bytes 1792 | tf_op jit(solution)/shard_map/psum | solution.py:250
  45.5 7.4 %all-to-all-start.1 = ((bf16[8,4,1024]{2,1,0:T(4,128)(2,1)}), bf16[8,4,1024]{2,1,0:T(4,128)(2,1)S(1)}, u32[]{:S(2)}, u32[]{:S(2)}) async-start(bf16[8,4,1024]{2,1,0:T(4,128)(2,1)} %param.14), calls=%async_computation.1 | async-start | bytes 131072 | tf_op jit(solution)/shard_map/all_to_all | solution.py:259
  53.1 6.1 %while.33 = (s32[]{:T(128)}, f32[6,32,1024]{2,1,0:T(8,128)S(1)}, s32[]{:T(128)}, f32[6,32,1024]{2,1,0:T(8,128)S(1)}, f32[32,1024]{1,0:T(8,128)S(1)}, /*index=5*/s32[]{:T(128)}) while((s32[]{:T(128)}, f32[6,32,1024]{2,1,0:T(8,128)S(1)}, s32[]{:T(128)}, f32[6,32,1024]{2,1,0:T(8,128)S(1)}, f32[32,1024]{1,0:T(8,128)S(1)}, ...), condition=%wide.region_4.5_spmd, body=%wide.region_3.4_spmd.sunk | while | flops 1540099 | bytes 6946895 | solution.py:75
  63.5 2.8 fusion.143
  66.3 2.8 fusion.133
  69.1 3.0 fusion.141
  72.0 4.5 %fusion.130 = f32[32,6,32,32]{3,0,2,1:T(8,128)} fusion(f32[6,32,32,32]{3,2,1,0:T(8,128)S(1)} %fusion.143), kind=kOutput, calls=%fused_computation.348 | convolution fusion | flops 75511808 | bytes 1572864 | tf_op jit(solution)/shard_map/while/body/eval_jaxpr/...nm,kn->...km/dot_general | solution.py:94
  76.5 5.0 %add_bitcast_fusion = f32[6,32,32,32]{3,2,1,0:T(8,128)} fusion(f32[32,6,32,32]{3,0,2,1:T(8,128)S(1)} %fusion.141, f32[6,32,32,32]{3,2,1,0:T(8,128)S(1)} %fusion.133), kind=kOutput, calls=%fused_computation.48 | convolution fusion | flops 75905024 | bytes 2359296 | tf_op jit(solution)/shard_map/while/body/eval_jaxpr/...nm,kn->...km/dot_general | solution.py:94
  81.5 3.8 %squeeze.122 = f32[6,32,1024]{2,1,0:T(8,128)} reshape(f32[6,32,32,32]{3,2,1,0:T(8,128)} %add_bitcast_fusion) | data formatting | bytes 1572864 | tf_op jit(solution)/shard_map/while/body/eval_jaxpr/squeeze | solution.py:143
  85.3 2.9 fusion.149
  88.2 5.5 %subtract_bitcast_fusion = f32[6,32,32,32]{3,2,1,0:T(8,128)} fusion(f32[32,6,32,32]{3,0,2,1:T(8,128)} %fusion.130, f32[6,32,32,32]{3,2,1,0:T(8,128)S(1)} %copy-done.3), kind=kOutput, calls=%fused_computation.47 | convolution fusion | flops 75905024 | bytes 2359296 | tf_op jit(solution)/shard_map/while/body/eval_jaxpr/...nm,kn->...km/dot_general | solution.py:94
  93.7 3.3 squeeze.123
  107.4 4.5 %fusion.126 = f32[32,6,32,32]{3,0,2,1:T(8,128)} fusion(f32[6,32,32,32]{3,2,1,0:T(8,128)S(1)} %squeeze.126), kind=kOutput, calls=%fused_computation.344 | convolution fusion | flops 75511808 | bytes 1572864 | tf_op jit(solution)/shard_map/while/body/eval_jaxpr/...nm,kn->...km/dot_general | solution.py:94
  111.9 4.5 %fusion.138 = f32[32,6,32,32]{3,0,2,1:T(8,128)} fusion(f32[6,32,32,32]{3,2,1,0:T(8,128)S(1)} %squeeze.126), kind=kOutput, calls=%fused_computation.356 | convolution fusion | flops 75511808 | bytes 1572864 | tf_op jit(solution)/shard_map/while/body/eval_jaxpr/...nm,kn->...km/dot_general | solution.py:94
  120.4 2.9 fusion.135
  123.4 2.9 fusion.128
  126.3 2.8 fusion.18
  129.2 2.8 subtract_multiply_fusion
  141.4 6.1 %while.34 = (s32[]{:T(128)}, f32[6,32,1024]{2,1,0:T(8,128)S(1)}, s32[]{:T(128)}, f32[6,32,1024]{2,1,0:T(8,128)S(1)}, f32[32,1024]{1,0:T(8,128)S(1)}, /*index=5*/s32[]{:T(128)}) while((s32[]{:T(128)}, f32[6,32,1024]{2,1,0:T(8,128)S(1)}, s32[]{:T(128)}, f32[6,32,1024]{2,1,0:T(8,128)S(1)}, f32[32,1024]{1,0:T(8,128)S(1)}, ...), condition=%wide.region_6.7_spmd, body=%wide.region_5.6_spmd.sunk | while | flops 1540099 | bytes 6946895 | solution.py:75
  151.5 44.3 %all-gather = f32[32,1,8]{2,1,0:T(1,128)S(1)} all-gather(f32[1,1,8]{2,1,0:T(1,128)S(1)} %fusion.201), channel_id=1, replica_groups=mesh['grp'=4,'dev'=8] {'grp','dev'}, dimensions={0}, use_global_device_ids=true | all-gather | bytes 1056 | tf_op jit(solution)/shard_map/all_gather | solution.py:275
  202.6 4.1 %collective-permute-done.2 = f32[3,1,32,32]{3,2,0,1:T(8,128)S(1)} collective-permute-done((f32[3,1,32,32]{3,2,0,1:T(8,128)S(1)}, f32[3,1,32,32]{3,2,0,1:T(8,128)S(1)}, u32[]{:S(2)}, u32[]{:S(2)}) %collective-permute-start.2) | collective-permute-done | bytes 12320 | tf_op jit(solution)/shard_map/ppermute | solution.py:22
  213.9 14.7 %all-reduce.36 = (f32[]{:T(128)}, f32[]{:T(128)}) all-reduce(f32[]{:T(128)} %get-tuple-element.125, f32[]{:T(128)} %get-tuple-element.124), channel_id=1, replica_groups=mesh['grp'=4,'dev'=8] {'dev'}, use_global_device_ids=true, to_apply=%region_11.12 | all-reduce | flops 2 | bytes 16 | tf_op jit(solution)/shard_map/psum | solution.py:286
  230.6 14.2 %psum.60 = f32[]{:T(128)} all-reduce(f32[]{:T(128)} %get-tuple-element.162), channel_id=1, replica_groups=mesh['grp'=4,'dev'=8] {'dev'}, use_global_device_ids=true, to_apply=%region_15.16 | all-reduce | flops 1 | bytes 8 | tf_op jit(solution)/shard_map/psum | solution.py:286
  248.8 2.9 collective-permute-done.4
  258.3 13.4 %psum.61 = f32[]{:T(128)} all-reduce(f32[]{:T(128)} %multiply_reduce_fusion.1), channel_id=1, replica_groups=mesh['grp'=4,'dev'=8] {'dev'}, use_global_device_ids=true, to_apply=%region_17.18 | all-reduce | flops 1 | bytes 8 | tf_op jit(solution)/shard_map/psum | solution.py:294
  273.6 4.8 %all-to-all-start.2 = ((f32[1,6,32,1024]{3,0,1,2:T(1,128)}), f32[1,6,32,1024]{3,0,1,2:T(1,128)S(1)}, u32[]{:S(2)}, u32[]{:S(2)}) async-start(f32[1,6,32,1024]{3,0,1,2:T(1,128)} %copy.300), calls=%async_computation.2 | async-start | bytes 1572864 | tf_op jit(solution)/shard_map/all_to_all | solution.py:274
  278.4 24.8 %psum.62 = f32[]{:T(128)} all-reduce(f32[]{:T(128)} %multiply_reduce_fusion), channel_id=1, replica_groups=mesh['grp'=4,'dev'=8] {'dev'}, use_global_device_ids=true, to_apply=%region_19.20 | all-reduce | flops 1 | bytes 8 | tf_op jit(solution)/shard_map/psum | solution.py:286
  304.6 2.9 collective-permute-start.6
  307.5 2.8 collective-permute-done.6
  317.3 14.2 %psum.63 = f32[]{:T(128)} all-reduce(f32[]{:T(128)} %fusion.79), channel_id=1, replica_groups=mesh['grp'=4,'dev'=8] {'dev'}, use_global_device_ids=true, to_apply=%region_21.22 | all-reduce | flops 1 | bytes 8 | tf_op jit(solution)/shard_map/psum | solution.py:294
  (300 shorter events, 77.7 us)
Async XLA Ops:
  1.4 12.9 %collective-permute-start = (f32[3,1,32,32]{3,2,0,1:T(8,128)S(1)}, f32[3,1,32,32]{3,2,0,1:T(8,128)S(1)}, u32[]{:S(2)}, u32[]{:S(2)}) collective-permute-start(f32[3,1,32,32]{3,2,0,1:T(8,128)S(1)} %copy.342), channel_id=1, source_target_pairs={{1,0},{2,1},{3,2},{4,3},{5,4},{6,5},{7,6},{9,8},{10,9},{11,10},{12... | collective-permute-start | bytes 36872 | tf_op jit(solution)/shard_map/ppermute | solution.py:22
  4.0 41.5 %all-to-all-start = ((bf16[8,4,1024]{2,1,0:T(4,128)(2,1)}), bf16[8,4,1024]{2,1,0:T(4,128)(2,1)S(1)}, u32[]{:S(2)}, u32[]{:S(2)}) async-start(bf16[8,4,1024]{2,1,0:T(4,128)(2,1)} %param.15), calls=%async_computation | async-start | bytes 131072 | tf_op jit(solution)/shard_map/all_to_all | solution.py:260
  45.4 14.6 %copy-start.30 = (f32[6]{0:T(128)}, f32[6]{0:T(128)S(1)}, u32[]{:S(2)}) copy-start(f32[6]{0:T(128)S(1)} %fusion.309) | copy-start | bytes 76
  45.5 7.5 %copy-start.16 = (bf16[8,4,1024]{2,1,0:T(4,128)(2,1)}, bf16[8,4,1024]{2,1,0:T(4,128)(2,1)S(1)}, u32[]{:S(2)}) copy-start(bf16[8,4,1024]{2,1,0:T(4,128)(2,1)S(1)} %all-to-all-done) | copy-start | bytes 196612
  45.5 13.7 %all-to-all-start.1 = ((bf16[8,4,1024]{2,1,0:T(4,128)(2,1)}), bf16[8,4,1024]{2,1,0:T(4,128)(2,1)S(1)}, u32[]{:S(2)}, u32[]{:S(2)}) async-start(bf16[8,4,1024]{2,1,0:T(4,128)(2,1)} %param.14), calls=%async_computation.1 | async-start | bytes 131072 | tf_op jit(solution)/shard_map/all_to_all | solution.py:259
  69.0 7.5 %copy-start.2 = (f32[6,32,32,32]{3,2,1,0:T(8,128)}, f32[6,32,32,32]{3,2,1,0:T(8,128)S(1)}, u32[]{:S(2)}) copy-start(f32[6,32,32,32]{3,2,1,0:T(8,128)S(1)} %fusion.133) | copy-start | bytes 2359300
  81.5 6.7 %copy-start.3 = (f32[6,32,32,32]{3,2,1,0:T(8,128)S(1)}, f32[6,32,32,32]{3,2,1,0:T(8,128)}, u32[]{:S(2)}) copy-start(f32[6,32,32,32]{3,2,1,0:T(8,128)} %copy-done.2) | copy-start | bytes 2359300
  93.7 4.2 %copy-start.13 = (f32[32,6,1024]{2,0,1:T(8,128)S(1)}, f32[32,6,1024]{2,0,1:T(8,128)}, u32[]{:S(2)}) copy-start(f32[32,6,1024]{2,0,1:T(8,128)} %fusion.149) | copy-start | bytes 2359300
  93.7 5.1 %copy-start.9 = (f32[6,32,1024]{2,1,0:T(8,128)S(1)}, f32[6,32,1024]{2,1,0:T(8,128)}, u32[]{:S(2)}) copy-start(f32[6,32,1024]{2,1,0:T(8,128)} %squeeze.122) | copy-start | bytes 2359300
  111.9 4.5 %copy-start.7 = (f32[2,6,32,1024]{3,2,1,0:T(8,128)S(1)}, f32[2,6,32,1024]{3,2,1,0:T(8,128)}, u32[]{:S(2)}) copy-start(f32[2,6,32,1024]{3,2,1,0:T(8,128)} %copy-done.6) | copy-start | bytes 4718596
  111.9 4.5 %copy-start.12 = (f32[32,6,1024]{2,0,1:T(8,128)S(1)}, f32[32,6,1024]{2,0,1:T(8,128)}, u32[]{:S(2)}) copy-start(f32[32,6,1024]{2,0,1:T(8,128)} %fusion.45) | copy-start | bytes 2359300
  123.3 3.0 copy-start.5
  126.3 2.9 copy-start.4
  132.0 7.2 %copy-start = (f32[6,32,32,32]{3,2,1,0:T(8,128)}, f32[6,32,32,32]{3,2,1,0:T(8,128)S(1)}, u32[]{:S(2)}) copy-start(f32[6,32,32,32]{3,2,1,0:T(8,128)S(1)} %subtract_multiply_fusion) | copy-start | bytes 2359300
  132.0 4.7 %copy-start.19 = (bf16[8,4,1024]{2,1,0:T(4,128)(2,1)S(1)}, bf16[8,4,1024]{2,1,0:T(4,128)(2,1)}, u32[]{:S(2)}) copy-start(bf16[8,4,1024]{2,1,0:T(4,128)(2,1)} %copy-done.18) | copy-start | bytes 196612
  141.4 6.2 %copy-start.8 = (f32[6,32,1024]{2,1,0:T(8,128)S(1)}, f32[6,32,1024]{2,1,0:T(8,128)}, u32[]{:S(2)}) copy-start(f32[6,32,1024]{2,1,0:T(8,128)} %reshape.438) | copy-start | bytes 2359300
  149.2 51.5 %copy-start.15 = (f32[3,2,32,32]{3,2,1,0:T(8,128)S(1)}, f32[3,2,32,32]{3,2,1,0:T(8,128)}, u32[]{:S(2)}) copy-start(f32[3,2,32,32]{3,2,1,0:T(8,128)} %param.11) | copy-start | bytes 73732
  149.2 51.4 %copy-start.26 = (f32[3,2,32,32]{3,2,1,0:T(8,128)S(1)}, f32[3,2,32,32]{3,2,1,0:T(8,128)}, u32[]{:S(2)}) copy-start(f32[3,2,32,32]{3,2,1,0:T(8,128)} %param.12) | copy-start | bytes 73732
  195.8 3.3 copy-start.27
  197.1 3.5 %collective-permute-start.1 = (f32[2,3,1,32,32]{4,3,1,2,0:T(8,128)S(1)}, f32[2,3,1,32,32]{4,3,1,2,0:T(8,128)S(1)}, u32[]{:S(2)}, u32[]{:S(2)}) collective-permute-start(f32[2,3,1,32,32]{4,3,1,2,0:T(8,128)S(1)} %pad_maximum_fusion.13), channel_id=1, source_target_pairs={{0,1},{1,2},{2,3},{3,4},{4,5},{5,6},{6,7},{8,9},{9,10},{10,11},{11... | collective-permute-start | bytes 73736 | tf_op jit(solution)/shard_map/ppermute | solution.py:22
  199.1 8.2 %copy-start.23 = (f32[1,2,32,32]{3,2,1,0:T(8,128)}, f32[1,2,32,32]{3,2,1,0:T(8,128)S(1)}, u32[]{:S(2)}) copy-start(f32[1,2,32,32]{3,2,1,0:T(8,128)S(1)} %squeeze.130) | copy-start | bytes 24580
  199.1 8.1 %copy-start.20 = (f32[2,32,32]{2,1,0:T(8,128)}, f32[2,32,32]{2,1,0:T(8,128)S(1)}, u32[]{:S(2)}) copy-start(f32[2,32,32]{2,1,0:T(8,128)S(1)} %mul.1363) | copy-start | bytes 24580
  200.7 6.1 %collective-permute-start.2 = (f32[3,1,32,32]{3,2,0,1:T(8,128)S(1)}, f32[3,1,32,32]{3,2,0,1:T(8,128)S(1)}, u32[]{:S(2)}, u32[]{:S(2)}) collective-permute-start(f32[3,1,32,32]{3,2,0,1:T(8,128)S(1)} %copy.343), channel_id=1, source_target_pairs={{1,0},{2,1},{3,2},{4,3},{5,4},{6,5},{7,6},{9,8},{10,9},{11,10},{12... | collective-permute-start | bytes 36872 | tf_op jit(solution)/shard_map/ppermute | solution.py:22
  206.9 3.2 copy-start.1
  208.2 4.2 %collective-permute-start.3 = (f32[2,3,1,32,32]{4,3,1,2,0:T(8,128)}, f32[2,3,1,32,32]{4,3,1,2,0:T(8,128)}, u32[]{:S(2)}, u32[]{:S(2)}) collective-permute-start(f32[2,3,1,32,32]{4,3,1,2,0:T(8,128)} %pad_maximum_fusion.17), channel_id=1, source_target_pairs={{0,1},{1,2},{2,3},{3,4},{4,5},{5,6},{6,7},{8,9},{9,10},{10,11},{11... | collective-permute-start | bytes 73736 | tf_op jit(solution)/shard_map/ppermute | solution.py:22
  212.4 39.5 %copy-start.24 = (f32[1,2,32,32]{3,2,1,0:T(8,128)S(1)}, f32[1,2,32,32]{3,2,1,0:T(8,128)}, u32[]{:S(2)}) copy-start(f32[1,2,32,32]{3,2,1,0:T(8,128)} %copy-done.23) | copy-start | bytes 24580
  212.4 39.6 %copy-start.21 = (f32[2,32,32]{2,1,0:T(8,128)S(1)}, f32[2,32,32]{2,1,0:T(8,128)}, u32[]{:S(2)}) copy-start(f32[2,32,32]{2,1,0:T(8,128)} %copy-done.20) | copy-start | bytes 24580
  246.2 5.4 %collective-permute-start.4 = (f32[3,1,32,32]{3,2,0,1:T(8,128)S(1)}, f32[3,1,32,32]{3,2,0,1:T(8,128)S(1)}, u32[]{:S(2)}, u32[]{:S(2)}) collective-permute-start(f32[3,1,32,32]{3,2,0,1:T(8,128)S(1)} %copy.344), channel_id=1, source_target_pairs={{1,0},{2,1},{3,2},{4,3},{5,4},{6,5},{7,6},{9,8},{10,9},{11,10},{12... | collective-permute-start | bytes 36872 | tf_op jit(solution)/shard_map/ppermute | solution.py:22
  252.4 3.5 %collective-permute-start.5 = (f32[2,3,1,32,32]{4,3,1,2,0:T(8,128)S(1)}, f32[2,3,1,32,32]{4,3,1,2,0:T(8,128)S(1)}, u32[]{:S(2)}, u32[]{:S(2)}) collective-permute-start(f32[2,3,1,32,32]{4,3,1,2,0:T(8,128)S(1)} %pad_maximum_fusion.21), channel_id=1, source_target_pairs={{0,1},{1,2},{2,3},{3,4},{4,5},{5,6},{6,7},{8,9},{9,10},{10,11},{11... | collective-permute-start | bytes 73736 | tf_op jit(solution)/shard_map/ppermute | solution.py:22
  273.6 59.8 %all-to-all-start.2 = ((f32[1,6,32,1024]{3,0,1,2:T(1,128)}), f32[1,6,32,1024]{3,0,1,2:T(1,128)S(1)}, u32[]{:S(2)}, u32[]{:S(2)}) async-start(f32[1,6,32,1024]{3,0,1,2:T(1,128)} %copy.300), calls=%async_computation.2 | async-start | bytes 1572864 | tf_op jit(solution)/shard_map/all_to_all | solution.py:274
  304.6 5.7 %collective-permute-start.6 = (f32[3,1,32,32]{3,2,0,1:T(8,128)S(1)}, f32[3,1,32,32]{3,2,0,1:T(8,128)S(1)}, u32[]{:S(2)}, u32[]{:S(2)}) collective-permute-start(f32[3,1,32,32]{3,2,0,1:T(8,128)S(1)} %copy.345), channel_id=1, source_target_pairs={{1,0},{2,1},{3,2},{4,3},{5,4},{6,5},{7,6},{9,8},{10,9},{11,10},{12... | collective-permute-start | bytes 36872 | tf_op jit(solution)/shard_map/ppermute | solution.py:22
  311.0 4.4 %collective-permute-start.7 = (f32[2,3,1,32,32]{4,3,1,2,0:T(8,128)S(1)}, f32[2,3,1,32,32]{4,3,1,2,0:T(8,128)S(1)}, u32[]{:S(2)}, u32[]{:S(2)}) collective-permute-start(f32[2,3,1,32,32]{4,3,1,2,0:T(8,128)S(1)} %pad_maximum_fusion.25), channel_id=1, source_target_pairs={{0,1},{1,2},{2,3},{3,4},{4,5},{5,6},{6,7},{8,9},{9,10},{10,11},{11... | collective-permute-start | bytes 73736 | tf_op jit(solution)/shard_map/ppermute | solution.py:22
  (14 other events, 30.0 us)
where the time goes:
time: 340 us; the launch traced here: 335 us
  blocking collectives  151 us (44%)
  matrix products  56 us (16%)
  starting transfers between devices  34.7 us (10%)
  local copies, waits for them, and re-layouts  32.8 us (10%)
  other arithmetic  27.7 us (8%)
  waiting for transfers between devices  12.7 us (4%)
  between operations  11.8 us (3%)
  loops' own time  8.84 us (3%)
    psum x3, blocking collectives, squared(): return lax.psum(jnp.sum(field * field), 'dev')  53.7 us
    dot_general x16, matrix products, inner_axis(): return jnp.einsum('...nm,kn->...km', field, matrix, precision=highest)  44.4 us
    all_gather x1, blocking collectives, shards(): gathered = lax.all_gather(local_rows, ('grp', 'dev'), axis=0, tiled=True)  44.3 us
    psum x2, blocking collectives, shards(): alpha = norm_now / lax.psum(jnp.sum(direction * image), 'dev')  27.5 us
    psum x1, blocking collectives, shards(): sums, counts = lax.psum((sums, counts), 'dev')  25.2 us
    ppermute x8, starting transfers between devices, shifted_2(): return lax.ppermute(block, axis, route)  17.6 us
    ppermute x8, waiting for transfers between devices, shifted_2(): return lax.ppermute(block, axis, route)  12.7 us
    dot_general x4, matrix products, last_axis(): return jnp.einsum('...n,kn->...k', field, matrix, precision=highest)  11.2 us
  transfers between devices with their start and end apart: 11, of which 5 were waited for; matrix products, arithmetic and copies ran while one was open for 6% of the time, Pallas kernels for 0%

commit v1 on v0

v1 whole, which is shorter than its diff:
```python
import functools
import jax
import jax.numpy as jnp
import numpy as np
from jax import lax
from jax.experimental import pallas as pl
from jax.experimental.pallas import tpu as pltpu
from jax.sharding import PartitionSpec as P

CG_STEPS = 3
shear_ref = 1.65
lame_ref = 1.25
green_ratio = (lame_ref + shear_ref) / (lame_ref + 2.0 * shear_ref)
relax_rate = 0.35
flow_scale = 4.0
spring_rate = 0.2
f32 = jnp.float32
bf16 = jnp.bfloat16
DIAG = ((0, 0), (1, 1), (2, 2))
PAIRS = ((0, 0), (1, 1), (2, 2), (1, 2), (0, 2), (0, 1))
SLOT = {(0, 0): 0, (1, 1): 1, (2, 2): 2, (1, 2): 3, (2, 1): 3, (0, 2): 4, (2, 0): 4, (0, 1): 5, (1, 0): 5}


def split_table(table):
    high = table.astype(np.float32).astype(bf16)
    low = (table - high.astype(np.float64)).astype(np.float32).astype(bf16)
    return np.stack([high, low])


def tables(vox):
    half = vox // 2
    n = np.arange(vox)[:, None]
    k = np.arange(half)[None, :]
    angle = 2.0 * np.pi * (n * k % vox) / vox
    cosine = np.cos(angle) * np.sqrt(2.0 / vox)
    sine = np.sin(angle) * np.sqrt(2.0 / vox)
    cosine[:, 0] = 1.0 / np.sqrt(vox)
    sine[:, 0] = (1.0 - 2.0 * (np.arange(vox) % 2)) / np.sqrt(vox)
    basis = np.concatenate([cosine, sine], axis=1)
    by_parity = basis.reshape(vox, 2, half)
    plane = np.einsum("ypk,zql->yzqpkl", by_parity, by_parity).reshape(vox * vox, vox * vox)
    line = basis.T
    forward_line = np.kron(np.eye(2), line)
    backward_line = np.kron(np.eye(6), line.T)
    wave = np.sin(2.0 * np.pi * np.arange(half) / vox)
    wave[0] = 0.0
    first = np.broadcast_to(wave[:, None, None], (half, half, half))
    second = np.broadcast_to(wave[None, :, None], (half, half, half))
    third = np.broadcast_to(wave[None, None, :], (half, half, half))
    square = first**2 + second**2 + third**2
    inverse = np.where(square > 0.0, 1.0 / np.where(square > 0.0, square, 1.0), 0.0)
    waves = (first, second, third)
    products = [waves[a] * waves[b] for a, b in PAIRS]
    rows = products + [inverse / shear_ref, green_ratio * inverse]
    multipliers = np.stack(rows).reshape(len(rows), half, half * half).astype(np.float32)
    return split_table(plane), split_table(forward_line), split_table(backward_line), multipliers


def split(value):
    high = value.astype(bf16)
    return high, (value - high.astype(f32)).astype(bf16)


def dot(left, right):
    return lax.dot_general(left, right, (((1,), (0,)), ((), ())), preferred_element_type=f32)


def dot_t(left, right):
    return lax.dot_general(left, right, (((1,), (1,)), ((), ())), preferred_element_type=f32)


def by_table(value, high, low, contract):
    rows = value.shape[0]
    value_high, value_low = split(value)
    both = contract(jnp.concatenate([value_high, value_low], axis=0), high)
    return both[:rows] + both[rows:] + contract(value_high, low)


def table_by(high, low, value):
    rows = high.shape[0]
    value_high, value_low = split(value)
    both = dot(jnp.concatenate([high, low], axis=0), value_high)
    return both[:rows] + both[rows:] + dot(high, value_low)


def lane_position(shape):
    return lax.broadcasted_iota(jnp.int32, shape, 1)


def row_position(shape):
    return lax.broadcasted_iota(jnp.int32, shape, 0)


class Stencil:
    def __init__(self, shape, width):
        self.rows, self.columns = shape
        self.width = width
        lane = lane_position(shape)
        row = row_position(shape)
        self.last_z = lane % width == width - 1
        self.first_z = lane % width == 0
        self.last_y = lane >= self.columns - width
        self.first_y = lane < width
        self.last_x = row == self.rows - 1
        self.first_x = row == 0

    def up_z(self, v):
        return jnp.where(self.last_z, 0.0, pltpu.roll(v, self.columns - 1, 1))

    def up_y(self, v):
        return jnp.where(self.last_y, 0.0, pltpu.roll(v, self.columns - self.width, 1))

    def up_x(self, v):
        return jnp.where(self.last_x, 0.0, pltpu.roll(v, self.rows - 1, 0))

    def down_z(self, v):
        return jnp.where(self.first_z, 0.0, pltpu.roll(v, 1, 1))

    def down_y(self, v):
        return jnp.where(self.first_y, 0.0, pltpu.roll(v, self.width, 1))

    def down_x(self, v):
        return jnp.where(self.first_x, 0.0, pltpu.roll(v, 1, 0))

    def strain(self, field):
        slopes = []
        for v in field:
            next_z = self.up_z(v)
            sum_z = v + next_z
            dif_z = next_z - v
            next_y = self.up_y(sum_z)
            sums = sum_z + next_y
            along_y = next_y - sum_z
            along_z = dif_z + self.up_y(dif_z)
            slopes.append((self.up_x(sums) - sums, along_y + self.up_x(along_y), along_z + self.up_x(along_z)))
        return [
            0.25 * slopes[0][0],
            0.25 * slopes[1][1],
            0.25 * slopes[2][2],
            0.125 * (slopes[2][1] + slopes[1][2]),
            0.125 * (slopes[2][0] + slopes[0][2]),
            0.125 * (slopes[1][0] + slopes[0][1]),
        ]

    def force(self, stress):
        result = []
        for b in range(3):
            along_x, along_y, along_z = (stress[SLOT[(a, b)]] for a in range(3))
            sum_x = along_x + self.down_z(along_x)
            first = sum_x + self.down_y(sum_x)
            sum_y = along_y + self.down_z(along_y)
            dif_z = self.down_z(along_z) - along_z
            back = self.down_y(sum_y)
            rest = (back - sum_y) + (dif_z + self.down_y(dif_z))
            result.append(0.25 * ((self.down_x(first) - first) + (rest + self.down_x(rest))))
        return result


def total(value):
    return jnp.sum(jnp.sum(value, axis=0, keepdims=True), axis=1, keepdims=True)


def measure(stress):
    return (
        stress[0] * stress[0]
        + stress[1] * stress[1]
        + stress[2] * stress[2]
        + 2.0 * (stress[3] * stress[3] + stress[4] * stress[4] + stress[5] * stress[5])
    )


def remaining(shear, size, steps, most):
    stiff = (2.0 * shear) * (2.0 * shear) * size

    def relax(count, left):
        ratio = stiff * left * left
        return left * ((1.0 - relax_rate) + relax_rate / (1.0 + ratio))

    left = lax.fori_loop(0, steps, relax, jnp.ones_like(stiff))
    return left, stiff * left * left


def deviator_of(strain):
    trace = strain[0] + strain[1] + strain[2]
    third = trace / 3.0
    return trace, [strain[0] - third, strain[1] - third, strain[2] - third] + list(strain[3:])


def gather_rows(source, target):
    devices, parts, planes, _ = source.shape
    for part in range(parts):
        for device in range(devices):
            target[part, device * planes : (device + 1) * planes, :] = source[device, part]


def micro_kernel(
    local, local_count, steps_ref, mesh_ref, lame_ref_, shear_ref_, mult_ref, fwd_ref, bwd_ref, table_hbm,
    strain_ref, response_ref, fields, table, sem, spectrum
):
    vox, columns = lame_ref_.shape
    half = vox // 2
    quarter = half * half
    width = vox_width(fields.shape[2])
    copies = [pltpu.make_async_copy(table_hbm.at[i], table.at[i], sem.at[i]) for i in range(2)]
    for copy in copies:
        copy.start()
    own = (lax.axis_index("grp") * lax.axis_size("dev") + lax.axis_index("dev")) * local_count + local
    steps = steps_ref[own]
    gather_rows(mesh_ref, fields)
    stencil = Stencil(fields.shape[1:], width)
    mesh_strain = stencil.strain([fields[c] for c in range(3)])
    mine = fields[3] == own.astype(f32)
    count = total(jnp.where(mine, 1.0, 0.0))
    load = [total(jnp.where(mine, part, 0.0)) / count for part in mesh_strain]
    trace, dev = deviator_of(load)
    lame = lame_ref_[...].astype(f32)
    shear = shear_ref_[...].astype(f32)
    size = measure([0.5 * part for part in dev])
    left, _ = remaining(shear, jnp.broadcast_to(size, shear.shape), steps, 4)
    bulk = lame + (2.0 / 3.0) * shear
    sources = jnp.concatenate([bulk * trace, 2.0 * shear * left], axis=0)
    for copy in copies:
        copy.wait()
    spectral = table_by(fwd_ref[0], fwd_ref[1], by_table(sources, table[0], table[1], dot))

    def block(field, px, py, pz):
        rows = slice(field * vox + px * half, field * vox + (px + 1) * half)
        lanes = slice((pz * 2 + py) * quarter, (pz * 2 + py + 1) * quarter)
        return rows, lanes

    parities = [(px, py, pz) for px in range(2) for py in range(2) for pz in range(2)]
    product = [mult_ref[i] for i in range(6)]
    inverse = mult_ref[6]
    scaled = mult_ref[7]

    def second(blocks, parity, a, b):
        if a == b:
            return -(product[SLOT[(a, b)]] * blocks[parity])
        other = tuple(1 - p if axis in (a, b) else p for axis, p in enumerate(parity))
        value = product[SLOT[(a, b)]] * blocks[other]
        return value if parity[a] == parity[b] else -value

    psi = {}
    raw = {}
    for parity in parities:
        rows, lanes = block(1, *parity)
        raw[parity] = spectral[rows, lanes]
        psi[parity] = inverse * raw[parity]
    phi = {}
    for parity in parities:
        rows, lanes = block(0, *parity)
        pressed = sum(
            (1.0 if a == b else 2.0) * dev[SLOT[(a, b)]] * second(psi, parity, a, b) for a, b in PAIRS
        )
        phi[parity] = (1.0 - green_ratio) * inverse * spectral[rows, lanes] + scaled * pressed
    for parity in parities:
        curl = {pair: second(psi, parity, *pair) for pair in PAIRS}
        for index, (a, b) in enumerate(PAIRS):
            def at(i, j):
                return curl[(min(i, j), max(i, j))]
            if a == b:
                sheared = sum(dev[SLOT[(b, c)]] * at(a, c) for c in range(3))
            else:
                sheared = 0.5 * sum(dev[SLOT[(b, c)]] * at(a, c) + dev[SLOT[(a, c)]] * at(b, c) for c in range(3))
            rows, lanes = block(index, *parity)
            spectrum[rows, lanes] = second(phi, parity, a, b) + sheared
    moved = table_by(bwd_ref[0], bwd_ref[1], by_table(spectrum[...], table[0], table[1], dot_t))
    strain = [load[i] + moved[i * vox : (i + 1) * vox] for i in range(6)]
    planes = strain_ref.shape[2]
    for i in range(6):
        for device in range(strain_ref.shape[0]):
            strain_ref[device, i] = strain[i][device * planes : (device + 1) * planes]
    trace, dev = deviator_of(strain)
    left, ratio = remaining(shear, measure([0.5 * part for part in dev]), steps, 4)
    push = bulk * trace
    pull = 2.0 * shear * left
    stress = [push + pull * dev[i] for i in range(3)] + [pull * dev[i] for i in range(3, 6)]
    parts = stress + [lame, shear / (1.0 + ratio)]
    lane = lane_position(response_ref.shape)
    row = jnp.zeros(response_ref.shape, f32)
    for index, part in enumerate(parts):
        row = jnp.where(lane == index, total(part) / float(vox * columns), row)
    response_ref[...] = row


def vox_width(columns):
    width = int(round(columns**0.5))
    return width


def macro_kernel(
    slots_ref, table_ref, table_v_ref, mesh_ref, force_in_ref, next_ref, row_ref, fields, forces, cells, result
):
    devices, _, planes, columns = mesh_ref.shape
    samples = table_v_ref.shape[0]
    rank = lax.axis_index("dev")
    group = lax.axis_index("grp")
    local_count = row_ref.shape[0]
    group_size = local_count * devices
    start = group * group_size
    for local in range(local_count):
        chosen = jnp.int32(0)
        for j in range(group_size):
            chosen = jnp.where(slots_ref[start + j] == rank * local_count + local, start + j, chosen)
        row_ref[local : local + 1, :] = table_v_ref[pl.ds(chosen, 1), :]
    gather_rows(mesh_ref, fields)
    gather_rows(force_in_ref, forces)
    rows = fields.shape[1]
    height = min(8, rows)
    span = min(512, columns)
    for top in range(0, rows, height):
        for side in range(0, columns, span):
            where = (slice(top, top + height), slice(side, side + span))
            label = fields[(3,) + where]

            def pick(sample, held):
                here = label == sample.astype(f32)
                return tuple(jnp.where(here, table_ref[sample, c], held[c]) for c in range(8))

            zero = jnp.zeros((height, span), f32)
            held = lax.fori_loop(0, samples, pick, (zero,) * 8, unroll=4)
            for c in range(8):
                cells[(c,) + where] = held[c]
    stencil = Stencil(fields.shape[1:], vox_width(columns))
    stress = [cells[c] for c in range(6)]
    pulled = stencil.force(stress)
    remainder = [forces[b] - pulled[b] - spring_rate * fields[b] for b in range(3)]
    direction = remainder
    norm_now = total(sum(r * r for r in remainder))
    update = None
    lame = cells[6]
    shear = 2.0 * cells[7]
    for turn in range(CG_STEPS):
        strain = stencil.strain(direction)
        pressure = lame * (strain[0] + strain[1] + strain[2])
        stress = [shear * strain[i] + pressure for i in range(3)] + [shear * strain[i] for i in range(3, 6)]
        pulled = stencil.force(stress)
        image = [pulled[b] + spring_rate * direction[b] for b in range(3)]
        alpha = norm_now / total(sum(direction[b] * image[b] for b in range(3)))
        moved = [alpha * direction[b] for b in range(3)]
        update = moved if update is None else [update[b] + moved[b] for b in range(3)]
        if turn + 1 < CG_STEPS:
            remainder = [remainder[b] - alpha * image[b] for b in range(3)]
            norm_next = total(sum(r * r for r in remainder))
            grow = norm_next / norm_now
            direction = [remainder[b] + grow * direction[b] for b in range(3)]
            norm_now = norm_next
    for b in range(3):
        done = fields[b] + update[b]
        for device in range(devices):
            result[device, b] = done[device * planes : (device + 1) * planes]
    next_ref[...] = result[rank]


def vmem():
    return pl.BlockSpec(memory_space=pltpu.VMEM)


def smem():
    return pl.BlockSpec(memory_space=pltpu.SMEM)


def shards(
    displacement, external_force, element_sample, lame_field, shear_field, plastic_steps, owner_slot
):
    group_size, planes, columns = lame_field.shape
    devices = lax.axis_size("dev")
    groups = lax.axis_size("grp")
    local_count = group_size // devices
    vox = planes * devices
    layers = displacement.shape[1]
    width = displacement.shape[2] * displacement.shape[3]
    plane, forward_line, backward_line, multipliers = tables(vox)
    params = pltpu.CompilerParams(vmem_limit_bytes=48 * 1024 * 1024)

    def spread(block):
        return lax.all_to_all(
            jnp.broadcast_to(block[None], (devices,) + block.shape), "dev", split_axis=0, concat_axis=0, tiled=True
        )

    mesh_part = jnp.concatenate([displacement, element_sample[None].astype(f32)]).reshape(4, layers, width)
    mesh_all = spread(mesh_part)
    force_all = spread(external_force.reshape(3, layers, width))
    moduli = []
    for field in (lame_field, shear_field):
        own = lax.all_to_all(
            field.reshape(devices, local_count, planes, columns), "dev", split_axis=0, concat_axis=0, tiled=True
        )
        moduli.append(own)
    strains = []
    rows = []
    for local in range(local_count):
        lame_own, shear_own = (field[:, local].reshape(vox, columns) for field in moduli)
        strain, response = pl.pallas_call(
            functools.partial(micro_kernel, local, local_count),
            name="micro",
            out_shape=(
                jax.ShapeDtypeStruct((devices, 6, planes, columns), f32),
                jax.ShapeDtypeStruct((1, 8), f32),
            ),
            in_specs=[smem()] + [vmem()] * 6 + [pl.BlockSpec(memory_space=pl.ANY)],
            out_specs=(vmem(), vmem()),
            scratch_shapes=[
                pltpu.VMEM((4, devices * layers, width), f32),
                pltpu.VMEM(plane.shape, bf16),
                pltpu.SemaphoreType.DMA((2,)),
                pltpu.VMEM((6 * vox, columns), f32),
            ],
            compiler_params=params,
        )(plastic_steps, mesh_all, lame_own, shear_own, multipliers, forward_line, backward_line, plane)
        strains.append(strain)
        rows.append(response)
    own_rows = rows[0] if local_count == 1 else jnp.concatenate(rows)
    everyone = groups * devices
    gathered = lax.all_to_all(
        jnp.broadcast_to(own_rows[None], (everyone,) + own_rows.shape),
        ("grp", "dev"), split_axis=0, concat_axis=0, tiled=True,
    ).reshape(everyone * local_count, 8)
    sent = jnp.stack(strains, axis=1)
    moved = lax.all_to_all(sent, "dev", split_axis=0, concat_axis=0, tiled=True)
    micro_strain = jnp.transpose(moved, (2, 0, 1, 3, 4)).reshape(6, group_size, planes, columns)
    following, picked = pl.pallas_call(
        macro_kernel,
        name="macro",
        out_shape=(
            jax.ShapeDtypeStruct((3, layers, width), f32),
            jax.ShapeDtypeStruct((local_count, 8), f32),
        ),
        in_specs=[smem(), smem()] + [vmem()] * 3,
        out_specs=(vmem(), vmem()),
        scratch_shapes=[
            pltpu.VMEM((4, devices * layers, width), f32),
            pltpu.VMEM((3, devices * layers, width), f32),
            pltpu.VMEM((8, devices * layers, width), f32),
            pltpu.VMEM((devices, 3, layers, width), f32),
        ],
        compiler_params=params,
    )(owner_slot, gathered, gathered, mesh_all, force_all)
    return (following.reshape(displacement.shape), picked, micro_strain)


def solution(mesh):
    in_specs = (
        P(None, "dev", None, None),
        P(None, "dev", None, None),
        P("dev", None, None),
        P("grp", "dev", None),
        P("grp", "dev", None),
        P(),
        P(),
    )
    out_specs = (P(None, "dev", None, None), P(("grp", "dev"), None), P(None, "grp", "dev", None))
    return jax.shard_map(shards, mesh=mesh, in_specs=in_specs, out_specs=out_specs, check_vma=False)
```

time: 340 us -> 90.5 us (0.27)
  the two profiles are of different devices: /device:TPU:5 before, /device:TPU:0 now
where the time goes in v1:
time: 90.5 us; the launch traced here: 89.6 us
  waiting for transfers between devices  27.1 us (30%)
  blocking collectives  25.2 us (28%)
  starting transfers between devices  13.7 us (15%)
  Pallas kernels  11.4 us (13%)
  local copies, waits for them, and re-layouts  10.8 us (12%)
    all_to_all x1, waiting for transfers between devices, shards(): moved = lax.all_to_all(sent, 'dev', split_axis=0, concat_axis=0, tiled=True)  14.4 us
    all_to_all x1, blocking collectives, shards(): lax.all_to_all(jnp.broadcast_to(own_rows[None], (everyone,) + own_rows.sh...  12.9 us
    all_to_all x1, blocking collectives, shards(): lax.all_to_all(field.reshape(devices, local_count, planes, columns), 'dev...  12.3 us
    all_to_all x2, waiting for transfers between devices, spread(): lax.all_to_all(jnp.broadcast_to(block[None], (devices,) + block.shape), '...  8.66 us
    all_to_all x2, starting transfers between devices, spread(): lax.all_to_all(jnp.broadcast_to(block[None], (devices,) + block.shape), '...  6.8 us
    unnamed x13, local copies, waits for them, and re-layouts  6.38 us
    pallas_call x1, Pallas kernels, shards(): pl.pallas_call(macro_kernel, name='macro', out_shape=(jax.ShapeDtypeStruc...  5.68 us
    pallas_call x1, Pallas kernels, shards(): pl.pallas_call(functools.partial(micro_kernel, local, local_count), name=...  5.68 us
  transfers between devices with their start and end apart: 4, of which 3 were waited for; matrix products, arithmetic and copies ran while one was open for 4% of the time, Pallas kernels for 13%

profile of v1, /device:TPU:0, one launch (start us, length us, event | category | flops | bytes accessed | tf_op | source)
XLA Modules:
  0.0 89.6 jit_solution(2289199360522730434)
XLA Ops:
  0.6 12.3 %all_to_all.30 = bf16[8,1,4,1024]{3,2,1,0:T(4,128)(2,1)S(1)} all-to-all(bf16[8,1,4,1024]{3,2,1,0:T(4,128)(2,1)} %bitcast.20), channel_id=1, replica_groups=mesh['grp'=4,'dev'=8] {'dev'}, dimensions={0} | all-to-all | bytes 131072 | tf_op jit(solution)/shard_map/all_to_all | solution.py:386
  12.9 3.4 %all-to-all-start.2 = ((bf16[8,1,4,1024]{3,2,1,0:T(4,128)(2,1)}), bf16[8,1,4,1024]{3,2,1,0:T(4,128)(2,1)S(1)}, u32[]{:S(2)}, u32[]{:S(2)}) async-start(bf16[8,1,4,1024]{3,2,1,0:T(4,128)(2,1)} %bitcast.21), calls=%async_computation.2 | async-start | bytes 131072 | tf_op jit(solution)/shard_map/all_to_all | solution.py:386
  16.2 0.8 convert_element_type.4
  17.0 0.1 concatenate.9
  17.1 1.0 %concatenate.8 = f32[1,3,2,1024]{3,2,1,0:T(2,128)S(1)} reshape(f32[3,2,32,32]{3,2,1,0:T(8,128)} %param.11) | data formatting | bytes 49152 | tf_op jit(solution)/shard_map/concatenate | solution.py:381
  18.1 0.0 copy-start.5
  18.1 4.0 %all-to-all-done.2 = bf16[8,1,4,1024]{3,2,1,0:T(4,128)(2,1)S(1)} async-done(((bf16[8,1,4,1024]{3,2,1,0:T(4,128)(2,1)}), bf16[8,1,4,1024]{3,2,1,0:T(4,128)(2,1)S(1)}, u32[]{:S(2)}, u32[]{:S(2)}) %all-to-all-start.2) | async-done | bytes 65568 | tf_op jit(solution)/shard_map/all_to_all | solution.py:386
  22.1 0.8 broadcast_in_dim.24
  22.9 3.4 %all-to-all-start = ((f32[8,4,2,1024]{3,2,1,0:T(2,128)}), f32[8,4,2,1024]{3,2,1,0:T(2,128)S(1)}, u32[]{:S(2)}, u32[]{:S(2)}) async-start(f32[8,4,2,1024]{3,2,1,0:T(2,128)} %broadcast_in_dim.24), calls=%async_computation | async-start | bytes 524288 | tf_op jit(solution)/shard_map/all_to_all | solution.py:377
  26.3 1.0 %broadcast_in_dim.27 = f32[3,2,1024]{2,1,0:T(2,128)S(1)} reshape(f32[3,2,32,32]{3,2,1,0:T(8,128)} %param.12) | data formatting | bytes 49152 | tf_op jit(solution)/shard_map/broadcast_in_dim | solution.py:378
  27.3 8.7 %all-to-all-done.mesh_ref = f32[8,4,2,1024]{3,2,1,0:T(2,128)S(1)} async-done(((f32[8,4,2,1024]{3,2,1,0:T(2,128)}), f32[8,4,2,1024]{3,2,1,0:T(2,128)S(1)}, u32[]{:S(2)}, u32[]{:S(2)}) %all-to-all-start) | async-done | bytes 262176 | tf_op jit(solution)/shard_map/all_to_all | solution.py:377
  36.0 0.7 broadcast_in_dim.28
  36.7 3.4 %all-to-all-start.4 = ((f32[8,3,2,1024]{3,2,1,0:T(2,128)}), f32[8,3,2,1024]{3,2,1,0:T(2,128)S(1)}, u32[]{:S(2)}, u32[]{:S(2)}) async-start(f32[8,3,2,1024]{3,2,1,0:T(2,128)} %broadcast_in_dim.28), calls=%async_computation.4 | async-start | bytes 393216 | tf_op jit(solution)/shard_map/all_to_all | solution.py:377
  40.1 0.0 copy-start
  40.2 2.2 %copy-done = bf16[2,1024,1024]{2,1,0:T(8,128)(2,1)S(1)} copy-done((bf16[2,1024,1024]{2,1,0:T(8,128)(2,1)S(1)}, bf16[2,1024,1024]{2,1,0:T(8,128)(2,1)}, u32[]{:S(2)}) %copy-start) | copy-done | bytes 4194328
  42.3 0.0 copy-start.1
  42.3 0.9 %copy-done.1 = bf16[2,192,192]{2,1,0:T(8,128)(2,1)S(1)} copy-done((bf16[2,192,192]{2,1,0:T(8,128)(2,1)S(1)}, bf16[2,192,192]{2,1,0:T(8,128)(2,1)}, u32[]{:S(2)}) %copy-start.1) | copy-done | bytes 147480
  43.3 0.0 copy-start.2
  43.3 0.9 %copy-done.2 = f32[8,16,256]{2,1,0:T(8,128)S(1)} copy-done((f32[8,16,256]{2,1,0:T(8,128)S(1)}, f32[8,16,256]{2,1,0:T(8,128)}, u32[]{:S(2)}) %copy-start.2) | copy-done | bytes 131096
  44.2 0.0 copy-start.3
  44.2 0.8 copy-done.3
  44.9 0.0 copy-start.4
  44.9 0.7 copy-done.4
  45.6 5.7 %micro.1 = (f32[8,6,4,1024]{3,2,1,0:T(4,128)}, f32[1,8]{1,0:T(1,128)S(1)}) custom-call(s32[32]{0:T(128)S(1)} %copy-done.4, f32[8,4,2,1024]{3,2,1,0:T(2,128)S(1)} %all-to-all-done.mesh_ref, bf16[32,1024]{1,0:T(8,128)(2,1)S(1)} %reshape_squeeze.6.lame_ref_, bf16[32,1024]{1,0:T(8,128)(2,1)S(1)} %reshape_squeeze.7.shear_ref_, f32[8,16,256]{2,1,0:T(8,128)S(1)} %copy-done.2, ...), custom_call_target="tpu_custom_call" | custom-call | tf_op jit(solution)/shard_map/micro/pallas_call | solution.py:394
  51.3 0.0 all-to-all-done.4.force_in_ref
  51.3 12.9 %all_to_all.31 = f32[32,1,8]{2,1,0:T(1,128)S(1)} all-to-all(f32[32,1,8]{2,1,0:T(1,128)S(1)} %broadcast_in_dim.26), channel_id=1, replica_groups=mesh['grp'=4,'dev'=8] {'grp','dev'}, dimensions={0} | all-to-all | bytes 2048 | tf_op jit(solution)/shard_map/all_to_all | solution.py:415
  64.2 3.5 %all-to-all-start.5 = ((f32[8,1,6,4,1024]{4,3,2,1,0:T(4,128)}), f32[8,1,6,4,1024]{4,3,2,1,0:T(4,128)S(1)}, u32[]{:S(2)}, u32[]{:S(2)}) async-start(f32[8,1,6,4,1024]{4,3,2,1,0:T(4,128)} %bitcast.6), calls=%async_computation.5 | async-start | bytes 1572864 | tf_op jit(solution)/shard_map/all_to_all | solution.py:420
  67.8 0.0 copy-done.5
  67.8 5.7 %macro.1 = (f32[3,2,1024]{2,1,0:T(2,128)S(1)}, f32[1,8]{1,0:T(1,128)}) custom-call(s32[32]{0:T(128)S(1)} %copy-done.5, f32[32,8]{1,0:T(8,128)S(1)} %bitcast.16, f32[32,8]{1,0:T(8,128)S(1)} %bitcast.17, f32[8,4,2,1024]{3,2,1,0:T(2,128)S(1)} %all-to-all-done.mesh_ref, f32[8,3,2,1024]{3,2,1,0:T(2,128)S(1)} %all-to-all-done.4.force_in_ref), custom_call_target="tpu_custom_call" | custom-call | tf_op jit(solution)/shard_map/macro/pallas_call | solution.py:422
  73.5 0.8 reshape.32
  74.2 14.4 %all-to-all-done.5 = f32[8,1,6,4,1024]{4,3,2,1,0:T(4,128)S(1)} async-done(((f32[8,1,6,4,1024]{4,3,2,1,0:T(4,128)}), f32[8,1,6,4,1024]{4,3,2,1,0:T(4,128)S(1)}, u32[]{:S(2)}, u32[]{:S(2)}) %all-to-all-start.5) | async-done | bytes 786464 | tf_op jit(solution)/shard_map/all_to_all | solution.py:420
  88.7 0.9 %copy.16 = f32[6,8,4,1024]{3,2,1,0:T(4,128)} copy(f32[6,8,4,1024]{3,2,0,1:T(4,128)S(1)} %bitcast.19) | data formatting | bytes 1572864
  (4 shorter events, 0.1 us)
Async XLA Ops:
  12.9 9.2 %all-to-all-start.2 = ((bf16[8,1,4,1024]{3,2,1,0:T(4,128)(2,1)}), bf16[8,1,4,1024]{3,2,1,0:T(4,128)(2,1)S(1)}, u32[]{:S(2)}, u32[]{:S(2)}) async-start(bf16[8,1,4,1024]{3,2,1,0:T(4,128)(2,1)} %bitcast.21), calls=%async_computation.2 | async-start | bytes 131072 | tf_op jit(solution)/shard_map/all_to_all | solution.py:386
  18.1 49.7 %copy-start.5 = (s32[32]{0:T(128)S(1)}, s32[32]{0:T(128)}, u32[]{:S(2)}) copy-start(s32[32]{0:T(128)} %slots_ref.1) | copy-start | bytes 388
  22.9 13.1 %all-to-all-start = ((f32[8,4,2,1024]{3,2,1,0:T(2,128)}), f32[8,4,2,1024]{3,2,1,0:T(2,128)S(1)}, u32[]{:S(2)}, u32[]{:S(2)}) async-start(f32[8,4,2,1024]{3,2,1,0:T(2,128)} %broadcast_in_dim.24), calls=%async_computation | async-start | bytes 524288 | tf_op jit(solution)/shard_map/all_to_all | solution.py:377
  36.7 14.6 %all-to-all-start.4 = ((f32[8,3,2,1024]{3,2,1,0:T(2,128)}), f32[8,3,2,1024]{3,2,1,0:T(2,128)S(1)}, u32[]{:S(2)}, u32[]{:S(2)}) async-start(f32[8,3,2,1024]{3,2,1,0:T(2,128)} %broadcast_in_dim.28), calls=%async_computation.4 | async-start | bytes 393216 | tf_op jit(solution)/shard_map/all_to_all | solution.py:377
  40.1 2.2 %copy-start = (bf16[2,1024,1024]{2,1,0:T(8,128)(2,1)S(1)}, bf16[2,1024,1024]{2,1,0:T(8,128)(2,1)}, u32[]{:S(2)}) copy-start(bf16[2,1024,1024]{2,1,0:T(8,128)(2,1)} %constant.11.clone.table_hbm) | copy-start | bytes 12582916
  42.3 0.9 %copy-start.1 = (bf16[2,192,192]{2,1,0:T(8,128)(2,1)S(1)}, bf16[2,192,192]{2,1,0:T(8,128)(2,1)}, u32[]{:S(2)}) copy-start(bf16[2,192,192]{2,1,0:T(8,128)(2,1)} %constant.10.clone.bwd_ref) | copy-start | bytes 442372
  43.3 0.9 %copy-start.2 = (f32[8,16,256]{2,1,0:T(8,128)S(1)}, f32[8,16,256]{2,1,0:T(8,128)}, u32[]{:S(2)}) copy-start(f32[8,16,256]{2,1,0:T(8,128)} %constant.8.clone.mult_ref) | copy-start | bytes 393220
  44.2 0.8 copy-start.3
  44.9 0.7 copy-start.4
  64.2 24.5 %all-to-all-start.5 = ((f32[8,1,6,4,1024]{4,3,2,1,0:T(4,128)}), f32[8,1,6,4,1024]{4,3,2,1,0:T(4,128)S(1)}, u32[]{:S(2)}, u32[]{:S(2)}) async-start(f32[8,1,6,4,1024]{4,3,2,1,0:T(4,128)} %bitcast.6), calls=%async_computation.5 | async-start | bytes 1572864 | tf_op jit(solution)/shard_map/all_to_all | solution.py:420

commit v2 on v1

--- a/solution.py
+++ b/solution.py
@@ -92,16 +92,17 @@
 
 
 class Stencil:
-    def __init__(self, shape, width):
+    def __init__(self, shape, width, devices):
         self.rows, self.columns = shape
         self.width = width
+        self.devices = devices
         lane = lane_position(shape)
-        row = row_position(shape)
+        row = row_position((devices, self.columns))
         self.last_z = lane % width == width - 1
         self.first_z = lane % width == 0
         self.last_y = lane >= self.columns - width
         self.first_y = lane < width
-        self.last_x = row == self.rows - 1
+        self.last_x = row == devices - 1
         self.first_x = row == 0
 
     def up_z(self, v):
@@ -111,7 +112,8 @@
         return jnp.where(self.last_y, 0.0, pltpu.roll(v, self.columns - self.width, 1))
 
     def up_x(self, v):
-        return jnp.where(self.last_x, 0.0, pltpu.roll(v, self.rows - 1, 0))
+        wrapped = jnp.where(self.last_x, 0.0, pltpu.roll(v[: self.devices], self.devices - 1, 0))
+        return jnp.concatenate([v[self.devices :], wrapped], axis=0)
 
     def down_z(self, v):
         return jnp.where(self.first_z, 0.0, pltpu.roll(v, 1, 1))
@@ -120,7 +122,8 @@
         return jnp.where(self.first_y, 0.0, pltpu.roll(v, self.width, 1))
 
     def down_x(self, v):
-        return jnp.where(self.first_x, 0.0, pltpu.roll(v, 1, 0))
+        wrapped = jnp.where(self.first_x, 0.0, pltpu.roll(v[self.rows - self.devices :], 1, 0))
+        return jnp.concatenate([wrapped, v[: self.rows - self.devices]], axis=0)
 
     def strain(self, field):
         slopes = []
@@ -186,35 +189,117 @@
     return trace, [strain[0] - third, strain[1] - third, strain[2] - third] + list(strain[3:])
 
 
-def gather_rows(source, target):
-    devices, parts, planes, _ = source.shape
+LAME_UNIT = 2.0**8
+SHEAR_UNIT = 2.0**9
+CODE_BASE = 2.0**11
+LABEL_BASE = 2.0**12
+LANES = 128
+
+
+def encode(lame, shear):
+    return (lame.astype(f32) * LAME_UNIT) * CODE_BASE + shear.astype(f32) * SHEAR_UNIT
+
+
+def decode(code):
+    high = jnp.floor(code * (1.0 / CODE_BASE))
+    return high * (1.0 / LAME_UNIT), (code - high * CODE_BASE) * (1.0 / SHEAR_UNIT)
+
+
+def pack_kernel(layers, moved_ref, force_ref, sample_ref, lame_ref, shear_ref, packet_ref, wide):
+    devices, local_count, planes, columns = lame_ref.shape
+    tiles = columns // LANES
+    for device in range(devices):
+        for local in range(local_count):
+            code = encode(lame_ref[device, local], shear_ref[device, local])
+            for tile in range(tiles):
+                packet_ref[device, pl.ds(local * planes * tiles + tile, planes, stride=tiles), :] = code[
+                    :, tile * LANES : (tile + 1) * LANES
+                ]
+    width = moved_ref.shape[1]
+    beside = LANES // width
+    start = 0
+    for ref in (moved_ref, force_ref, sample_ref):
+        rows = ref.shape[0]
+        wide[start : start + rows, :] = jnp.concatenate([ref[...].astype(f32)] * beside, axis=1)
+        start += rows
+    count = start // beside
+    slot = lane_position((count, LANES)) // width
+    merged = wide[pl.ds(0, count, stride=beside), :]
+    for place in range(1, beside):
+        merged = jnp.where(slot == place, wide[pl.ds(place, count, stride=beside), :], merged)
+    nodes = 6 * count // 7
+    each = (count - nodes) // layers
+    base = local_count * planes * tiles
+    for device in range(devices):
+        packet_ref[device, base : base + nodes, :] = merged[:nodes]
+    for pair in range((layers + 1) // 2):
+        first = merged[nodes + 2 * pair * each : nodes + (2 * pair + 1) * each]
+        if 2 * pair + 1 < layers:
+            first = first * LABEL_BASE + merged[nodes + (2 * pair + 1) * each : nodes + (2 * pair + 2) * each]
+        else:
+            first = first * LABEL_BASE
+        for device in range(devices):
+            packet_ref[device, base + nodes + pair * each : base + nodes + (pair + 1) * each, :] = first
+
+
+def read_fields(packet_ref, base, layers, fields):
+    parts, rows, columns = fields.shape
+    devices = rows // layers
+    tiles = columns // LANES
+    step = packet_ref.shape[0] // devices
     for part in range(parts):
-        for device in range(devices):
-            target[part, device * planes : (device + 1) * planes, :] = source[device, part]
+        for layer in range(layers):
+            for tile in range(tiles):
+                if part < 6:
+                    at = base + (part * layers + layer) * tiles + tile
+                    piece = packet_ref[pl.ds(at, devices, stride=step), :]
+                else:
+                    at = base + (6 * layers + layer // 2) * tiles + tile
+                    both = packet_ref[pl.ds(at, devices, stride=step), :]
+                    high = jnp.floor(both * (1.0 / LABEL_BASE))
+                    piece = high if layer % 2 == 0 else both - high * LABEL_BASE
+                fields[part, layer * devices : (layer + 1) * devices, tile * LANES : (tile + 1) * LANES] = piece
 
 
 def micro_kernel(
-    local, local_count, steps_ref, mesh_ref, lame_ref_, shear_ref_, mult_ref, fwd_ref, bwd_ref, table_hbm,
-    strain_ref, response_ref, fields, table, sem, spectrum
+    local, local_count, layers, steps_ref, packet_ref, mult_hbm, fwd_hbm, bwd_hbm, table_hbm,
+    sent_ref, response_ref, fields, moduli, mult_ref, fwd_ref, bwd_ref, table, spectrum, ordered, sem
 ):
-    vox, columns = lame_ref_.shape
+    devices, planes = sent_ref.shape[0], sent_ref.shape[1] // 6
+    vox, columns = moduli.shape[1:]
     half = vox // 2
     quarter = half * half
     width = vox_width(fields.shape[2])
-    copies = [pltpu.make_async_copy(table_hbm.at[i], table.at[i], sem.at[i]) for i in range(2)]
+    pairs = [(mult_hbm, mult_ref), (fwd_hbm, fwd_ref), (bwd_hbm, bwd_ref)]
+    pieces = sem.shape[0] - len(pairs)
+    height = columns // (pieces // 2)
+    for piece in range(pieces):
+        where = (piece * height // columns, pl.ds(piece * height % columns, height))
+        pairs.append((table_hbm.at[where], table.at[where]))
+    copies = [pltpu.make_async_copy(source, target, sem.at[i]) for i, (source, target) in enumerate(pairs)]
     for copy in copies:
         copy.start()
     own = (lax.axis_index("grp") * lax.axis_size("dev") + lax.axis_index("dev")) * local_count + local
     steps = steps_ref[own]
-    gather_rows(mesh_ref, fields)
-    stencil = Stencil(fields.shape[1:], width)
+    tiles = columns // LANES
+    step = packet_ref.shape[0] // devices
+    read_fields(packet_ref, local_count * planes * tiles, layers, fields)
+    for device in range(devices):
+        for tile in range(tiles):
+            at = device * step + local * planes * tiles + tile
+            code = packet_ref[pl.ds(at, planes, stride=tiles), :]
+            for kind, value in enumerate(decode(code)):
+                moduli[
+                    kind, device * planes : (device + 1) * planes, tile * LANES : (tile + 1) * LANES
+                ] = value
+    stencil = Stencil(fields.shape[1:], width, fields.shape[1] // layers)
     mesh_strain = stencil.strain([fields[c] for c in range(3)])
-    mine = fields[3] == own.astype(f32)
+    mine = fields[6] == own.astype(f32)
     count = total(jnp.where(mine, 1.0, 0.0))
     load = [total(jnp.where(mine, part, 0.0)) / count for part in mesh_strain]
     trace, dev = deviator_of(load)
-    lame = lame_ref_[...].astype(f32)
-    shear = shear_ref_[...].astype(f32)
+    lame = moduli[0]
+    shear = moduli[1]
     size = measure([0.5 * part for part in dev])
     left, _ = remaining(shear, jnp.broadcast_to(size, shear.shape), steps, 4)
     bulk = lame + (2.0 / 3.0) * shear
@@ -265,22 +350,39 @@
             rows, lanes = block(index, *parity)
             spectrum[rows, lanes] = second(phi, parity, a, b) + sheared
     moved = table_by(bwd_ref[0], bwd_ref[1], by_table(spectrum[...], table[0], table[1], dot_t))
+    if 2 * planes == 8:
+        low = row_position((2 * planes, columns)) < planes
+        for pair in range(3):
+            for chip in range(devices // 2):
+                first, second_ = (
+                    moved[i * vox + 2 * chip * planes : i * vox + 2 * (chip + 1) * planes]
+                    for i in (2 * pair, 2 * pair + 1)
+                )
+                rows = slice(2 * pair * planes, 2 * (pair + 1) * planes)
+                ordered[2 * chip, rows] = jnp.where(low, first, pltpu.roll(second_, planes, 0))
+                ordered[2 * chip + 1, rows] = jnp.where(low, pltpu.roll(first, planes, 0), second_)
+    else:
+        for i in range(6):
+            for device in range(devices):
+                ordered[device, i * planes : (i + 1) * planes] = moved[
+                    i * vox + device * planes : i * vox + (device + 1) * planes
+                ]
+    for device in range(devices):
+        sent_ref[device] = ordered[device].astype(bf16)
     strain = [load[i] + moved[i * vox : (i + 1) * vox] for i in range(6)]
-    planes = strain_ref.shape[2]
-    for i in range(6):
-        for device in range(strain_ref.shape[0]):
-            strain_ref[device, i] = strain[i][device * planes : (device + 1) * planes]
     trace, dev = deviator_of(strain)
     left, ratio = remaining(shear, measure([0.5 * part for part in dev]), steps, 4)
     push = bulk * trace
     pull = 2.0 * shear * left
     stress = [push + pull * dev[i] for i in range(3)] + [pull * dev[i] for i in range(3, 6)]
     parts = stress + [lame, shear / (1.0 + ratio)]
-    lane = lane_position(response_ref.shape)
-    row = jnp.zeros(response_ref.shape, f32)
+    lane = lane_position((1, response_ref.shape[1]))
+    row = jnp.zeros(lane.shape, f32)
     for index, part in enumerate(parts):
         row = jnp.where(lane == index, total(part) / float(vox * columns), row)
-    response_ref[...] = row
+    for index, part in enumerate(load):
+        row = jnp.where(lane == 8 + index, part, row)
+    response_ref[...] = jnp.broadcast_to(row, response_ref.shape)
 
 
 def vox_width(columns):
@@ -289,9 +391,10 @@
 
 
 def macro_kernel(
-    slots_ref, table_ref, table_v_ref, mesh_ref, force_in_ref, next_ref, row_ref, fields, forces, cells, result
+    layers, base, slots_ref, table_ref, table_v_ref, packet_ref, next_ref, row_ref, fields, cells, result
 ):
-    devices, _, planes, columns = mesh_ref.shape
+    columns = next_ref.shape[2]
+    devices = fields.shape[1] // layers
     samples = table_v_ref.shape[0]
     rank = lax.axis_index("dev")
     group = lax.axis_index("grp")
@@ -302,16 +405,15 @@
         chosen = jnp.int32(0)
         for j in range(group_size):
             chosen = jnp.where(slots_ref[start + j] == rank * local_count + local, start + j, chosen)
-        row_ref[local : local + 1, :] = table_v_ref[pl.ds(chosen, 1), :]
-    gather_rows(mesh_ref, fields)
-    gather_rows(force_in_ref, forces)
+        row_ref[local : local + 1, :] = table_v_ref[pl.ds(chosen, 1), 0:8]
+    read_fields(packet_ref, base, layers, fields)
     rows = fields.shape[1]
     height = min(8, rows)
     span = min(512, columns)
     for top in range(0, rows, height):
         for side in range(0, columns, span):
             where = (slice(top, top + height), slice(side, side + span))
-            label = fields[(3,) + where]
+            label = fields[(6,) + where]
 
             def pick(sample, held):
                 here = label == sample.astype(f32)
@@ -321,10 +423,10 @@
             held = lax.fori_loop(0, samples, pick, (zero,) * 8, unroll=4)
             for c in range(8):
                 cells[(c,) + where] = held[c]
-    stencil = Stencil(fields.shape[1:], vox_width(columns))
+    stencil = Stencil(fields.shape[1:], vox_width(columns), devices)
     stress = [cells[c] for c in range(6)]
     pulled = stencil.force(stress)
-    remainder = [forces[b] - pulled[b] - spring_rate * fields[b] for b in range(3)]
+    remainder = [fields[3 + b] - pulled[b] - spring_rate * fields[b] for b in range(3)]
     direction = remainder
     norm_now = total(sum(r * r for r in remainder))
     update = None
@@ -347,9 +449,9 @@
             norm_now = norm_next
     for b in range(3):
         done = fields[b] + update[b]
-        for device in range(devices):
-            result[device, b] = done[device * planes : (device + 1) * planes]
-    next_ref[...] = result[rank]
+        result[b] = done
+        for layer in range(layers):
+            next_ref[b, layer : layer + 1, :] = result[b, pl.ds(layer * devices + rank, 1), :]
 
 
 def vmem():
@@ -371,71 +473,82 @@
     layers = displacement.shape[1]
     width = displacement.shape[2] * displacement.shape[3]
     plane, forward_line, backward_line, multipliers = tables(vox)
-    params = pltpu.CompilerParams(vmem_limit_bytes=48 * 1024 * 1024)
-
-    def spread(block):
-        return lax.all_to_all(
-            jnp.broadcast_to(block[None], (devices,) + block.shape), "dev", split_axis=0, concat_axis=0, tiled=True
-        )
-
-    mesh_part = jnp.concatenate([displacement, element_sample[None].astype(f32)]).reshape(4, layers, width)
-    mesh_all = spread(mesh_part)
-    force_all = spread(external_force.reshape(3, layers, width))
-    moduli = []
-    for field in (lame_field, shear_field):
-        own = lax.all_to_all(
-            field.reshape(devices, local_count, planes, columns), "dev", split_axis=0, concat_axis=0, tiled=True
-        )
-        moduli.append(own)
-    strains = []
+    params = pltpu.CompilerParams(vmem_limit_bytes=60 * 1024 * 1024)
+
+    side = displacement.shape[3]
+    lines = layers * displacement.shape[2]
+    tiles = columns // LANES
+    base = local_count * planes * tiles
+    length = base + (6 * layers + (layers + 1) // 2) * tiles
+    packet = pl.pallas_call(
+        functools.partial(pack_kernel, layers),
+        name="pack",
+        out_shape=jax.ShapeDtypeStruct((devices, length, LANES), f32),
+        in_specs=[vmem()] * 5,
+        out_specs=vmem(),
+        scratch_shapes=[pltpu.VMEM((7 * lines, LANES), f32)],
+        compiler_params=params,
+    )(
+        displacement.reshape(3 * lines, side), external_force.reshape(3 * lines, side),
+        element_sample.reshape(lines, side),
+        lame_field.reshape(devices, local_count, planes, columns),
+        shear_field.reshape(devices, local_count, planes, columns),
+    )
+    packets = lax.all_to_all(packet, "dev", split_axis=0, concat_axis=0, tiled=True).reshape(devices * length, LANES)
+    everyone = groups * devices
+    sents = []
     rows = []
     for local in range(local_count):
-        lame_own, shear_own = (field[:, local].reshape(vox, columns) for field in moduli)
-        strain, response = pl.pallas_call(
-            functools.partial(micro_kernel, local, local_count),
+        sent, response = pl.pallas_call(
+            functools.partial(micro_kernel, local, local_count, layers),
             name="micro",
             out_shape=(
-                jax.ShapeDtypeStruct((devices, 6, planes, columns), f32),
-                jax.ShapeDtypeStruct((1, 8), f32),
+                jax.ShapeDtypeStruct((devices, 6 * planes, columns), bf16),
+                jax.ShapeDtypeStruct((everyone, 16), f32),
             ),
-            in_specs=[smem()] + [vmem()] * 6 + [pl.BlockSpec(memory_space=pl.ANY)],
+            in_specs=[smem(), vmem()] + [pl.BlockSpec(memory_space=pltpu.HBM)] * 4,
             out_specs=(vmem(), vmem()),
             scratch_shapes=[
-                pltpu.VMEM((4, devices * layers, width), f32),
+                pltpu.VMEM((7, devices * layers, width), f32),
+                pltpu.VMEM((2, vox, columns), f32),
+                pltpu.VMEM(multipliers.shape, f32),
+                pltpu.VMEM(forward_line.shape, bf16),
+                pltpu.VMEM(backward_line.shape, bf16),
                 pltpu.VMEM(plane.shape, bf16),
-                pltpu.SemaphoreType.DMA((2,)),
                 pltpu.VMEM((6 * vox, columns), f32),
+                pltpu.VMEM((devices, 6 * planes, columns), f32),
+                pltpu.SemaphoreType.DMA((3 + 16,)),
             ],
             compiler_params=params,
-        )(plastic_steps, mesh_all, lame_own, shear_own, multipliers, forward_line, backward_line, plane)
-        strains.append(strain)
+        )(
+            plastic_steps, packets, multipliers, forward_line, backward_line, plane,
+        )
+        sents.append(sent)
         rows.append(response)
-    own_rows = rows[0] if local_count == 1 else jnp.concatenate(rows)
-    everyone = groups * devices
     gathered = lax.all_to_all(
-        jnp.broadcast_to(own_rows[None], (everyone,) + own_rows.shape),
-        ("grp", "dev"), split_axis=0, concat_axis=0, tiled=True,
-    ).reshape(everyone * local_count, 8)
-    sent = jnp.stack(strains, axis=1)
-    moved = lax.all_to_all(sent, "dev", split_axis=0, concat_axis=0, tiled=True)
-    micro_strain = jnp.transpose(moved, (2, 0, 1, 3, 4)).reshape(6, group_size, planes, columns)
+        jnp.stack(rows, axis=1), ("grp", "dev"), split_axis=0, concat_axis=0, tiled=True
+    ).reshape(everyone * local_count, 16)
+    moved = lax.all_to_all(jnp.stack(sents, axis=1), "dev", split_axis=0, concat_axis=0, tiled=True)
+    group_rows = lax.dynamic_slice_in_dim(gathered, lax.axis_index("grp") * group_size, group_size)
+    loads = group_rows[:, 8:14].T
+    change = jnp.transpose(moved.reshape(group_size, 6, planes, columns), (1, 0, 2, 3))
+    micro_strain = loads[:, :, None, None] + change.astype(f32)
     following, picked = pl.pallas_call(
-        macro_kernel,
+        functools.partial(macro_kernel, layers, base),
         name="macro",
         out_shape=(
             jax.ShapeDtypeStruct((3, layers, width), f32),
             jax.ShapeDtypeStruct((local_count, 8), f32),
         ),
-        in_specs=[smem(), smem()] + [vmem()] * 3,
+        in_specs=[smem(), smem()] + [vmem()] * 2,
         out_specs=(vmem(), vmem()),
         scratch_shapes=[
-            pltpu.VMEM((4, devices * layers, width), f32),
+            pltpu.VMEM((7, devices * layers, width), f32),
+            pltpu.VMEM((8, devices * layers, width), f32),
             pltpu.VMEM((3, devices * layers, width), f32),
-            pltpu.VMEM((8, devices * layers, width), f32),
-            pltpu.VMEM((devices, 3, layers, width), f32),
         ],
         compiler_params=params,
-    )(owner_slot, gathered, gathered, mesh_all, force_all)
+    )(owner_slot, gathered, gathered, packets)
     return (following.reshape(displacement.shape), picked, micro_strain)
 
 

time: 90.5 us -> 61.5 us (0.68)
  waiting for transfers between devices: 27.1 us -> 4.41 us
  starting transfers between devices: 13.7 us -> 3.45 us
  local copies, waits for them, and re-layouts: 10.8 us -> 1.9 us
  blocking collectives: 25.2 us -> 33.1 us
  Pallas kernels: 11.4 us -> 16.5 us
    all_to_all x4 -> x1, waiting for transfers between devices: 27.1 us -> 4.41 us  [shards(): lax.all_to_all(jnp.stack(sents, axis=1), 'dev', split_axis=0, concat_axis...]
    all_to_all x4 -> x1, starting transfers between devices: 13.7 us -> 3.45 us  [shards(): lax.all_to_all(jnp.stack(sents, axis=1), 'dev', split_axis=0, concat_axis...]
    all_to_all x2, blocking collectives: 25.2 us -> 33.1 us  [the longest x1 22.5 us: shards(): lax.all_to_all(packet, 'dev', split_axis=0, concat_axis=0, tiled=True)]
    unnamed x13 -> x2, local copies, waits for them, and re-layouts: 6.38 us -> 0.01 us
    pallas_call x2 -> x3, Pallas kernels: 11.4 us -> 16.5 us  [the longest x1 8.03 us: shards(): pl.pallas_call(functools.partial(micro_kernel, local, local_count, layers...]
    broadcast_in_dim x4 -> x0, local copies, waits for them, and re-layouts: 2.53 us -> none  [the longest x3 2.52 us: spread(): jnp.broadcast_to(block[None], (devices,) + block.shape)]
    concatenate x2 -> x0, local copies, waits for them, and re-layouts: 1.09 us -> none  [shards(): jnp.concatenate([displacement, element_sample[None].astype(f32)])]
    add x0 -> x1, other arithmetic: none -> 1.08 us  [shards(): micro_strain = loads[:, :, None, None] + change.astype(f32)]
  transfers between devices with their start and end apart: 4 -> 1, of which waited for: 3 -> 1; matrix products, arithmetic and copies ran while one was open for 4% -> 3% of each run, Pallas kernels for 13% -> 10%
where the time goes in v2:
time: 61.5 us; the launch traced here: 61.1 us
  blocking collectives  33.1 us (54%)
  Pallas kernels  16.5 us (27%)
  waiting for transfers between devices  4.41 us (7%)
  starting transfers between devices  3.45 us (6%)
  local copies, waits for them, and re-layouts  1.9 us (3%)
  other arithmetic  1.08 us (2%)
  between operations  0.67 us (1%)
    all_to_all x1, blocking collectives, shards(): lax.all_to_all(packet, 'dev', split_axis=0, concat_axis=0, tiled=True)  22.5 us
    all_to_all x1, blocking collectives, shards(): lax.all_to_all(jnp.stack(rows, axis=1), ('grp', 'dev'), split_axis=0, con...  10.6 us
    pallas_call x1, Pallas kernels, shards(): pl.pallas_call(functools.partial(micro_kernel, local, local_count, layers...  8.03 us
    pallas_call x1, Pallas kernels, shards(): pl.pallas_call(functools.partial(macro_kernel, layers, base), name='macro...  6.4 us
    all_to_all x1, waiting for transfers between devices, shards(): lax.all_to_all(jnp.stack(sents, axis=1), 'dev', split_axis=0, concat_axis...  4.41 us
    all_to_all x1, starting transfers between devices, shards(): lax.all_to_all(jnp.stack(sents, axis=1), 'dev', split_axis=0, concat_axis...  3.45 us
    pallas_call x1, Pallas kernels, shards(): pl.pallas_call(functools.partial(pack_kernel, layers), name='pack', out_s...  2.06 us
    reshape x1, local copies, waits for them, and re-layouts, shards(): return (following.reshape(displacement.shape), picked, micro_strain)  1.48 us
  transfers between devices with their start and end apart: 1, of which 1 were waited for; matrix products, arithmetic and copies ran while one was open for 3% of the time, Pallas kernels for 10%

profile of v2, /device:TPU:0, one launch (start us, length us, event | category | flops | bytes accessed | tf_op | source)
XLA Modules:
  0.0 61.1 jit_solution(5161864515883234016)
XLA Ops:
  0.6 2.1 %pack.1 = f32[8,136,128]{2,1,0:T(8,128)} custom-call(f32[192,32]{1,0:T(8,128)} %bitcast.28, f32[192,32]{1,0:T(8,128)} %bitcast.29, s32[64,32]{1,0:T(8,128)} %bitcast.32, bf16[8,1,4,1024]{3,2,1,0:T(4,128)(2,1)} %bitcast.30, bf16[8,1,4,1024]{3,2,1,0:T(4,128)(2,1)} %bitcast.31), custom_call_target="tpu_custom_call" | custom-call | tf_op jit(solution)/shard_map/pack/pallas_call | solution.py:483
  2.7 22.5 %all_to_all.15 = f32[8,136,128]{2,1,0:T(8,128)} all-to-all(f32[8,136,128]{2,1,0:T(8,128)} %pack.1), channel_id=1, replica_groups=mesh['grp'=4,'dev'=8] {'dev'}, dimensions={0} | all-to-all | bytes 1114112 | tf_op jit(solution)/shard_map/all_to_all | solution.py:497
  25.2 8.0 %micro.1 = (bf16[8,24,1024]{2,1,0:T(8,128)(2,1)}, f32[32,16]{1,0:T(8,128)}) custom-call(s32[32]{0:T(128)} %steps_ref.1, f32[1088,128]{1,0:T(8,128)} %bitcast.22, f32[8,16,256]{2,1,0:T(8,128)} %constant.20.clone.mult_hbm, bf16[2,64,64]{2,1,0:T(8,128)(2,1)} %constant.21.clone.fwd_hbm, bf16[2,192,192]{2,1,0:T(8,128)(2,1)} %constant.22.clone.bwd_hbm, ...), custom_call_target="tpu_custom_call" | custom-call | tf_op jit(solution)/shard_map/micro/pallas_call | solution.py:502
  33.2 10.6 %all_to_all.16 = f32[32,1,16]{2,1,0:T(1,128)S(1)} all-to-all(f32[32,1,16]{2,1,0:T(1,128)} %bitcast.33), channel_id=1, replica_groups=mesh['grp'=4,'dev'=8] {'grp','dev'}, dimensions={0} | all-to-all | bytes 4096 | tf_op jit(solution)/shard_map/all_to_all | solution.py:528
  43.8 0.0 copy-start
  43.8 3.5 %all-to-all-start.2 = ((bf16[8,1,24,1024]{3,2,1,0:T(8,128)(2,1)}), bf16[8,1,24,1024]{3,2,1,0:T(8,128)(2,1)S(1)}, u32[]{:S(2)}, u32[]{:S(2)}) async-start(bf16[8,1,24,1024]{3,2,1,0:T(8,128)(2,1)} %bitcast.24), calls=%async_computation.2 | async-start | bytes 786432 | tf_op jit(solution)/shard_map/all_to_all | solution.py:531
  47.3 0.1 slice_bitcast_fusion
  47.4 0.1 copy.18
  47.5 0.0 copy-done
  47.5 6.4 %macro.1 = (f32[3,2,1024]{2,1,0:T(2,128)}, f32[1,8]{1,0:T(1,128)}) custom-call(s32[32]{0:T(128)} %slots_ref.1, f32[32,16]{1,0:T(8,128)} %bitcast.26, f32[32,16]{1,0:T(8,128)} %bitcast.27, f32[1088,128]{1,0:T(8,128)} %bitcast.23), custom_call_target="tpu_custom_call" | custom-call | tf_op jit(solution)/shard_map/macro/pallas_call | solution.py:536
  53.9 1.5 %reshape.42 = f32[3,2,32,32]{3,2,1,0:T(8,128)} reshape(f32[3,2,1024]{2,1,0:T(2,128)} %get-tuple-element.8) | data formatting | bytes 49152 | tf_op jit(solution)/shard_map/reshape | solution.py:552
  55.4 4.4 %all-to-all-done.2 = bf16[8,1,24,1024]{3,2,1,0:T(8,128)(2,1)S(1)} async-done(((bf16[8,1,24,1024]{3,2,1,0:T(8,128)(2,1)}), bf16[8,1,24,1024]{3,2,1,0:T(8,128)(2,1)S(1)}, u32[]{:S(2)}, u32[]{:S(2)}) %all-to-all-start.2) | async-done | bytes 393248 | tf_op jit(solution)/shard_map/all_to_all | solution.py:531
  59.8 0.2 reshape.43
  60.0 1.1 %bitcast_add_fusion = f32[6,8,4,1024]{3,2,1,0:T(4,128)} fusion(f32[8,6,4,1024]{3,2,1,0:T(4,128)S(1)} %reshape.43, f32[6,8]{1,0:T(8,128)S(1)} %copy.18), kind=kLoop, calls=%fused_computation | loop fusion | flops 196608 | bytes 1573056 | tf_op jit(solution)/shard_map/add | solution.py:535
  (1 shorter events, 0.0 us)
Async XLA Ops:
  43.8 3.6 %copy-start = (f32[32,1,16]{2,1,0:T(1,128)}, f32[32,1,16]{2,1,0:T(1,128)S(1)}, u32[]{:S(2)}) copy-start(f32[32,1,16]{2,1,0:T(1,128)S(1)} %all_to_all.16) | copy-start | bytes 6148
  43.8 15.9 %all-to-all-start.2 = ((bf16[8,1,24,1024]{3,2,1,0:T(8,128)(2,1)}), bf16[8,1,24,1024]{3,2,1,0:T(8,128)(2,1)S(1)}, u32[]{:S(2)}, u32[]{:S(2)}) async-start(bf16[8,1,24,1024]{3,2,1,0:T(8,128)(2,1)} %bitcast.24), calls=%async_computation.2 | async-start | bytes 786432 | tf_op jit(solution)/shard_map/all_to_all | solution.py:531

commit v3 on v2

--- a/solution.py
+++ b/solution.py
@@ -37,15 +37,17 @@
     cosine[:, 0] = 1.0 / np.sqrt(vox)
     sine[:, 0] = (1.0 - 2.0 * (np.arange(vox) % 2)) / np.sqrt(vox)
     basis = np.concatenate([cosine, sine], axis=1)
+    order = np.concatenate([np.arange(0, half, 2), np.arange(1, half, 2)])
     by_parity = basis.reshape(vox, 2, half)
-    plane = np.einsum("ypk,zql->yzqpkl", by_parity, by_parity).reshape(vox * vox, vox * vox)
+    folded = by_parity[:half, :, order].reshape(half, 2, 2, half // 2)
+    plane = np.einsum("ypek,zql->eyzqpkl", folded, by_parity).reshape(2, half * vox, half * vox)
     line = basis.T
     forward_line = np.kron(np.eye(2), line)
     backward_line = np.kron(np.eye(6), line.T)
     wave = np.sin(2.0 * np.pi * np.arange(half) / vox)
     wave[0] = 0.0
     first = np.broadcast_to(wave[:, None, None], (half, half, half))
-    second = np.broadcast_to(wave[None, :, None], (half, half, half))
+    second = np.broadcast_to(wave[order][None, :, None], (half, half, half))
     third = np.broadcast_to(wave[None, None, :], (half, half, half))
     square = first**2 + second**2 + third**2
     inverse = np.where(square > 0.0, 1.0 / np.where(square > 0.0, square, 1.0), 0.0)
@@ -81,6 +83,21 @@
     value_high, value_low = split(value)
     both = dot(jnp.concatenate([high, low], axis=0), value_high)
     return both[:rows] + both[rows:] + dot(high, value_low)
+
+
+def forward_plane(value, table):
+    half = value.shape[1] // 2
+    low, high = value[:, :half], value[:, half:]
+    even = by_table(low + high, table[0, 0], table[1, 0], dot)
+    odd = by_table(low - high, table[0, 1], table[1, 1], dot)
+    return jnp.concatenate([even, odd], axis=1)
+
+
+def backward_plane(value, table):
+    half = value.shape[1] // 2
+    even = by_table(value[:, :half], table[0, 0], table[1, 0], dot_t)
+    odd = by_table(value[:, half:], table[0, 1], table[1, 1], dot_t)
+    return jnp.concatenate([even + odd, even - odd], axis=1)
 
 
 def lane_position(shape):
@@ -205,7 +222,7 @@
     return high * (1.0 / LAME_UNIT), (code - high * CODE_BASE) * (1.0 / SHEAR_UNIT)
 
 
-def pack_kernel(layers, moved_ref, force_ref, sample_ref, lame_ref, shear_ref, packet_ref, wide):
+def pack_kernel(layers, moved_ref, sample_ref, force_ref, lame_ref, shear_ref, packet_ref, wide):
     devices, local_count, planes, columns = lame_ref.shape
     tiles = columns // LANES
     for device in range(devices):
@@ -218,7 +235,7 @@
     width = moved_ref.shape[1]
     beside = LANES // width
     start = 0
-    for ref in (moved_ref, force_ref, sample_ref):
+    for ref in (moved_ref, sample_ref, force_ref):
         rows = ref.shape[0]
         wide[start : start + rows, :] = jnp.concatenate([ref[...].astype(f32)] * beside, axis=1)
         start += rows
@@ -227,60 +244,83 @@
     merged = wide[pl.ds(0, count, stride=beside), :]
     for place in range(1, beside):
         merged = jnp.where(slot == place, wide[pl.ds(place, count, stride=beside), :], merged)
-    nodes = 6 * count // 7
-    each = (count - nodes) // layers
+    nodes = 3 * count // 7
+    each = nodes // (3 * layers)
     base = local_count * planes * tiles
+    spare = base + nodes + (layers + 1) // 2 * each
     for device in range(devices):
         packet_ref[device, base : base + nodes, :] = merged[:nodes]
     for pair in range((layers + 1) // 2):
-        first = merged[nodes + 2 * pair * each : nodes + (2 * pair + 1) * each]
+        at = nodes + 2 * pair * each
+        label = merged[at : at + each] * LABEL_BASE
         if 2 * pair + 1 < layers:
-            first = first * LABEL_BASE + merged[nodes + (2 * pair + 1) * each : nodes + (2 * pair + 2) * each]
-        else:
-            first = first * LABEL_BASE
+            label = label + merged[at + each : at + 2 * each]
         for device in range(devices):
-            packet_ref[device, base + nodes + pair * each : base + nodes + (pair + 1) * each, :] = first
+            packet_ref[device, base + nodes + pair * each : base + nodes + (pair + 1) * each, :] = label
+    part = force_rows(layers) * each
+    for device in range(devices):
+        start = count - nodes if device % 2 == 0 else count - part
+        packet_ref[device, spare : spare + part, :] = merged[start : start + part]
+
+
+def force_rows(layers):
+    return (3 * layers + 1) // 2
 
 
 def read_fields(packet_ref, base, layers, fields):
-    parts, rows, columns = fields.shape
+    _, rows, columns = fields.shape
     devices = rows // layers
     tiles = columns // LANES
     step = packet_ref.shape[0] // devices
-    for part in range(parts):
+    for part in range(4):
         for layer in range(layers):
             for tile in range(tiles):
-                if part < 6:
-                    at = base + (part * layers + layer) * tiles + tile
-                    piece = packet_ref[pl.ds(at, devices, stride=step), :]
-                else:
-                    at = base + (6 * layers + layer // 2) * tiles + tile
-                    both = packet_ref[pl.ds(at, devices, stride=step), :]
-                    high = jnp.floor(both * (1.0 / LABEL_BASE))
-                    piece = high if layer % 2 == 0 else both - high * LABEL_BASE
+                row = part * layers + (layer if part < 3 else layer // 2)
+                piece = packet_ref[pl.ds(base + row * tiles + tile, devices, stride=step), :]
+                if part == 3:
+                    high = jnp.floor(piece * (1.0 / LABEL_BASE))
+                    piece = high if layer % 2 == 0 else piece - high * LABEL_BASE
                 fields[part, layer * devices : (layer + 1) * devices, tile * LANES : (tile + 1) * LANES] = piece
 
 
+def read_force(packet_ref, other_ref, base, layers, forces, even):
+    _, rows, columns = forces.shape
+    devices = rows // layers
+    tiles = columns // LANES
+    step = packet_ref.shape[0] // devices
+    start = base + (3 * layers + (layers + 1) // 2) * tiles
+    held = force_rows(layers)
+    for part in range(3):
+        for layer in range(layers):
+            row = part * layers + layer
+            first = row < held
+            local = row if first else row - (3 * layers - held)
+            for tile in range(tiles):
+                at = pl.ds(start + local * tiles + tile, devices, stride=step)
+                mine, other = packet_ref[at, :], other_ref[at, :]
+                piece = jnp.where(even, mine, other) if first else jnp.where(even, other, mine)
+                forces[part, layer * devices : (layer + 1) * devices, tile * LANES : (tile + 1) * LANES] = piece
+
+
 def micro_kernel(
-    local, local_count, layers, steps_ref, packet_ref, mult_hbm, fwd_hbm, bwd_hbm, table_hbm,
-    sent_ref, response_ref, fields, moduli, mult_ref, fwd_ref, bwd_ref, table, spectrum, ordered, sem
+    local, local_count, layers, steps_hbm, packet_hbm, mult_hbm, fwd_hbm, bwd_hbm, table_hbm,
+    sent_hbm, response_ref, packet_ref, fields, moduli, mult_ref, fwd_ref, bwd_ref, table, spectrum, ordered, sent_ref, steps_ref, sem
 ):
     devices, planes = sent_ref.shape[0], sent_ref.shape[1] // 6
     vox, columns = moduli.shape[1:]
     half = vox // 2
     quarter = half * half
     width = vox_width(fields.shape[2])
-    pairs = [(mult_hbm, mult_ref), (fwd_hbm, fwd_ref), (bwd_hbm, bwd_ref)]
-    pieces = sem.shape[0] - len(pairs)
-    height = columns // (pieces // 2)
-    for piece in range(pieces):
-        where = (piece * height // columns, pl.ds(piece * height % columns, height))
-        pairs.append((table_hbm.at[where], table.at[where]))
+    pairs = [(packet_hbm, packet_ref), (steps_hbm, steps_ref)]
+    pairs += [(table_hbm.at[part, fold], table.at[part, fold]) for fold in range(2) for part in range(2)]
+    pairs += [(fwd_hbm, fwd_ref), (mult_hbm, mult_ref), (bwd_hbm, bwd_ref)]
     copies = [pltpu.make_async_copy(source, target, sem.at[i]) for i, (source, target) in enumerate(pairs)]
     for copy in copies:
         copy.start()
     own = (lax.axis_index("grp") * lax.axis_size("dev") + lax.axis_index("dev")) * local_count + local
+    copies[1].wait()
     steps = steps_ref[own]
+    copies[0].wait()
     tiles = columns // LANES
     step = packet_ref.shape[0] // devices
     read_fields(packet_ref, local_count * planes * tiles, layers, fields)
@@ -294,7 +334,7 @@
                 ] = value
     stencil = Stencil(fields.shape[1:], width, fields.shape[1] // layers)
     mesh_strain = stencil.strain([fields[c] for c in range(3)])
-    mine = fields[6] == own.astype(f32)
+    mine = fields[3] == own.astype(f32)
     count = total(jnp.where(mine, 1.0, 0.0))
     load = [total(jnp.where(mine, part, 0.0)) / count for part in mesh_strain]
     trace, dev = deviator_of(load)
@@ -304,14 +344,18 @@
     left, _ = remaining(shear, jnp.broadcast_to(size, shear.shape), steps, 4)
     bulk = lame + (2.0 / 3.0) * shear
     sources = jnp.concatenate([bulk * trace, 2.0 * shear * left], axis=0)
-    for copy in copies:
+    for copy in copies[2:]:
         copy.wait()
-    spectral = table_by(fwd_ref[0], fwd_ref[1], by_table(sources, table[0], table[1], dot))
+    spectral = table_by(fwd_ref[0], fwd_ref[1], forward_plane(sources, table))
 
     def block(field, px, py, pz):
         rows = slice(field * vox + px * half, field * vox + (px + 1) * half)
-        lanes = slice((pz * 2 + py) * quarter, (pz * 2 + py + 1) * quarter)
-        return rows, lanes
+        start = (pz * 2 + py) * quarter // 2
+        return rows, [slice(fold * 2 * quarter + start, fold * 2 * quarter + start + quarter // 2) for fold in range(2)]
+
+    def take(field, parity):
+        rows, pieces = block(field, *parity)
+        return jnp.concatenate([spectral[rows, lanes] for lanes in pieces], axis=1)
 
     parities = [(px, py, pz) for px in range(2) for py in range(2) for pz in range(2)]
     product = [mult_ref[i] for i in range(6)]
@@ -328,16 +372,14 @@
     psi = {}
     raw = {}
     for parity in parities:
-        rows, lanes = block(1, *parity)
-        raw[parity] = spectral[rows, lanes]
+        raw[parity] = take(1, parity)
         psi[parity] = inverse * raw[parity]
     phi = {}
     for parity in parities:
-        rows, lanes = block(0, *parity)
         pressed = sum(
             (1.0 if a == b else 2.0) * dev[SLOT[(a, b)]] * second(psi, parity, a, b) for a, b in PAIRS
         )
-        phi[parity] = (1.0 - green_ratio) * inverse * spectral[rows, lanes] + scaled * pressed
+        phi[parity] = (1.0 - green_ratio) * inverse * take(0, parity) + scaled * pressed
     for parity in parities:
         curl = {pair: second(psi, parity, *pair) for pair in PAIRS}
         for index, (a, b) in enumerate(PAIRS):
@@ -347,9 +389,11 @@
                 sheared = sum(dev[SLOT[(b, c)]] * at(a, c) for c in range(3))
             else:
                 sheared = 0.5 * sum(dev[SLOT[(b, c)]] * at(a, c) + dev[SLOT[(a, c)]] * at(b, c) for c in range(3))
-            rows, lanes = block(index, *parity)
-            spectrum[rows, lanes] = second(phi, parity, a, b) + sheared
-    moved = table_by(bwd_ref[0], bwd_ref[1], by_table(spectrum[...], table[0], table[1], dot_t))
+            value = second(phi, parity, a, b) + sheared
+            rows, pieces = block(index, *parity)
+            for fold, lanes in enumerate(pieces):
+                spectrum[rows, lanes] = value[:, fold * quarter // 2 : (fold + 1) * quarter // 2]
+    moved = table_by(bwd_ref[0], bwd_ref[1], backward_plane(spectrum[...], table))
     if 2 * planes == 8:
         low = row_position((2 * planes, columns)) < planes
         for pair in range(3):
@@ -369,6 +413,8 @@
                 ]
     for device in range(devices):
         sent_ref[device] = ordered[device].astype(bf16)
+    send = pltpu.make_async_copy(sent_ref, sent_hbm, sem.at[len(pairs)])
+    send.start()
     strain = [load[i] + moved[i * vox : (i + 1) * vox] for i in range(6)]
     trace, dev = deviator_of(strain)
     left, ratio = remaining(shear, measure([0.5 * part for part in dev]), steps, 4)
@@ -383,6 +429,7 @@
     for index, part in enumerate(load):
         row = jnp.where(lane == 8 + index, part, row)
     response_ref[...] = jnp.broadcast_to(row, response_ref.shape)
+    send.wait()
 
 
 def vox_width(columns):
@@ -391,7 +438,7 @@
 
 
 def macro_kernel(
-    layers, base, slots_ref, table_ref, table_v_ref, packet_ref, next_ref, row_ref, fields, cells, result
+    layers, base, slots_ref, table_ref, table_v_ref, packet_ref, other_ref, next_ref, row_ref, fields, forces, cells, result
 ):
     columns = next_ref.shape[2]
     devices = fields.shape[1] // layers
@@ -407,13 +454,14 @@
             chosen = jnp.where(slots_ref[start + j] == rank * local_count + local, start + j, chosen)
         row_ref[local : local + 1, :] = table_v_ref[pl.ds(chosen, 1), 0:8]
     read_fields(packet_ref, base, layers, fields)
+    read_force(packet_ref, other_ref, base, layers, forces, rank % 2 == 0)
     rows = fields.shape[1]
     height = min(8, rows)
     span = min(512, columns)
     for top in range(0, rows, height):
         for side in range(0, columns, span):
             where = (slice(top, top + height), slice(side, side + span))
-            label = fields[(6,) + where]
+            label = fields[(3,) + where]
 
             def pick(sample, held):
                 here = label == sample.astype(f32)
@@ -426,7 +474,7 @@
     stencil = Stencil(fields.shape[1:], vox_width(columns), devices)
     stress = [cells[c] for c in range(6)]
     pulled = stencil.force(stress)
-    remainder = [fields[3 + b] - pulled[b] - spring_rate * fields[b] for b in range(3)]
+    remainder = [forces[b] - pulled[b] - spring_rate * fields[b] for b in range(3)]
     direction = remainder
     norm_now = total(sum(r * r for r in remainder))
     update = None
@@ -458,6 +506,10 @@
     return pl.BlockSpec(memory_space=pltpu.VMEM)
 
 
+def hbm():
+    return pl.BlockSpec(memory_space=pltpu.HBM)
+
+
 def smem():
     return pl.BlockSpec(memory_space=pltpu.SMEM)
 
@@ -479,7 +531,7 @@
     lines = layers * displacement.shape[2]
     tiles = columns // LANES
     base = local_count * planes * tiles
-    length = base + (6 * layers + (layers + 1) // 2) * tiles
+    length = base + (3 * layers + (layers + 1) // 2 + force_rows(layers)) * tiles
     packet = pl.pallas_call(
         functools.partial(pack_kernel, layers),
         name="pack",
@@ -489,12 +541,13 @@
         scratch_shapes=[pltpu.VMEM((7 * lines, LANES), f32)],
         compiler_params=params,
     )(
-        displacement.reshape(3 * lines, side), external_force.reshape(3 * lines, side),
-        element_sample.reshape(lines, side),
+        displacement.reshape(3 * lines, side), element_sample.reshape(lines, side),
+        external_force.reshape(3 * lines, side),
         lame_field.reshape(devices, local_count, planes, columns),
         shear_field.reshape(devices, local_count, planes, columns),
     )
     packets = lax.all_to_all(packet, "dev", split_axis=0, concat_axis=0, tiled=True).reshape(devices * length, LANES)
+    neighbour = lax.ppermute(packets, "dev", [(i, i ^ 1) for i in range(devices)])
     everyone = groups * devices
     sents = []
     rows = []
@@ -506,10 +559,11 @@
                 jax.ShapeDtypeStruct((devices, 6 * planes, columns), bf16),
                 jax.ShapeDtypeStruct((everyone, 16), f32),
             ),
-            in_specs=[smem(), vmem()] + [pl.BlockSpec(memory_space=pltpu.HBM)] * 4,
-            out_specs=(vmem(), vmem()),
+            in_specs=[hbm()] * 6,
+            out_specs=(hbm(), vmem()),
             scratch_shapes=[
-                pltpu.VMEM((7, devices * layers, width), f32),
+                pltpu.VMEM((devices * length, LANES), f32),
+                pltpu.VMEM((4, devices * layers, width), f32),
                 pltpu.VMEM((2, vox, columns), f32),
                 pltpu.VMEM(multipliers.shape, f32),
                 pltpu.VMEM(forward_line.shape, bf16),
@@ -517,7 +571,9 @@
                 pltpu.VMEM(plane.shape, bf16),
                 pltpu.VMEM((6 * vox, columns), f32),
                 pltpu.VMEM((devices, 6 * planes, columns), f32),
-                pltpu.SemaphoreType.DMA((3 + 16,)),
+                pltpu.VMEM((devices, 6 * planes, columns), bf16),
+                pltpu.SMEM(plastic_steps.shape, jnp.int32),
+                pltpu.SemaphoreType.DMA((10,)),
             ],
             compiler_params=params,
         )(
@@ -540,15 +596,16 @@
             jax.ShapeDtypeStruct((3, layers, width), f32),
             jax.ShapeDtypeStruct((local_count, 8), f32),
         ),
-        in_specs=[smem(), smem()] + [vmem()] * 2,
+        in_specs=[smem(), smem()] + [vmem()] * 3,
         out_specs=(vmem(), vmem()),
         scratch_shapes=[
-            pltpu.VMEM((7, devices * layers, width), f32),
+            pltpu.VMEM((4, devices * layers, width), f32),
+            pltpu.VMEM((3, devices * layers, width), f32),
             pltpu.VMEM((8, devices * layers, width), f32),
             pltpu.VMEM((3, devices * layers, width), f32),
         ],
         compiler_params=params,
-    )(owner_slot, gathered, gathered, packets)
+    )(owner_slot, gathered, gathered, packets, neighbour)
     return (following.reshape(displacement.shape), picked, micro_strain)
 
 

time: 61.5 us -> 56.9 us (0.925)
  Pallas kernels: 16.5 us -> 14.1 us
  blocking collectives: 33.1 us -> 31 us
  waiting for transfers between devices: 4.41 us -> 3.09 us
  local copies, waits for them, and re-layouts: 1.9 us -> 2.66 us
    all_to_all x1, waiting for transfers between devices: 4.41 us -> 1.77 us  [shards(): lax.all_to_all(jnp.stack(sents, axis=1), 'dev', split_axis=0, concat_axis...]
    pallas_call x1, Pallas kernels: 8.03 us -> 5.51 us  [shards(): pl.pallas_call(functools.partial(micro_kernel, local, local_count, layers...]
    all_to_all x1, blocking collectives: 22.5 us -> 20.4 us  [shards(): lax.all_to_all(packet, 'dev', split_axis=0, concat_axis=0, tiled=True)]
    ppermute x0 -> x1, waiting for transfers between devices: none -> 1.32 us  [shards(): lax.ppermute(packets, 'dev', [(i, i ^ 1) for i in range(devices)])]
    unnamed x2 -> x6, local copies, waits for them, and re-layouts: 0.01 us -> 0.77 us
  transfers between devices with their start and end apart: 1 -> 2, of which waited for: 1 -> 2; matrix products, arithmetic and copies ran while one was open for 3% -> 3% of each run, Pallas kernels for 10% -> 12%
where the time goes in v3:
time: 56.9 us; the launch traced here: 56.4 us
  blocking collectives  31 us (54%)
  Pallas kernels  14.1 us (25%)
  starting transfers between devices  3.85 us (7%)
  waiting for transfers between devices  3.09 us (5%)
  local copies, waits for them, and re-layouts  2.66 us (5%)
  other arithmetic  1.08 us (2%)
  between operations  0.67 us (1%)
    all_to_all x1, blocking collectives, shards(): lax.all_to_all(packet, 'dev', split_axis=0, concat_axis=0, tiled=True)  20.4 us
    all_to_all x1, blocking collectives, shards(): lax.all_to_all(jnp.stack(rows, axis=1), ('grp', 'dev'), split_axis=0, con...  10.6 us
    pallas_call x1, Pallas kernels, shards(): pl.pallas_call(functools.partial(macro_kernel, layers, base), name='macro...  6.56 us
    pallas_call x1, Pallas kernels, shards(): pl.pallas_call(functools.partial(micro_kernel, local, local_count, layers...  5.51 us
    all_to_all x1, starting transfers between devices, shards(): lax.all_to_all(jnp.stack(sents, axis=1), 'dev', split_axis=0, concat_axis...  3.45 us
    pallas_call x1, Pallas kernels, shards(): pl.pallas_call(functools.partial(pack_kernel, layers), name='pack', out_s...  2.04 us
    all_to_all x1, waiting for transfers between devices, shards(): lax.all_to_all(jnp.stack(sents, axis=1), 'dev', split_axis=0, concat_axis...  1.77 us
    reshape x1, local copies, waits for them, and re-layouts, shards(): return (following.reshape(displacement.shape), picked, micro_strain)  1.48 us
  transfers between devices with their start and end apart: 2, of which 2 were waited for; matrix products, arithmetic and copies ran while one was open for 3% of the time, Pallas kernels for 12%

profile of v3, /device:TPU:0, one launch (start us, length us, event | category | flops | bytes accessed | tf_op | source)
XLA Modules:
  0.0 56.4 jit_solution(17122433508289192232)
XLA Ops:
  0.6 2.0 %pack.1 = f32[8,112,128]{2,1,0:T(8,128)} custom-call(f32[192,32]{1,0:T(8,128)} %bitcast.29, s32[64,32]{1,0:T(8,128)} %bitcast.33, f32[192,32]{1,0:T(8,128)} %bitcast.30, bf16[8,1,4,1024]{3,2,1,0:T(4,128)(2,1)} %bitcast.31, bf16[8,1,4,1024]{3,2,1,0:T(4,128)(2,1)} %bitcast.32), custom_call_target="tpu_custom_call" | custom-call | tf_op jit(solution)/shard_map/pack/pallas_call | solution.py:535
  2.7 20.4 %all_to_all.15 = f32[8,112,128]{2,1,0:T(8,128)} all-to-all(f32[8,112,128]{2,1,0:T(8,128)} %pack.1), channel_id=1, replica_groups=mesh['grp'=4,'dev'=8] {'dev'}, dimensions={0} | all-to-all | bytes 917504 | tf_op jit(solution)/shard_map/all_to_all | solution.py:549
  23.1 0.0 copy-start
  23.1 5.5 %micro.1 = (bf16[8,24,1024]{2,1,0:T(8,128)(2,1)}, f32[32,16]{1,0:T(8,128)}) custom-call(s32[32]{0:T(128)} %steps_hbm.1, f32[896,128]{1,0:T(8,128)} %bitcast.22, f32[8,16,256]{2,1,0:T(8,128)} %constant.20.clone.mult_hbm, bf16[2,64,64]{2,1,0:T(8,128)(2,1)} %constant.21.clone.fwd_hbm, bf16[2,192,192]{2,1,0:T(8,128)(2,1)} %constant.22.clone.bwd_hbm, ...), custom_call_target="tpu_custom_call" | custom-call | tf_op jit(solution)/shard_map/micro/pallas_call | solution.py:555
  28.6 10.6 %all_to_all.16 = f32[32,1,16]{2,1,0:T(1,128)S(1)} all-to-all(f32[32,1,16]{2,1,0:T(1,128)} %bitcast.34), channel_id=1, replica_groups=mesh['grp'=4,'dev'=8] {'grp','dev'}, dimensions={0} | all-to-all | bytes 4096 | tf_op jit(solution)/shard_map/all_to_all | solution.py:584
  39.1 0.0 copy-start.2
  39.1 3.5 %all-to-all-start.2 = ((bf16[8,1,24,1024]{3,2,1,0:T(8,128)(2,1)}), bf16[8,1,24,1024]{3,2,1,0:T(8,128)(2,1)S(1)}, u32[]{:S(2)}, u32[]{:S(2)}) async-start(bf16[8,1,24,1024]{3,2,1,0:T(8,128)(2,1)} %bitcast.25), calls=%async_computation.2 | async-start | bytes 786432 | tf_op jit(solution)/shard_map/all_to_all | solution.py:587
  42.6 0.0 copy-done
  42.6 0.4 collective-permute-start
  43.0 0.1 slice_bitcast_fusion
  43.1 0.1 copy.18
  43.2 1.3 %collective-permute-done.other_ref = f32[896,128]{1,0:T(8,128)S(1)} collective-permute-done((f32[896,128]{1,0:T(8,128)S(1)}, f32[896,128]{1,0:T(8,128)S(1)}, u32[]{:S(2)}, u32[]{:S(2)}) %collective-permute-start) | collective-permute-done | bytes 458784 | tf_op jit(solution)/shard_map/ppermute | solution.py:550
  44.5 0.0 copy-start.1
  44.5 0.0 copy-done.2
  44.5 0.8 %copy-done.1 = f32[896,128]{1,0:T(8,128)} copy-done((f32[896,128]{1,0:T(8,128)}, f32[896,128]{1,0:T(8,128)S(1)}, u32[]{:S(2)}) %copy-start.1) | copy-done | bytes 458776
  45.3 6.6 %macro.1 = (f32[3,2,1024]{2,1,0:T(2,128)}, f32[1,8]{1,0:T(1,128)}) custom-call(s32[32]{0:T(128)} %slots_ref.1, f32[32,16]{1,0:T(8,128)} %bitcast.27, f32[32,16]{1,0:T(8,128)} %bitcast.28, f32[896,128]{1,0:T(8,128)} %bitcast.23, f32[896,128]{1,0:T(8,128)} %copy-done.1), custom_call_target="tpu_custom_call" | custom-call | tf_op jit(solution)/shard_map/macro/pallas_call | solution.py:592
  51.8 1.5 %reshape.42 = f32[3,2,32,32]{3,2,1,0:T(8,128)} reshape(f32[3,2,1024]{2,1,0:T(2,128)} %get-tuple-element.8) | data formatting | bytes 49152 | tf_op jit(solution)/shard_map/reshape | solution.py:609
  53.3 1.8 %all-to-all-done.2 = bf16[8,1,24,1024]{3,2,1,0:T(8,128)(2,1)S(1)} async-done(((bf16[8,1,24,1024]{3,2,1,0:T(8,128)(2,1)}), bf16[8,1,24,1024]{3,2,1,0:T(8,128)(2,1)S(1)}, u32[]{:S(2)}, u32[]{:S(2)}) %all-to-all-start.2) | async-done | bytes 393248 | tf_op jit(solution)/shard_map/all_to_all | solution.py:587
  55.1 0.2 reshape.43
  55.3 1.1 %bitcast_add_fusion = f32[6,8,4,1024]{3,2,1,0:T(4,128)} fusion(f32[8,6,4,1024]{3,2,1,0:T(4,128)S(1)} %reshape.43, f32[6,8]{1,0:T(8,128)S(1)} %copy.18), kind=kLoop, calls=%fused_computation | loop fusion | flops 196608 | bytes 1573056 | tf_op jit(solution)/shard_map/add | solution.py:591
  (1 shorter events, 0.0 us)
Async XLA Ops:
  23.1 19.6 %copy-start = (f32[8,112,128]{2,1,0:T(8,128)S(1)}, f32[8,112,128]{2,1,0:T(8,128)}, u32[]{:S(2)}) copy-start(f32[8,112,128]{2,1,0:T(8,128)} %all_to_all.15) | copy-start | bytes 1376260
  39.1 5.4 %copy-start.2 = (f32[32,1,16]{2,1,0:T(1,128)}, f32[32,1,16]{2,1,0:T(1,128)S(1)}, u32[]{:S(2)}) copy-start(f32[32,1,16]{2,1,0:T(1,128)S(1)} %all_to_all.16) | copy-start | bytes 6148
  39.1 15.9 %all-to-all-start.2 = ((bf16[8,1,24,1024]{3,2,1,0:T(8,128)(2,1)}), bf16[8,1,24,1024]{3,2,1,0:T(8,128)(2,1)S(1)}, u32[]{:S(2)}, u32[]{:S(2)}) async-start(bf16[8,1,24,1024]{3,2,1,0:T(8,128)(2,1)} %bitcast.25), calls=%async_computation.2 | async-start | bytes 786432 | tf_op jit(solution)/shard_map/all_to_all | solution.py:587
  42.6 1.9 %collective-permute-start = (f32[896,128]{1,0:T(8,128)S(1)}, f32[896,128]{1,0:T(8,128)S(1)}, u32[]{:S(2)}, u32[]{:S(2)}) collective-permute-start(f32[896,128]{1,0:T(8,128)S(1)} %bitcast.24), channel_id=1, source_target_pairs={{0,1},{1,0},{2,3},{3,2},{4,5},{5,4},{6,7},{7,6},{8,9},{9,8},{10,11... | collective-permute-start | bytes 1376264 | tf_op jit(solution)/shard_map/ppermute | solution.py:550
  44.5 0.8 %copy-start.1 = (f32[896,128]{1,0:T(8,128)}, f32[896,128]{1,0:T(8,128)S(1)}, u32[]{:S(2)}) copy-start(f32[896,128]{1,0:T(8,128)S(1)} %collective-permute-done.other_ref) | copy-start | bytes 1376260

commit v4 on v3

--- a/solution.py
+++ b/solution.py
@@ -79,10 +79,9 @@
 
 
 def table_by(high, low, value):
-    rows = high.shape[0]
     value_high, value_low = split(value)
-    both = dot(jnp.concatenate([high, low], axis=0), value_high)
-    return both[:rows] + both[rows:] + dot(high, value_low)
+    deep = jnp.concatenate([high, low, high], axis=1)
+    return dot(deep, jnp.concatenate([value_high, value_high, value_low], axis=0))
 
 
 def forward_plane(value, table):
@@ -304,7 +303,7 @@
 
 def micro_kernel(
     local, local_count, layers, steps_hbm, packet_hbm, mult_hbm, fwd_hbm, bwd_hbm, table_hbm,
-    sent_hbm, response_ref, packet_ref, fields, moduli, mult_ref, fwd_ref, bwd_ref, table, spectrum, ordered, sent_ref, steps_ref, sem
+    sent_hbm, response_hbm, packet_ref, fields, moduli, mult_ref, fwd_ref, bwd_ref, table, spectrum, ordered, sent_ref, response_ref, steps_ref, sem
 ):
     devices, planes = sent_ref.shape[0], sent_ref.shape[1] // 6
     vox, columns = moduli.shape[1:]
@@ -429,7 +428,10 @@
     for index, part in enumerate(load):
         row = jnp.where(lane == 8 + index, part, row)
     response_ref[...] = jnp.broadcast_to(row, response_ref.shape)
+    answer = pltpu.make_async_copy(response_ref, response_hbm, sem.at[len(pairs) + 1])
+    answer.start()
     send.wait()
+    answer.wait()
 
 
 def vox_width(columns):
@@ -525,7 +527,9 @@
     layers = displacement.shape[1]
     width = displacement.shape[2] * displacement.shape[3]
     plane, forward_line, backward_line, multipliers = tables(vox)
-    params = pltpu.CompilerParams(vmem_limit_bytes=60 * 1024 * 1024)
+    pack_params, params, macro_params = (
+        pltpu.CompilerParams(vmem_limit_bytes=size * 1024 * 1024) for size in (60, 60, 16)
+    )
 
     side = displacement.shape[3]
     lines = layers * displacement.shape[2]
@@ -539,7 +543,7 @@
         in_specs=[vmem()] * 5,
         out_specs=vmem(),
         scratch_shapes=[pltpu.VMEM((7 * lines, LANES), f32)],
-        compiler_params=params,
+        compiler_params=pack_params,
     )(
         displacement.reshape(3 * lines, side), element_sample.reshape(lines, side),
         external_force.reshape(3 * lines, side),
@@ -560,7 +564,7 @@
                 jax.ShapeDtypeStruct((everyone, 16), f32),
             ),
             in_specs=[hbm()] * 6,
-            out_specs=(hbm(), vmem()),
+            out_specs=(hbm(), hbm()),
             scratch_shapes=[
                 pltpu.VMEM((devices * length, LANES), f32),
                 pltpu.VMEM((4, devices * layers, width), f32),
@@ -572,8 +576,9 @@
                 pltpu.VMEM((6 * vox, columns), f32),
                 pltpu.VMEM((devices, 6 * planes, columns), f32),
                 pltpu.VMEM((devices, 6 * planes, columns), bf16),
+                pltpu.VMEM((everyone, 16), f32),
                 pltpu.SMEM(plastic_steps.shape, jnp.int32),
-                pltpu.SemaphoreType.DMA((10,)),
+                pltpu.SemaphoreType.DMA((11,)),
             ],
             compiler_params=params,
         )(
@@ -604,7 +609,7 @@
             pltpu.VMEM((8, devices * layers, width), f32),
             pltpu.VMEM((3, devices * layers, width), f32),
         ],
-        compiler_params=params,
+        compiler_params=macro_params,
     )(owner_slot, gathered, gathered, packets, neighbour)
     return (following.reshape(displacement.shape), picked, micro_strain)
 

time: 56.9 us -> 56.3 us (0.989)
  waiting for transfers between devices: 3.09 us -> 5.57 us
  Pallas kernels: 14.1 us -> 12.5 us
  local copies, waits for them, and re-layouts: 2.66 us -> 1.17 us
    all_to_all x1, waiting for transfers between devices: 1.77 us -> 4.24 us  [shards(): lax.all_to_all(jnp.stack(sents, axis=1), 'dev', split_axis=0, concat_axis...]
    pallas_call x1, Pallas kernels: 6.56 us -> 5.58 us  [shards(): pl.pallas_call(functools.partial(macro_kernel, layers, base), name='macro...]
    unnamed x6 -> x4, local copies, waits for them, and re-layouts: 0.77 us -> 0.01 us
    reshape x1, local copies, waits for them, and re-layouts: 1.48 us -> 0.75 us  [shards(): return (following.reshape(displacement.shape), picked, micro_strain)]
    pallas_call x1, Pallas kernels: 5.51 us -> 4.9 us  [shards(): pl.pallas_call(functools.partial(micro_kernel, local, local_count, layers...]
  transfers between devices with their start and end apart: 2 -> 2, of which waited for: 2 -> 2; matrix products, arithmetic and copies ran while one was open for 3% -> 2% of each run, Pallas kernels for 12% -> 10%
where the time goes in v4:
time: 56.3 us; the launch traced here: 56 us
  blocking collectives  31.1 us (55%)
  Pallas kernels  12.5 us (22%)
  waiting for transfers between devices  5.57 us (10%)
  starting transfers between devices  3.85 us (7%)
  local copies, waits for them, and re-layouts  1.17 us (2%)
  other arithmetic  1.08 us (2%)
  between operations  0.67 us (1%)
    all_to_all x1, blocking collectives, shards(): lax.all_to_all(packet, 'dev', split_axis=0, concat_axis=0, tiled=True)  20.4 us
    all_to_all x1, blocking collectives, shards(): lax.all_to_all(jnp.stack(rows, axis=1), ('grp', 'dev'), split_axis=0, con...  10.7 us
    pallas_call x1, Pallas kernels, shards(): pl.pallas_call(functools.partial(macro_kernel, layers, base), name='macro...  5.58 us
    pallas_call x1, Pallas kernels, shards(): pl.pallas_call(functools.partial(micro_kernel, local, local_count, layers...  4.9 us
    all_to_all x1, waiting for transfers between devices, shards(): lax.all_to_all(jnp.stack(sents, axis=1), 'dev', split_axis=0, concat_axis...  4.24 us
    all_to_all x1, starting transfers between devices, shards(): lax.all_to_all(jnp.stack(sents, axis=1), 'dev', split_axis=0, concat_axis...  3.45 us
    pallas_call x1, Pallas kernels, shards(): pl.pallas_call(functools.partial(pack_kernel, layers), name='pack', out_s...  2.04 us
    ppermute x1, waiting for transfers between devices, shards(): lax.ppermute(packets, 'dev', [(i, i ^ 1) for i in range(devices)])  1.32 us
  transfers between devices with their start and end apart: 2, of which 2 were waited for; matrix products, arithmetic and copies ran while one was open for 2% of the time, Pallas kernels for 10%

profile of v4, /device:TPU:0, one launch (start us, length us, event | category | flops | bytes accessed | tf_op | source)
XLA Modules:
  0.0 56.0 jit_solution(672289145878461296)
XLA Ops:
  0.6 2.0 %pack.1 = f32[8,112,128]{2,1,0:T(8,128)} custom-call(f32[192,32]{1,0:T(8,128)} %bitcast.29, s32[64,32]{1,0:T(8,128)} %bitcast.33, f32[192,32]{1,0:T(8,128)} %bitcast.30, bf16[8,1,4,1024]{3,2,1,0:T(4,128)(2,1)} %bitcast.31, bf16[8,1,4,1024]{3,2,1,0:T(4,128)(2,1)} %bitcast.32), custom_call_target="tpu_custom_call" | custom-call | tf_op jit(solution)/shard_map/pack/pallas_call | solution.py:539
  2.7 20.4 %all_to_all.15 = f32[8,112,128]{2,1,0:T(8,128)} all-to-all(f32[8,112,128]{2,1,0:T(8,128)} %pack.1), channel_id=1, replica_groups=mesh['grp'=4,'dev'=8] {'dev'}, dimensions={0} | all-to-all | bytes 917504 | tf_op jit(solution)/shard_map/all_to_all | solution.py:553
  23.1 0.0 copy-start
  23.1 0.0 copy-start.1
  23.1 4.9 %micro.1 = (bf16[8,24,1024]{2,1,0:T(8,128)(2,1)}, f32[32,16]{1,0:T(8,128)}) custom-call(s32[32]{0:T(128)} %steps_hbm.1, f32[896,128]{1,0:T(8,128)} %bitcast.22, f32[8,16,256]{2,1,0:T(8,128)} %constant.20.clone.mult_hbm, bf16[2,64,64]{2,1,0:T(8,128)(2,1)} %constant.21.clone.fwd_hbm, bf16[2,192,192]{2,1,0:T(8,128)(2,1)} %constant.22.clone.bwd_hbm, ...), custom_call_target="tpu_custom_call" | custom-call | tf_op jit(solution)/shard_map/micro/pallas_call | solution.py:559
  28.0 10.7 %all_to_all.16 = f32[32,1,16]{2,1,0:T(1,128)S(1)} all-to-all(f32[32,1,16]{2,1,0:T(1,128)} %bitcast.34), channel_id=1, replica_groups=mesh['grp'=4,'dev'=8] {'grp','dev'}, dimensions={0} | all-to-all | bytes 4096 | tf_op jit(solution)/shard_map/all_to_all | solution.py:589
  38.7 3.5 %all-to-all-start.2 = ((bf16[8,1,24,1024]{3,2,1,0:T(8,128)(2,1)}), bf16[8,1,24,1024]{3,2,1,0:T(8,128)(2,1)S(1)}, u32[]{:S(2)}, u32[]{:S(2)}) async-start(bf16[8,1,24,1024]{3,2,1,0:T(8,128)(2,1)} %bitcast.28), calls=%async_computation.2 | async-start | bytes 786432 | tf_op jit(solution)/shard_map/all_to_all | solution.py:592
  42.1 0.0 copy-done
  42.2 0.4 collective-permute-start
  42.6 0.1 slice_bitcast_fusion
  42.6 0.1 copy.18
  42.7 1.3 %collective-permute-done.other_ref = f32[896,128]{1,0:T(8,128)S(1)} collective-permute-done((f32[896,128]{1,0:T(8,128)S(1)}, f32[896,128]{1,0:T(8,128)S(1)}, u32[]{:S(2)}, u32[]{:S(2)}) %collective-permute-start) | collective-permute-done | bytes 458784 | tf_op jit(solution)/shard_map/ppermute | solution.py:554
  44.0 0.0 copy-done.1
  44.0 5.6 %macro.1 = (f32[3,2,1024]{2,1,0:T(2,128)S(1)}, f32[1,8]{1,0:T(1,128)}) custom-call(s32[32]{0:T(128)S(1)} %copy-done.1, f32[32,16]{1,0:T(8,128)S(1)} %bitcast.26, f32[32,16]{1,0:T(8,128)S(1)} %bitcast.27, f32[896,128]{1,0:T(8,128)S(1)} %bitcast.24, f32[896,128]{1,0:T(8,128)S(1)} %collective-permute-done.other_ref), custom_call_target="tpu_custom_call" | custom-call | tf_op jit(solution)/shard_map/macro/pallas_call | solution.py:597
  49.6 0.8 %reshape.42 = f32[3,2,32,32]{3,2,1,0:T(8,128)} reshape(f32[3,2,1024]{2,1,0:T(2,128)S(1)} %get-tuple-element.8) | data formatting | bytes 49152 | tf_op jit(solution)/shard_map/reshape | solution.py:614
  50.4 4.2 %all-to-all-done.2 = bf16[8,1,24,1024]{3,2,1,0:T(8,128)(2,1)S(1)} async-done(((bf16[8,1,24,1024]{3,2,1,0:T(8,128)(2,1)}), bf16[8,1,24,1024]{3,2,1,0:T(8,128)(2,1)S(1)}, u32[]{:S(2)}, u32[]{:S(2)}) %all-to-all-start.2) | async-done | bytes 393248 | tf_op jit(solution)/shard_map/all_to_all | solution.py:592
  54.6 0.2 reshape.43
  54.9 1.1 %bitcast_add_fusion = f32[6,8,4,1024]{3,2,1,0:T(4,128)} fusion(f32[8,6,4,1024]{3,2,1,0:T(4,128)S(1)} %reshape.43, f32[6,8]{1,0:T(8,128)S(1)} %copy.18), kind=kLoop, calls=%fused_computation | loop fusion | flops 196608 | bytes 1573056 | tf_op jit(solution)/shard_map/add | solution.py:596
  (1 shorter events, 0.0 us)
Async XLA Ops:
  23.1 19.1 %copy-start = (f32[8,112,128]{2,1,0:T(8,128)S(1)}, f32[8,112,128]{2,1,0:T(8,128)}, u32[]{:S(2)}) copy-start(f32[8,112,128]{2,1,0:T(8,128)} %all_to_all.15) | copy-start | bytes 1376260
  23.1 21.0 %copy-start.1 = (s32[32]{0:T(128)S(1)}, s32[32]{0:T(128)}, u32[]{:S(2)}) copy-start(s32[32]{0:T(128)} %slots_ref.1) | copy-start | bytes 388
  38.7 15.9 %all-to-all-start.2 = ((bf16[8,1,24,1024]{3,2,1,0:T(8,128)(2,1)}), bf16[8,1,24,1024]{3,2,1,0:T(8,128)(2,1)S(1)}, u32[]{:S(2)}, u32[]{:S(2)}) async-start(bf16[8,1,24,1024]{3,2,1,0:T(8,128)(2,1)} %bitcast.28), calls=%async_computation.2 | async-start | bytes 786432 | tf_op jit(solution)/shard_map/all_to_all | solution.py:592
  42.2 1.9 %collective-permute-start = (f32[896,128]{1,0:T(8,128)S(1)}, f32[896,128]{1,0:T(8,128)S(1)}, u32[]{:S(2)}, u32[]{:S(2)}) collective-permute-start(f32[896,128]{1,0:T(8,128)S(1)} %bitcast.23), channel_id=1, source_target_pairs={{0,1},{1,0},{2,3},{3,2},{4,5},{5,4},{6,7},{7,6},{8,9},{9,8},{10,11... | collective-permute-start | bytes 1376264 | tf_op jit(solution)/shard_map/ppermute | solution.py:554

commit v5 on v4

--- a/solution.py
+++ b/solution.py
@@ -107,6 +107,42 @@
     return lax.broadcasted_iota(jnp.int32, shape, 0)
 
 
+def plane_slopes(stencil, v):
+    next_z = stencil.up_z(v)
+    sum_z = v + next_z
+    dif_z = next_z - v
+    next_y = stencil.up_y(sum_z)
+    return sum_z + next_y, next_y - sum_z, dif_z + stencil.up_y(dif_z)
+
+
+def strain_from(slopes):
+    return [
+        0.25 * slopes[0][0],
+        0.25 * slopes[1][1],
+        0.25 * slopes[2][2],
+        0.125 * (slopes[2][1] + slopes[1][2]),
+        0.125 * (slopes[2][0] + slopes[0][2]),
+        0.125 * (slopes[1][0] + slopes[0][1]),
+    ]
+
+
+class TileStencil:
+    def __init__(self, shape, width):
+        self.rows, self.width = shape[0], width
+        lane = lane_position(shape)
+        self.last_z = lane % width == width - 1
+        self.inside = lane < LANES - width
+        self.last_y = (lane >= LANES - width) & (row_position(shape) == self.rows - 1)
+
+    def up_z(self, v):
+        return jnp.where(self.last_z, 0.0, pltpu.roll(v, LANES - 1, 1))
+
+    def up_y(self, v):
+        turned = pltpu.roll(v, LANES - self.width, 1)
+        following = pltpu.roll(turned, self.rows - 1, 0)
+        return jnp.where(self.last_y, 0.0, jnp.where(self.inside, turned, following))
+
+
 class Stencil:
     def __init__(self, shape, width, devices):
         self.rows, self.columns = shape
@@ -129,7 +165,7 @@
 
     def up_x(self, v):
         wrapped = jnp.where(self.last_x, 0.0, pltpu.roll(v[: self.devices], self.devices - 1, 0))
-        return jnp.concatenate([v[self.devices :], wrapped], axis=0)
+        return wrapped if self.rows == self.devices else jnp.concatenate([v[self.devices :], wrapped], axis=0)
 
     def down_z(self, v):
         return jnp.where(self.first_z, 0.0, pltpu.roll(v, 1, 1))
@@ -139,27 +175,14 @@
 
     def down_x(self, v):
         wrapped = jnp.where(self.first_x, 0.0, pltpu.roll(v[self.rows - self.devices :], 1, 0))
-        return jnp.concatenate([wrapped, v[: self.rows - self.devices]], axis=0)
+        return wrapped if self.rows == self.devices else jnp.concatenate([wrapped, v[: self.rows - self.devices]], axis=0)
 
     def strain(self, field):
         slopes = []
         for v in field:
-            next_z = self.up_z(v)
-            sum_z = v + next_z
-            dif_z = next_z - v
-            next_y = self.up_y(sum_z)
-            sums = sum_z + next_y
-            along_y = next_y - sum_z
-            along_z = dif_z + self.up_y(dif_z)
+            sums, along_y, along_z = plane_slopes(self, v)
             slopes.append((self.up_x(sums) - sums, along_y + self.up_x(along_y), along_z + self.up_x(along_z)))
-        return [
-            0.25 * slopes[0][0],
-            0.25 * slopes[1][1],
-            0.25 * slopes[2][2],
-            0.125 * (slopes[2][1] + slopes[1][2]),
-            0.125 * (slopes[2][0] + slopes[0][2]),
-            0.125 * (slopes[1][0] + slopes[0][1]),
-        ]
+        return strain_from(slopes)
 
     def force(self, stress):
         result = []
@@ -210,6 +233,7 @@
 CODE_BASE = 2.0**11
 LABEL_BASE = 2.0**12
 LANES = 128
+SUM_ROWS = 8
 
 
 def encode(lame, shear):
@@ -245,41 +269,62 @@
         merged = jnp.where(slot == place, wide[pl.ds(place, count, stride=beside), :], merged)
     nodes = 3 * count // 7
     each = nodes // (3 * layers)
-    base = local_count * planes * tiles
-    spare = base + nodes + (layers + 1) // 2 * each
-    for device in range(devices):
-        packet_ref[device, base : base + nodes, :] = merged[:nodes]
-    for pair in range((layers + 1) // 2):
-        at = nodes + 2 * pair * each
-        label = merged[at : at + each] * LABEL_BASE
-        if 2 * pair + 1 < layers:
-            label = label + merged[at + each : at + 2 * each]
+    labels = [merged[nodes + layer * each : nodes + (layer + 1) * each] for layer in range(layers)]
+    at = local_count * planes * tiles
+    for part in range(3):
         for device in range(devices):
-            packet_ref[device, base + nodes + pair * each : base + nodes + (pair + 1) * each, :] = label
+            packet_ref[device, at : at + each, :] = merged[part * layers * each : (part * layers + 1) * each]
+        at += each
+    for first in range(0, layers, 2):
+        pair = labels[first] * LABEL_BASE
+        if first + 1 < layers:
+            pair = pair + labels[first + 1]
+        for device in range(devices):
+            packet_ref[device, at : at + each, :] = pair
+        at += each
+    pull = merged[count - nodes :] - spring_rate * merged[:nodes]
     part = force_rows(layers) * each
     for device in range(devices):
-        start = count - nodes if device % 2 == 0 else count - part
-        packet_ref[device, spare : spare + part, :] = merged[start : start + part]
+        packet_ref[device, at : at + part, :] = pull[:part] if device % 2 == 0 else pull[nodes - part :]
+    at += part
+    stencil = TileStencil((each, LANES), width)
+    slopes = [
+        [plane_slopes(stencil, merged[(c * layers + layer) * each : (c * layers + layer + 1) * each]) for c in range(3)]
+        for layer in range(layers)
+    ]
+    strains = []
+    for layer in range(layers):
+        below = [(-sums, along_y, along_z) for sums, along_y, along_z in slopes[layer]]
+        if layer + 1 < layers:
+            below = [tuple(low + high for low, high in zip(*both)) for both in zip(below, slopes[layer + 1])]
+        strains.append(strain_from(below) + [jnp.ones((each, LANES), f32)])
+    start = lax.axis_index("grp") * (devices * local_count)
+    for device in range(devices):
+        for local in range(local_count):
+            own = (start + device * local_count + local).astype(f32)
+            hits = [label == own for label in labels]
+            for c in range(7):
+                value = sum(jnp.where(hit, strain[c], 0.0) for hit, strain in zip(hits, strains))
+                row = at + local * SUM_ROWS + c
+                packet_ref[device, row : row + 1, :] = jnp.sum(value, axis=0, keepdims=True)
+            packet_ref[device, at + local * SUM_ROWS + 7 : at + (local + 1) * SUM_ROWS, :] = jnp.zeros((1, LANES), f32)
 
 
 def force_rows(layers):
     return (3 * layers + 1) // 2
 
 
-def read_fields(packet_ref, base, layers, fields):
-    _, rows, columns = fields.shape
-    devices = rows // layers
-    tiles = columns // LANES
+def read_plane(packet_ref, row, devices, tiles):
     step = packet_ref.shape[0] // devices
-    for part in range(4):
-        for layer in range(layers):
-            for tile in range(tiles):
-                row = part * layers + (layer if part < 3 else layer // 2)
-                piece = packet_ref[pl.ds(base + row * tiles + tile, devices, stride=step), :]
-                if part == 3:
-                    high = jnp.floor(piece * (1.0 / LABEL_BASE))
-                    piece = high if layer % 2 == 0 else piece - high * LABEL_BASE
-                fields[part, layer * devices : (layer + 1) * devices, tile * LANES : (tile + 1) * LANES] = piece
+    return jnp.concatenate(
+        [packet_ref[pl.ds(row + tile, devices, stride=step), :] for tile in range(tiles)], axis=1
+    )
+
+
+def read_label(packet_ref, base, layer, devices, tiles):
+    both = read_plane(packet_ref, base + (3 + layer // 2) * tiles, devices, tiles)
+    high = jnp.floor(both * (1.0 / LABEL_BASE))
+    return high if layer % 2 == 0 else both - high * LABEL_BASE
 
 
 def read_force(packet_ref, other_ref, base, layers, forces, even):
@@ -287,7 +332,7 @@
     devices = rows // layers
     tiles = columns // LANES
     step = packet_ref.shape[0] // devices
-    start = base + (3 * layers + (layers + 1) // 2) * tiles
+    start = base + (3 + (layers + 1) // 2) * tiles
     held = force_rows(layers)
     for part in range(3):
         for layer in range(layers):
@@ -303,13 +348,12 @@
 
 def micro_kernel(
     local, local_count, layers, steps_hbm, packet_hbm, mult_hbm, fwd_hbm, bwd_hbm, table_hbm,
-    sent_hbm, response_hbm, packet_ref, fields, moduli, mult_ref, fwd_ref, bwd_ref, table, spectrum, ordered, sent_ref, response_ref, steps_ref, sem
+    sent_hbm, response_hbm, packet_ref, moduli, mult_ref, fwd_ref, bwd_ref, table, spectrum, ordered, sent_ref, response_ref, steps_ref, sem
 ):
     devices, planes = sent_ref.shape[0], sent_ref.shape[1] // 6
     vox, columns = moduli.shape[1:]
     half = vox // 2
     quarter = half * half
-    width = vox_width(fields.shape[2])
     pairs = [(packet_hbm, packet_ref), (steps_hbm, steps_ref)]
     pairs += [(table_hbm.at[part, fold], table.at[part, fold]) for fold in range(2) for part in range(2)]
     pairs += [(fwd_hbm, fwd_ref), (mult_hbm, mult_ref), (bwd_hbm, bwd_ref)]
@@ -322,7 +366,6 @@
     copies[0].wait()
     tiles = columns // LANES
     step = packet_ref.shape[0] // devices
-    read_fields(packet_ref, local_count * planes * tiles, layers, fields)
     for device in range(devices):
         for tile in range(tiles):
             at = device * step + local * planes * tiles + tile
@@ -331,11 +374,22 @@
                 moduli[
                     kind, device * planes : (device + 1) * planes, tile * LANES : (tile + 1) * LANES
                 ] = value
-    stencil = Stencil(fields.shape[1:], width, fields.shape[1] // layers)
-    mesh_strain = stencil.strain([fields[c] for c in range(3)])
-    mine = fields[3] == own.astype(f32)
-    count = total(jnp.where(mine, 1.0, 0.0))
-    load = [total(jnp.where(mine, part, 0.0)) / count for part in mesh_strain]
+    base = local_count * planes * tiles
+    stencil = Stencil((devices, columns), vox_width(columns), devices)
+    following = []
+    for c in range(3):
+        plane = read_plane(packet_ref, base + c * tiles, devices, tiles)
+        following.append(plane_slopes(stencil, stencil.up_x(plane)))
+    mine = read_label(packet_ref, base, layers - 1, devices, tiles) == own.astype(f32)
+    sums = 0.0
+    for device in range(devices):
+        at = (device + 1) * step - (local_count - local) * SUM_ROWS
+        sums = sums + packet_ref[at : at + SUM_ROWS, :]
+    sums = jnp.sum(sums, axis=1, keepdims=True)
+    load = [
+        (sums[c : c + 1] + total(jnp.where(mine, part, 0.0))) / sums[6:7]
+        for c, part in enumerate(strain_from(following))
+    ]
     trace, dev = deviator_of(load)
     lame = moduli[0]
     shear = moduli[1]
@@ -440,10 +494,10 @@
 
 
 def macro_kernel(
-    layers, base, slots_ref, table_ref, table_v_ref, packet_ref, other_ref, next_ref, row_ref, fields, forces, cells, result
+    layers, base, slots_ref, table_ref, table_v_ref, packet_ref, other_ref, next_ref, row_ref, labels, forces, cells, result
 ):
     columns = next_ref.shape[2]
-    devices = fields.shape[1] // layers
+    devices = labels.shape[0] // layers
     samples = table_v_ref.shape[0]
     rank = lax.axis_index("dev")
     group = lax.axis_index("grp")
@@ -455,15 +509,18 @@
         for j in range(group_size):
             chosen = jnp.where(slots_ref[start + j] == rank * local_count + local, start + j, chosen)
         row_ref[local : local + 1, :] = table_v_ref[pl.ds(chosen, 1), 0:8]
-    read_fields(packet_ref, base, layers, fields)
+    for layer in range(layers):
+        labels[layer * devices : (layer + 1) * devices, :] = read_label(
+            packet_ref, base, layer, devices, columns // LANES
+        )
     read_force(packet_ref, other_ref, base, layers, forces, rank % 2 == 0)
-    rows = fields.shape[1]
+    rows = labels.shape[0]
     height = min(8, rows)
     span = min(512, columns)
     for top in range(0, rows, height):
         for side in range(0, columns, span):
             where = (slice(top, top + height), slice(side, side + span))
-            label = fields[(3,) + where]
+            label = labels[where]
 
             def pick(sample, held):
                 here = label == sample.astype(f32)
@@ -473,10 +530,10 @@
             held = lax.fori_loop(0, samples, pick, (zero,) * 8, unroll=4)
             for c in range(8):
                 cells[(c,) + where] = held[c]
-    stencil = Stencil(fields.shape[1:], vox_width(columns), devices)
+    stencil = Stencil(labels.shape, vox_width(columns), devices)
     stress = [cells[c] for c in range(6)]
     pulled = stencil.force(stress)
-    remainder = [forces[b] - pulled[b] - spring_rate * fields[b] for b in range(3)]
+    remainder = [forces[b] - pulled[b] for b in range(3)]
     direction = remainder
     norm_now = total(sum(r * r for r in remainder))
     update = None
@@ -498,8 +555,7 @@
             direction = [remainder[b] + grow * direction[b] for b in range(3)]
             norm_now = norm_next
     for b in range(3):
-        done = fields[b] + update[b]
-        result[b] = done
+        result[b] = update[b]
         for layer in range(layers):
             next_ref[b, layer : layer + 1, :] = result[b, pl.ds(layer * devices + rank, 1), :]
 
@@ -535,7 +591,7 @@
     lines = layers * displacement.shape[2]
     tiles = columns // LANES
     base = local_count * planes * tiles
-    length = base + (3 * layers + (layers + 1) // 2 + force_rows(layers)) * tiles
+    length = base + (3 + (layers + 1) // 2 + force_rows(layers)) * tiles + local_count * SUM_ROWS
     packet = pl.pallas_call(
         functools.partial(pack_kernel, layers),
         name="pack",
@@ -567,7 +623,6 @@
             out_specs=(hbm(), hbm()),
             scratch_shapes=[
                 pltpu.VMEM((devices * length, LANES), f32),
-                pltpu.VMEM((4, devices * layers, width), f32),
                 pltpu.VMEM((2, vox, columns), f32),
                 pltpu.VMEM(multipliers.shape, f32),
                 pltpu.VMEM(forward_line.shape, bf16),
@@ -604,14 +659,14 @@
         in_specs=[smem(), smem()] + [vmem()] * 3,
         out_specs=(vmem(), vmem()),
         scratch_shapes=[
-            pltpu.VMEM((4, devices * layers, width), f32),
+            pltpu.VMEM((devices * layers, width), f32),
             pltpu.VMEM((3, devices * layers, width), f32),
             pltpu.VMEM((8, devices * layers, width), f32),
             pltpu.VMEM((3, devices * layers, width), f32),
         ],
         compiler_params=macro_params,
     )(owner_slot, gathered, gathered, packets, neighbour)
-    return (following.reshape(displacement.shape), picked, micro_strain)
+    return (displacement + following.reshape(displacement.shape), picked, micro_strain)
 
 
 def solution(mesh):

time: 56.3 us -> 55.1 us (0.979)
  blocking collectives: 31.1 us -> 29.7 us
  other arithmetic: 1.08 us -> 1.74 us
  local copies, waits for them, and re-layouts: 1.17 us -> 0.53 us
    all_to_all x1, blocking collectives: 20.4 us -> 19.1 us  [shards(): lax.all_to_all(packet, 'dev', split_axis=0, concat_axis=0, tiled=True)]
    add x0 -> x1, other arithmetic: none -> 0.66 us  [shards(): displacement + following.reshape(displacement.shape)]
    reshape x1, local copies, waits for them, and re-layouts: 0.75 us -> 0.1 us  [shards(): following.reshape(displacement.shape)]
where the time goes in v5:
time: 55.1 us; the launch traced here: 54.7 us
  blocking collectives  29.7 us (54%)
  Pallas kernels  12.8 us (23%)
  waiting for transfers between devices  5.44 us (10%)
  starting transfers between devices  3.85 us (7%)
  other arithmetic  1.74 us (3%)
  between operations  0.69 us (1%)
    all_to_all x1, blocking collectives, shards(): lax.all_to_all(packet, 'dev', split_axis=0, concat_axis=0, tiled=True)  19.1 us
    all_to_all x1, blocking collectives, shards(): lax.all_to_all(jnp.stack(rows, axis=1), ('grp', 'dev'), split_axis=0, con...  10.5 us
    pallas_call x1, Pallas kernels, shards(): pl.pallas_call(functools.partial(macro_kernel, layers, base), name='macro...  5.67 us
    pallas_call x1, Pallas kernels, shards(): pl.pallas_call(functools.partial(micro_kernel, local, local_count, layers...  4.95 us
    all_to_all x1, waiting for transfers between devices, shards(): lax.all_to_all(jnp.stack(sents, axis=1), 'dev', split_axis=0, concat_axis...  4.21 us
    all_to_all x1, starting transfers between devices, shards(): lax.all_to_all(jnp.stack(sents, axis=1), 'dev', split_axis=0, concat_axis...  3.45 us
    pallas_call x1, Pallas kernels, shards(): pl.pallas_call(functools.partial(pack_kernel, layers), name='pack', out_s...  2.17 us
    ppermute x1, waiting for transfers between devices, shards(): lax.ppermute(packets, 'dev', [(i, i ^ 1) for i in range(devices)])  1.23 us
  transfers between devices with their start and end apart: 2, of which 2 were waited for; matrix products, arithmetic and copies ran while one was open for 2% of the time, Pallas kernels for 10%

profile of v5, /device:TPU:0, one launch (start us, length us, event | category | flops | bytes accessed | tf_op | source)
XLA Modules:
  0.0 54.7 jit_solution(4567142344316396009)
XLA Ops:
  0.6 2.2 %pack.1 = f32[8,96,128]{2,1,0:T(8,128)} custom-call(f32[192,32]{1,0:T(8,128)} %bitcast.29, s32[64,32]{1,0:T(8,128)} %bitcast.33, f32[192,32]{1,0:T(8,128)} %bitcast.30, bf16[8,1,4,1024]{3,2,1,0:T(4,128)(2,1)} %bitcast.31, bf16[8,1,4,1024]{3,2,1,0:T(4,128)(2,1)} %bitcast.32), custom_call_target="tpu_custom_call" | custom-call | tf_op jit(solution)/shard_map/pack/pallas_call | solution.py:595
  2.8 0.0 copy-start.1
  2.8 19.1 %all_to_all.15 = f32[8,96,128]{2,1,0:T(8,128)} all-to-all(f32[8,96,128]{2,1,0:T(8,128)} %pack.1), channel_id=1, replica_groups=mesh['grp'=4,'dev'=8] {'dev'}, dimensions={0} | all-to-all | bytes 786432 | tf_op jit(solution)/shard_map/all_to_all | solution.py:609
  21.9 0.0 copy-start
  21.9 0.0 copy-start.2
  21.9 5.0 %micro.1 = (bf16[8,24,1024]{2,1,0:T(8,128)(2,1)}, f32[32,16]{1,0:T(8,128)}) custom-call(s32[32]{0:T(128)} %steps_hbm.1, f32[768,128]{1,0:T(8,128)} %bitcast.22, f32[8,16,256]{2,1,0:T(8,128)} %constant.20.clone.mult_hbm, bf16[2,64,64]{2,1,0:T(8,128)(2,1)} %constant.21.clone.fwd_hbm, bf16[2,192,192]{2,1,0:T(8,128)(2,1)} %constant.22.clone.bwd_hbm, ...), custom_call_target="tpu_custom_call" | custom-call | tf_op jit(solution)/shard_map/micro/pallas_call | solution.py:615
  26.9 10.5 %all_to_all.16 = f32[32,1,16]{2,1,0:T(1,128)S(1)} all-to-all(f32[32,1,16]{2,1,0:T(1,128)} %bitcast.34), channel_id=1, replica_groups=mesh['grp'=4,'dev'=8] {'grp','dev'}, dimensions={0} | all-to-all | bytes 4096 | tf_op jit(solution)/shard_map/all_to_all | solution.py:644
  37.4 3.5 %all-to-all-start.2 = ((bf16[8,1,24,1024]{3,2,1,0:T(8,128)(2,1)}), bf16[8,1,24,1024]{3,2,1,0:T(8,128)(2,1)S(1)}, u32[]{:S(2)}, u32[]{:S(2)}) async-start(bf16[8,1,24,1024]{3,2,1,0:T(8,128)(2,1)} %bitcast.28), calls=%async_computation.2 | async-start | bytes 786432 | tf_op jit(solution)/shard_map/all_to_all | solution.py:647
  40.9 0.0 copy-done
  40.9 0.4 collective-permute-start
  41.3 0.1 slice_bitcast_fusion
  41.4 0.1 copy.18
  41.5 1.2 %collective-permute-done.other_ref = f32[768,128]{1,0:T(8,128)S(1)} collective-permute-done((f32[768,128]{1,0:T(8,128)S(1)}, f32[768,128]{1,0:T(8,128)S(1)}, u32[]{:S(2)}, u32[]{:S(2)}) %collective-permute-start) | collective-permute-done | bytes 393248 | tf_op jit(solution)/shard_map/ppermute | solution.py:610
  42.7 0.0 copy-done.1
  42.7 5.7 %macro.1 = (f32[3,2,1024]{2,1,0:T(2,128)S(1)}, f32[1,8]{1,0:T(1,128)}) custom-call(s32[32]{0:T(128)S(1)} %copy-done.1, f32[32,16]{1,0:T(8,128)S(1)} %bitcast.26, f32[32,16]{1,0:T(8,128)S(1)} %bitcast.27, f32[768,128]{1,0:T(8,128)S(1)} %bitcast.24, f32[768,128]{1,0:T(8,128)S(1)} %collective-permute-done.other_ref), custom_call_target="tpu_custom_call" | custom-call | tf_op jit(solution)/shard_map/macro/pallas_call | solution.py:652
  48.4 0.1 reshape.42
  48.5 0.0 copy-done.2
  48.5 0.7 %add.14 = f32[3,2,32,32]{3,2,1,0:T(8,128)} add(f32[3,2,32,32]{3,2,1,0:T(8,128)S(1)} %copy-done.2, f32[3,2,32,32]{3,2,1,0:T(8,128)S(1)} %reshape.42) | non-fusion elementwise | flops 6144 | bytes 73728 | tf_op jit(solution)/shard_map/add | solution.py:669
  49.1 4.2 %all-to-all-done.2 = bf16[8,1,24,1024]{3,2,1,0:T(8,128)(2,1)S(1)} async-done(((bf16[8,1,24,1024]{3,2,1,0:T(8,128)(2,1)}), bf16[8,1,24,1024]{3,2,1,0:T(8,128)(2,1)S(1)}, u32[]{:S(2)}, u32[]{:S(2)}) %all-to-all-start.2) | async-done | bytes 393248 | tf_op jit(solution)/shard_map/all_to_all | solution.py:647
  53.4 0.2 reshape.43
  53.6 1.1 %bitcast_add_fusion = f32[6,8,4,1024]{3,2,1,0:T(4,128)} fusion(f32[8,6,4,1024]{3,2,1,0:T(4,128)S(1)} %reshape.43, f32[6,8]{1,0:T(8,128)S(1)} %copy.18), kind=kLoop, calls=%fused_computation | loop fusion | flops 196608 | bytes 1573056 | tf_op jit(solution)/shard_map/add | solution.py:651
  (1 shorter events, 0.0 us)
Async XLA Ops:
  2.8 39.9 %copy-start.1 = (s32[32]{0:T(128)S(1)}, s32[32]{0:T(128)}, u32[]{:S(2)}) copy-start(s32[32]{0:T(128)} %slots_ref.1) | copy-start | bytes 388
  21.9 19.0 %copy-start = (f32[8,96,128]{2,1,0:T(8,128)S(1)}, f32[8,96,128]{2,1,0:T(8,128)}, u32[]{:S(2)}) copy-start(f32[8,96,128]{2,1,0:T(8,128)} %all_to_all.15) | copy-start | bytes 1179652
  21.9 26.6 %copy-start.2 = (f32[3,2,32,32]{3,2,1,0:T(8,128)S(1)}, f32[3,2,32,32]{3,2,1,0:T(8,128)}, u32[]{:S(2)}) copy-start(f32[3,2,32,32]{3,2,1,0:T(8,128)} %param.11) | copy-start | bytes 73732
  37.4 15.9 %all-to-all-start.2 = ((bf16[8,1,24,1024]{3,2,1,0:T(8,128)(2,1)}), bf16[8,1,24,1024]{3,2,1,0:T(8,128)(2,1)S(1)}, u32[]{:S(2)}, u32[]{:S(2)}) async-start(bf16[8,1,24,1024]{3,2,1,0:T(8,128)(2,1)} %bitcast.28), calls=%async_computation.2 | async-start | bytes 786432 | tf_op jit(solution)/shard_map/all_to_all | solution.py:647
  40.9 1.8 %collective-permute-start = (f32[768,128]{1,0:T(8,128)S(1)}, f32[768,128]{1,0:T(8,128)S(1)}, u32[]{:S(2)}, u32[]{:S(2)}) collective-permute-start(f32[768,128]{1,0:T(8,128)S(1)} %bitcast.23), channel_id=1, source_target_pairs={{0,1},{1,0},{2,3},{3,2},{4,5},{5,4},{6,7},{7,6},{8,9},{9,8},{10,11... | collective-permute-start | bytes 1179656 | tf_op jit(solution)/shard_map/ppermute | solution.py:610

commit v6 on v5

--- a/solution.py
+++ b/solution.py
@@ -233,7 +233,7 @@
 CODE_BASE = 2.0**11
 LABEL_BASE = 2.0**12
 LANES = 128
-SUM_ROWS = 8
+SUM_ROWS = 4
 
 
 def encode(lame, shear):
@@ -283,9 +283,12 @@
             packet_ref[device, at : at + each, :] = pair
         at += each
     pull = merged[count - nodes :] - spring_rate * merged[:nodes]
-    part = force_rows(layers) * each
-    for device in range(devices):
-        packet_ref[device, at : at + part, :] = pull[:part] if device % 2 == 0 else pull[nodes - part :]
+    part = nodes // 4
+    upper = lax.axis_index("grp") % 2 == 1
+    for core in range(2):
+        quarter = jnp.where(upper, pull[(2 + core) * part : (3 + core) * part], pull[core * part : (core + 1) * part])
+        for device in range(core, devices, 2):
+            packet_ref[device, at : at + part, :] = quarter
     at += part
     stencil = TileStencil((each, LANES), width)
     slopes = [
@@ -299,19 +302,20 @@
             below = [tuple(low + high for low, high in zip(*both)) for both in zip(below, slopes[layer + 1])]
         strains.append(strain_from(below) + [jnp.ones((each, LANES), f32)])
     start = lax.axis_index("grp") * (devices * local_count)
+    left = lane_position((1, LANES)) < LANES // 2
     for device in range(devices):
         for local in range(local_count):
             own = (start + device * local_count + local).astype(f32)
             hits = [label == own for label in labels]
+            sums = []
             for c in range(7):
                 value = sum(jnp.where(hit, strain[c], 0.0) for hit, strain in zip(hits, strains))
+                value = jnp.sum(value, axis=0, keepdims=True)
+                sums.append(value + pltpu.roll(value, LANES // 2, 1))
+            sums.append(jnp.zeros((1, LANES), f32))
+            for c in range(SUM_ROWS):
                 row = at + local * SUM_ROWS + c
-                packet_ref[device, row : row + 1, :] = jnp.sum(value, axis=0, keepdims=True)
-            packet_ref[device, at + local * SUM_ROWS + 7 : at + (local + 1) * SUM_ROWS, :] = jnp.zeros((1, LANES), f32)
-
-
-def force_rows(layers):
-    return (3 * layers + 1) // 2
+                packet_ref[device, row : row + 1, :] = jnp.where(left, sums[c], sums[c + SUM_ROWS])
 
 
 def read_plane(packet_ref, row, devices, tiles):
@@ -327,23 +331,24 @@
     return high if layer % 2 == 0 else both - high * LABEL_BASE
 
 
-def read_force(packet_ref, other_ref, base, layers, forces, even):
+def read_force(tail_refs, layers, forces):
     _, rows, columns = forces.shape
     devices = rows // layers
     tiles = columns // LANES
-    step = packet_ref.shape[0] // devices
-    start = base + (3 + (layers + 1) // 2) * tiles
-    held = force_rows(layers)
-    for part in range(3):
-        for layer in range(layers):
-            row = part * layers + layer
-            first = row < held
-            local = row if first else row - (3 * layers - held)
-            for tile in range(tiles):
-                at = pl.ds(start + local * tiles + tile, devices, stride=step)
-                mine, other = packet_ref[at, :], other_ref[at, :]
-                piece = jnp.where(even, mine, other) if first else jnp.where(even, other, mine)
-                forces[part, layer * devices : (layer + 1) * devices, tile * LANES : (tile + 1) * LANES] = piece
+    step = tail_refs[0].shape[0] // devices
+    part = 3 * layers * tiles // 4
+    odd_core = lax.axis_index("dev") % 2
+    odd_group = lax.axis_index("grp") % 2
+    for row in range(3 * layers):
+        for tile in range(tiles):
+            quarter, at = divmod(row * tiles + tile, part)
+            own, core, side, across = (ref[pl.ds(at, devices, stride=step), :] for ref in tail_refs)
+            same_core = odd_core == quarter % 2
+            here, there = jnp.where(same_core, own, core), jnp.where(same_core, side, across)
+            c, layer = divmod(row, layers)
+            forces[c, layer * devices : (layer + 1) * devices, tile * LANES : (tile + 1) * LANES] = jnp.where(
+                odd_group == quarter // 2, here, there
+            )
 
 
 def micro_kernel(
@@ -385,10 +390,11 @@
     for device in range(devices):
         at = (device + 1) * step - (local_count - local) * SUM_ROWS
         sums = sums + packet_ref[at : at + SUM_ROWS, :]
-    sums = jnp.sum(sums, axis=1, keepdims=True)
+    left_half = lane_position(sums.shape) < LANES // 2
+    sums = [jnp.sum(jnp.where(left_half == side, sums, 0.0), axis=1, keepdims=True) for side in (True, False)]
+    sums = [half_sums[row : row + 1] for half_sums in sums for row in range(SUM_ROWS)]
     load = [
-        (sums[c : c + 1] + total(jnp.where(mine, part, 0.0))) / sums[6:7]
-        for c, part in enumerate(strain_from(following))
+        (sums[c] + total(jnp.where(mine, part, 0.0))) / sums[6] for c, part in enumerate(strain_from(following))
     ]
     trace, dev = deviator_of(load)
     lame = moduli[0]
@@ -494,7 +500,7 @@
 
 
 def macro_kernel(
-    layers, base, slots_ref, table_ref, table_v_ref, packet_ref, other_ref, next_ref, row_ref, labels, forces, cells, result
+    layers, base, slots_ref, table_ref, table_v_ref, packet_ref, own_ref, core_ref, side_ref, across_ref, next_ref, row_ref, labels, forces, cells, result
 ):
     columns = next_ref.shape[2]
     devices = labels.shape[0] // layers
@@ -513,7 +519,7 @@
         labels[layer * devices : (layer + 1) * devices, :] = read_label(
             packet_ref, base, layer, devices, columns // LANES
         )
-    read_force(packet_ref, other_ref, base, layers, forces, rank % 2 == 0)
+    read_force((own_ref, core_ref, side_ref, across_ref), layers, forces)
     rows = labels.shape[0]
     height = min(8, rows)
     span = min(512, columns)
@@ -591,7 +597,8 @@
     lines = layers * displacement.shape[2]
     tiles = columns // LANES
     base = local_count * planes * tiles
-    length = base + (3 + (layers + 1) // 2 + force_rows(layers)) * tiles + local_count * SUM_ROWS
+    tail = base + (3 + (layers + 1) // 2) * tiles
+    length = tail + 3 * layers * tiles // 4 + local_count * SUM_ROWS
     packet = pl.pallas_call(
         functools.partial(pack_kernel, layers),
         name="pack",
@@ -607,7 +614,11 @@
         shear_field.reshape(devices, local_count, planes, columns),
     )
     packets = lax.all_to_all(packet, "dev", split_axis=0, concat_axis=0, tiled=True).reshape(devices * length, LANES)
-    neighbour = lax.ppermute(packets, "dev", [(i, i ^ 1) for i in range(devices)])
+    own_tail = packets.reshape(devices, length, LANES)[:, tail:].reshape(-1, LANES)
+    tails = [own_tail, lax.ppermute(own_tail, "dev", [(i, i ^ 1) for i in range(devices)])]
+    tails.append(lax.ppermute(own_tail, "grp", [(i, i ^ 1) for i in range(groups)]))
+    flips = [(i, i ^ 1 ^ devices) for i in range(groups * devices)]
+    tails.append(lax.ppermute(own_tail, ("grp", "dev"), flips))
     everyone = groups * devices
     sents = []
     rows = []
@@ -656,7 +667,7 @@
             jax.ShapeDtypeStruct((3, layers, width), f32),
             jax.ShapeDtypeStruct((local_count, 8), f32),
         ),
-        in_specs=[smem(), smem()] + [vmem()] * 3,
+        in_specs=[smem(), smem()] + [vmem()] * 6,
         out_specs=(vmem(), vmem()),
         scratch_shapes=[
             pltpu.VMEM((devices * layers, width), f32),
@@ -665,7 +676,7 @@
             pltpu.VMEM((3, devices * layers, width), f32),
         ],
         compiler_params=macro_params,
-    )(owner_slot, gathered, gathered, packets, neighbour)
+    )(owner_slot, gathered, gathered, packets, *tails)
     return (displacement + following.reshape(displacement.shape), picked, micro_strain)
 
 

time: 55.1 us -> 53.7 us (0.975)
  starting transfers between devices: 3.85 us -> 5.54 us
  waiting for transfers between devices: 5.44 us -> 3.84 us
  blocking collectives: 29.7 us -> 28.3 us
    all_to_all x1, waiting for transfers between devices: 4.21 us -> 0.2 us  [shards(): lax.all_to_all(jnp.stack(sents, axis=1), 'dev', split_axis=0, concat_axis...]
    ppermute x1 -> x3, waiting for transfers between devices: 1.23 us -> 3.64 us  [the longest x1 1.88 us: shards(): lax.ppermute(own_tail, 'grp', [(i, i ^ 1) for i in range(groups)])]
    ppermute x1 -> x3, starting transfers between devices: 0.4 us -> 2.08 us  [the longest x1 1.44 us: shards(): lax.ppermute(own_tail, 'grp', [(i, i ^ 1) for i in range(groups)])]
    all_to_all x1, blocking collectives: 19.1 us -> 17.7 us  [shards(): lax.all_to_all(packet, 'dev', split_axis=0, concat_axis=0, tiled=True)]
  transfers between devices with their start and end apart: 2 -> 4, of which waited for: 2 -> 3; matrix products, arithmetic and copies ran while one was open for 2% -> 2% of each run, Pallas kernels for 10% -> 10%
where the time goes in v6:
time: 53.7 us; the launch traced here: 53.3 us
  blocking collectives  28.3 us (53%)
  Pallas kernels  12.6 us (23%)
  starting transfers between devices  5.54 us (10%)
  waiting for transfers between devices  3.84 us (7%)
  other arithmetic  1.74 us (3%)
  between operations  0.7 us (1%)
    all_to_all x1, blocking collectives, shards(): lax.all_to_all(packet, 'dev', split_axis=0, concat_axis=0, tiled=True)  17.7 us
    all_to_all x1, blocking collectives, shards(): lax.all_to_all(jnp.stack(rows, axis=1), ('grp', 'dev'), split_axis=0, con...  10.6 us
    pallas_call x1, Pallas kernels, shards(): pl.pallas_call(functools.partial(macro_kernel, layers, base), name='macro...  5.56 us
    pallas_call x1, Pallas kernels, shards(): pl.pallas_call(functools.partial(micro_kernel, local, local_count, layers...  4.87 us
    all_to_all x1, starting transfers between devices, shards(): lax.all_to_all(jnp.stack(sents, axis=1), 'dev', split_axis=0, concat_axis...  3.45 us
    pallas_call x1, Pallas kernels, shards(): pl.pallas_call(functools.partial(pack_kernel, layers), name='pack', out_s...  2.18 us
    ppermute x1, waiting for transfers between devices, shards(): lax.ppermute(own_tail, 'grp', [(i, i ^ 1) for i in range(groups)])  1.88 us
    ppermute x1, waiting for transfers between devices, shards(): tails.append(lax.ppermute(own_tail, ('grp', 'dev'), flips))  1.76 us
  transfers between devices with their start and end apart: 4, of which 3 were waited for; matrix products, arithmetic and copies ran while one was open for 2% of the time, Pallas kernels for 10%

profile of v6, /device:TPU:0, one launch (start us, length us, event | category | flops | bytes accessed | tf_op | source)
XLA Modules:
  0.0 53.3 jit_solution(18430688350850558153)
XLA Ops:
  0.6 2.2 %pack.1 = f32[8,80,128]{2,1,0:T(8,128)} custom-call(f32[192,32]{1,0:T(8,128)} %bitcast.33, s32[64,32]{1,0:T(8,128)} %bitcast.37, f32[192,32]{1,0:T(8,128)} %bitcast.34, bf16[8,1,4,1024]{3,2,1,0:T(4,128)(2,1)} %bitcast.35, bf16[8,1,4,1024]{3,2,1,0:T(4,128)(2,1)} %bitcast.36), custom_call_target="tpu_custom_call" | custom-call | tf_op jit(solution)/shard_map/pack/pallas_call | solution.py:602
  2.8 0.0 copy-start.1
  2.8 17.7 %all_to_all.15 = f32[8,80,128]{2,1,0:T(8,128)} all-to-all(f32[8,80,128]{2,1,0:T(8,128)} %pack.1), channel_id=1, replica_groups=mesh['grp'=4,'dev'=8] {'dev'}, dimensions={0} | all-to-all | bytes 655360 | tf_op jit(solution)/shard_map/all_to_all | solution.py:616
  20.5 0.0 copy-start
  20.5 0.0 copy-start.2
  20.5 4.9 %micro.1 = (bf16[8,24,1024]{2,1,0:T(8,128)(2,1)}, f32[32,16]{1,0:T(8,128)}) custom-call(s32[32]{0:T(128)} %steps_hbm.1, f32[640,128]{1,0:T(8,128)} %bitcast.23, f32[8,16,256]{2,1,0:T(8,128)} %constant.20.clone.mult_hbm, bf16[2,64,64]{2,1,0:T(8,128)(2,1)} %constant.21.clone.fwd_hbm, bf16[2,192,192]{2,1,0:T(8,128)(2,1)} %constant.22.clone.bwd_hbm, ...), custom_call_target="tpu_custom_call" | custom-call | tf_op jit(solution)/shard_map/micro/pallas_call | solution.py:626
  25.4 10.6 %all_to_all.16 = f32[32,1,16]{2,1,0:T(1,128)S(1)} all-to-all(f32[32,1,16]{2,1,0:T(1,128)} %bitcast.38), channel_id=1, replica_groups=mesh['grp'=4,'dev'=8] {'grp','dev'}, dimensions={0} | all-to-all | bytes 4096 | tf_op jit(solution)/shard_map/all_to_all | solution.py:655
  36.0 3.5 %all-to-all-start.2 = ((bf16[8,1,24,1024]{3,2,1,0:T(8,128)(2,1)}), bf16[8,1,24,1024]{3,2,1,0:T(8,128)(2,1)S(1)}, u32[]{:S(2)}, u32[]{:S(2)}) async-start(bf16[8,1,24,1024]{3,2,1,0:T(8,128)(2,1)} %bitcast.32), calls=%async_computation.2 | async-start | bytes 786432 | tf_op jit(solution)/shard_map/all_to_all | solution.py:658
  39.5 0.0 copy-done
  39.5 0.6 %collective-permute-start.2 = (f32[128,128]{1,0:T(8,128)S(1)}, f32[128,128]{1,0:T(8,128)S(1)}, u32[]{:S(2)}, u32[]{:S(2)}) collective-permute-start(f32[128,128]{1,0:T(8,128)S(1)} %bitcast.25), channel_id=1, source_target_pairs={{0,9},{1,8},{2,11},{3,10},{4,13},{5,12},{6,15},{7,14},{8,1},{9,0},... | collective-permute-start | bytes 196616 | tf_op jit(solution)/shard_map/ppermute | solution.py:621
  40.2 1.4 %collective-permute-start.1 = (f32[128,128]{1,0:T(8,128)S(1)}, f32[128,128]{1,0:T(8,128)S(1)}, u32[]{:S(2)}, u32[]{:S(2)}) collective-permute-start(f32[128,128]{1,0:T(8,128)S(1)} %bitcast.26), channel_id=1, source_target_pairs={{0,8},{8,0},{16,24},{24,16},{1,9},{9,1},{17,25},{25,17},{2,10},{10... | collective-permute-start | bytes 196616 | tf_op jit(solution)/shard_map/ppermute | solution.py:619
  41.6 0.0 collective-permute-start
  41.6 0.1 slice_bitcast_fusion
  41.7 0.1 copy.18
  41.8 1.8 %collective-permute-done.2.across_ref = f32[128,128]{1,0:T(8,128)S(1)} collective-permute-done((f32[128,128]{1,0:T(8,128)S(1)}, f32[128,128]{1,0:T(8,128)S(1)}, u32[]{:S(2)}, u32[]{:S(2)}) %collective-permute-start.2) | collective-permute-done | bytes 65568 | tf_op jit(solution)/shard_map/ppermute | solution.py:621
  43.5 1.9 %collective-permute-done.1.side_ref = f32[128,128]{1,0:T(8,128)S(1)} collective-permute-done((f32[128,128]{1,0:T(8,128)S(1)}, f32[128,128]{1,0:T(8,128)S(1)}, u32[]{:S(2)}, u32[]{:S(2)}) %collective-permute-start.1) | collective-permute-done | bytes 65568 | tf_op jit(solution)/shard_map/ppermute | solution.py:619
  45.4 0.0 collective-permute-done.core_ref
  45.4 0.0 copy-done.1
  45.4 5.6 %macro.1 = (f32[3,2,1024]{2,1,0:T(2,128)S(1)}, f32[1,8]{1,0:T(1,128)}) custom-call(s32[32]{0:T(128)S(1)} %copy-done.1, f32[32,16]{1,0:T(8,128)S(1)} %bitcast.30, f32[32,16]{1,0:T(8,128)S(1)} %bitcast.31, f32[640,128]{1,0:T(8,128)S(1)} %bitcast.24, f32[128,128]{1,0:T(8,128)S(1)} %bitcast.28, f32[128,128]{1,0:T(8,128)S(1)} %collective-permute-done.core_ref, ...), custom_call_target="tpu_custom_call" | custom-call | tf_op jit(solution)/shard_map/macro/pallas_call | solution.py:663
  51.0 0.1 reshape.46
  51.1 0.0 copy-done.2
  51.1 0.7 %add.14 = f32[3,2,32,32]{3,2,1,0:T(8,128)} add(f32[3,2,32,32]{3,2,1,0:T(8,128)S(1)} %copy-done.2, f32[3,2,32,32]{3,2,1,0:T(8,128)S(1)} %reshape.46) | non-fusion elementwise | flops 6144 | bytes 73728 | tf_op jit(solution)/shard_map/add | solution.py:680
  51.8 0.2 all-to-all-done.2
  52.0 0.2 reshape.47
  52.2 1.1 %bitcast_add_fusion = f32[6,8,4,1024]{3,2,1,0:T(4,128)} fusion(f32[8,6,4,1024]{3,2,1,0:T(4,128)S(1)} %reshape.47, f32[6,8]{1,0:T(8,128)S(1)} %copy.18), kind=kLoop, calls=%fused_computation | loop fusion | flops 196608 | bytes 1573056 | tf_op jit(solution)/shard_map/add | solution.py:662
  (2 shorter events, 0.0 us)
Async XLA Ops:
  2.8 42.6 %copy-start.1 = (s32[32]{0:T(128)S(1)}, s32[32]{0:T(128)}, u32[]{:S(2)}) copy-start(s32[32]{0:T(128)} %slots_ref.1) | copy-start | bytes 388
  20.5 19.0 %copy-start = (f32[8,80,128]{2,1,0:T(8,128)S(1)}, f32[8,80,128]{2,1,0:T(8,128)}, u32[]{:S(2)}) copy-start(f32[8,80,128]{2,1,0:T(8,128)} %all_to_all.15) | copy-start | bytes 983044
  20.5 30.6 %copy-start.2 = (f32[3,2,32,32]{3,2,1,0:T(8,128)S(1)}, f32[3,2,32,32]{3,2,1,0:T(8,128)}, u32[]{:S(2)}) copy-start(f32[3,2,32,32]{3,2,1,0:T(8,128)} %param.11) | copy-start | bytes 73732
  36.0 15.9 %all-to-all-start.2 = ((bf16[8,1,24,1024]{3,2,1,0:T(8,128)(2,1)}), bf16[8,1,24,1024]{3,2,1,0:T(8,128)(2,1)S(1)}, u32[]{:S(2)}, u32[]{:S(2)}) async-start(bf16[8,1,24,1024]{3,2,1,0:T(8,128)(2,1)} %bitcast.32), calls=%async_computation.2 | async-start | bytes 786432 | tf_op jit(solution)/shard_map/all_to_all | solution.py:658
  39.5 4.0 %collective-permute-start.2 = (f32[128,128]{1,0:T(8,128)S(1)}, f32[128,128]{1,0:T(8,128)S(1)}, u32[]{:S(2)}, u32[]{:S(2)}) collective-permute-start(f32[128,128]{1,0:T(8,128)S(1)} %bitcast.25), channel_id=1, source_target_pairs={{0,9},{1,8},{2,11},{3,10},{4,13},{5,12},{6,15},{7,14},{8,1},{9,0},... | collective-permute-start | bytes 196616 | tf_op jit(solution)/shard_map/ppermute | solution.py:621
  40.2 5.2 %collective-permute-start.1 = (f32[128,128]{1,0:T(8,128)S(1)}, f32[128,128]{1,0:T(8,128)S(1)}, u32[]{:S(2)}, u32[]{:S(2)}) collective-permute-start(f32[128,128]{1,0:T(8,128)S(1)} %bitcast.26), channel_id=1, source_target_pairs={{0,8},{8,0},{16,24},{24,16},{1,9},{9,1},{17,25},{25,17},{2,10},{10... | collective-permute-start | bytes 196616 | tf_op jit(solution)/shard_map/ppermute | solution.py:619
  41.6 3.8 %collective-permute-start = (f32[128,128]{1,0:T(8,128)S(1)}, f32[128,128]{1,0:T(8,128)S(1)}, u32[]{:S(2)}, u32[]{:S(2)}) collective-permute-start(f32[128,128]{1,0:T(8,128)S(1)} %bitcast.27), channel_id=1, source_target_pairs={{0,1},{1,0},{2,3},{3,2},{4,5},{5,4},{6,7},{7,6},{8,9},{9,8},{10,11... | collective-permute-start | bytes 196616 | tf_op jit(solution)/shard_map/ppermute | solution.py:618

commit v7 on v6

--- a/solution.py
+++ b/solution.py
@@ -43,7 +43,7 @@
     plane = np.einsum("ypek,zql->eyzqpkl", folded, by_parity).reshape(2, half * vox, half * vox)
     line = basis.T
     forward_line = np.kron(np.eye(2), line)
-    backward_line = np.kron(np.eye(6), line.T)
+    backward_line = np.kron(np.eye(2), line.T)
     wave = np.sin(2.0 * np.pi * np.arange(half) / vox)
     wave[0] = 0.0
     first = np.broadcast_to(wave[:, None, None], (half, half, half))
@@ -366,8 +366,6 @@
     for copy in copies:
         copy.start()
     own = (lax.axis_index("grp") * lax.axis_size("dev") + lax.axis_index("dev")) * local_count + local
-    copies[1].wait()
-    steps = steps_ref[own]
     copies[0].wait()
     tiles = columns // LANES
     step = packet_ref.shape[0] // devices
@@ -396,6 +394,8 @@
     load = [
         (sums[c] + total(jnp.where(mine, part, 0.0))) / sums[6] for c, part in enumerate(strain_from(following))
     ]
+    copies[1].wait()
+    steps = steps_ref[own]
     trace, dev = deviator_of(load)
     lame = moduli[0]
     shear = moduli[1]
@@ -403,7 +403,7 @@
     left, _ = remaining(shear, jnp.broadcast_to(size, shear.shape), steps, 4)
     bulk = lame + (2.0 / 3.0) * shear
     sources = jnp.concatenate([bulk * trace, 2.0 * shear * left], axis=0)
-    for copy in copies[2:]:
+    for copy in copies[2:7]:
         copy.wait()
     spectral = table_by(fwd_ref[0], fwd_ref[1], forward_plane(sources, table))
 
@@ -417,6 +417,7 @@
         return jnp.concatenate([spectral[rows, lanes] for lanes in pieces], axis=1)
 
     parities = [(px, py, pz) for px in range(2) for py in range(2) for pz in range(2)]
+    copies[7].wait()
     product = [mult_ref[i] for i in range(6)]
     inverse = mult_ref[6]
     scaled = mult_ref[7]
@@ -452,7 +453,11 @@
             rows, pieces = block(index, *parity)
             for fold, lanes in enumerate(pieces):
                 spectrum[rows, lanes] = value[:, fold * quarter // 2 : (fold + 1) * quarter // 2]
-    moved = table_by(bwd_ref[0], bwd_ref[1], backward_plane(spectrum[...], table))
+    lines = backward_plane(spectrum[...], table)
+    copies[8].wait()
+    moved = jnp.concatenate(
+        [table_by(bwd_ref[0], bwd_ref[1], lines[i * vox : (i + 2) * vox]) for i in range(0, 6, 2)], axis=0
+    )
     if 2 * planes == 8:
         low = row_position((2 * planes, columns)) < planes
         for pair in range(3):

time: 53.7 us -> 53.6 us (level)
  no operation moved by 1% of the time
where the time goes in v7:
time: 53.6 us; the launch traced here: 53.2 us
  blocking collectives  28.4 us (53%)
  Pallas kernels  12.5 us (23%)
  starting transfers between devices  5.54 us (10%)
  waiting for transfers between devices  3.84 us (7%)
  other arithmetic  1.74 us (3%)
  between operations  0.7 us (1%)
    all_to_all x1, blocking collectives, shards(): lax.all_to_all(packet, 'dev', split_axis=0, concat_axis=0, tiled=True)  17.7 us
    all_to_all x1, blocking collectives, shards(): lax.all_to_all(jnp.stack(rows, axis=1), ('grp', 'dev'), split_axis=0, con...  10.6 us
    pallas_call x1, Pallas kernels, shards(): pl.pallas_call(functools.partial(macro_kernel, layers, base), name='macro...  5.56 us
    pallas_call x1, Pallas kernels, shards(): pl.pallas_call(functools.partial(micro_kernel, local, local_count, layers...  4.8 us
    all_to_all x1, starting transfers between devices, shards(): lax.all_to_all(jnp.stack(sents, axis=1), 'dev', split_axis=0, concat_axis...  3.45 us
    pallas_call x1, Pallas kernels, shards(): pl.pallas_call(functools.partial(pack_kernel, layers), name='pack', out_s...  2.18 us
    ppermute x1, waiting for transfers between devices, shards(): lax.ppermute(own_tail, 'grp', [(i, i ^ 1) for i in range(groups)])  1.88 us
    ppermute x1, waiting for transfers between devices, shards(): tails.append(lax.ppermute(own_tail, ('grp', 'dev'), flips))  1.76 us
  transfers between devices with their start and end apart: 4, of which 3 were waited for; matrix products, arithmetic and copies ran while one was open for 2% of the time, Pallas kernels for 10%

profile of v7, /device:TPU:0, one launch (start us, length us, event | category | flops | bytes accessed | tf_op | source)
XLA Modules:
  0.0 53.2 jit_solution(16308223782687067356)
XLA Ops:
  0.6 2.2 %pack.1 = f32[8,80,128]{2,1,0:T(8,128)} custom-call(f32[192,32]{1,0:T(8,128)} %bitcast.33, s32[64,32]{1,0:T(8,128)} %bitcast.37, f32[192,32]{1,0:T(8,128)} %bitcast.34, bf16[8,1,4,1024]{3,2,1,0:T(4,128)(2,1)} %bitcast.35, bf16[8,1,4,1024]{3,2,1,0:T(4,128)(2,1)} %bitcast.36), custom_call_target="tpu_custom_call" | custom-call | tf_op jit(solution)/shard_map/pack/pallas_call | solution.py:607
  2.8 0.0 copy-start.1
  2.8 17.7 %all_to_all.15 = f32[8,80,128]{2,1,0:T(8,128)} all-to-all(f32[8,80,128]{2,1,0:T(8,128)} %pack.1), channel_id=1, replica_groups=mesh['grp'=4,'dev'=8] {'dev'}, dimensions={0} | all-to-all | bytes 655360 | tf_op jit(solution)/shard_map/all_to_all | solution.py:621
  20.5 0.0 copy-start
  20.5 0.0 copy-start.2
  20.5 4.8 %micro.1 = (bf16[8,24,1024]{2,1,0:T(8,128)(2,1)}, f32[32,16]{1,0:T(8,128)}) custom-call(s32[32]{0:T(128)} %steps_hbm.1, f32[640,128]{1,0:T(8,128)} %bitcast.23, f32[8,16,256]{2,1,0:T(8,128)} %constant.20.clone.mult_hbm, bf16[2,64,64]{2,1,0:T(8,128)(2,1)} %constant.21.clone.fwd_hbm, bf16[2,64,64]{2,1,0:T(8,128)(2,1)} %constant.22.clone.bwd_hbm, ...), custom_call_target="tpu_custom_call" | custom-call | tf_op jit(solution)/shard_map/micro/pallas_call | solution.py:631
  25.3 10.6 %all_to_all.16 = f32[32,1,16]{2,1,0:T(1,128)S(1)} all-to-all(f32[32,1,16]{2,1,0:T(1,128)} %bitcast.38), channel_id=1, replica_groups=mesh['grp'=4,'dev'=8] {'grp','dev'}, dimensions={0} | all-to-all | bytes 4096 | tf_op jit(solution)/shard_map/all_to_all | solution.py:660
  36.0 3.5 %all-to-all-start.2 = ((bf16[8,1,24,1024]{3,2,1,0:T(8,128)(2,1)}), bf16[8,1,24,1024]{3,2,1,0:T(8,128)(2,1)S(1)}, u32[]{:S(2)}, u32[]{:S(2)}) async-start(bf16[8,1,24,1024]{3,2,1,0:T(8,128)(2,1)} %bitcast.32), calls=%async_computation.2 | async-start | bytes 786432 | tf_op jit(solution)/shard_map/all_to_all | solution.py:663
  39.4 0.0 copy-done
  39.5 0.6 %collective-permute-start.2 = (f32[128,128]{1,0:T(8,128)S(1)}, f32[128,128]{1,0:T(8,128)S(1)}, u32[]{:S(2)}, u32[]{:S(2)}) collective-permute-start(f32[128,128]{1,0:T(8,128)S(1)} %bitcast.25), channel_id=1, source_target_pairs={{0,9},{1,8},{2,11},{3,10},{4,13},{5,12},{6,15},{7,14},{8,1},{9,0},... | collective-permute-start | bytes 196616 | tf_op jit(solution)/shard_map/ppermute | solution.py:626
  40.1 1.4 %collective-permute-start.1 = (f32[128,128]{1,0:T(8,128)S(1)}, f32[128,128]{1,0:T(8,128)S(1)}, u32[]{:S(2)}, u32[]{:S(2)}) collective-permute-start(f32[128,128]{1,0:T(8,128)S(1)} %bitcast.26), channel_id=1, source_target_pairs={{0,8},{8,0},{16,24},{24,16},{1,9},{9,1},{17,25},{25,17},{2,10},{10... | collective-permute-start | bytes 196616 | tf_op jit(solution)/shard_map/ppermute | solution.py:624
  41.6 0.0 collective-permute-start
  41.6 0.1 slice_bitcast_fusion
  41.6 0.1 copy.18
  41.7 1.8 %collective-permute-done.2.across_ref = f32[128,128]{1,0:T(8,128)S(1)} collective-permute-done((f32[128,128]{1,0:T(8,128)S(1)}, f32[128,128]{1,0:T(8,128)S(1)}, u32[]{:S(2)}, u32[]{:S(2)}) %collective-permute-start.2) | collective-permute-done | bytes 65568 | tf_op jit(solution)/shard_map/ppermute | solution.py:626
  43.5 1.9 %collective-permute-done.1.side_ref = f32[128,128]{1,0:T(8,128)S(1)} collective-permute-done((f32[128,128]{1,0:T(8,128)S(1)}, f32[128,128]{1,0:T(8,128)S(1)}, u32[]{:S(2)}, u32[]{:S(2)}) %collective-permute-start.1) | collective-permute-done | bytes 65568 | tf_op jit(solution)/shard_map/ppermute | solution.py:624
  45.4 0.0 collective-permute-done.core_ref
  45.4 0.0 copy-done.1
  45.4 5.6 %macro.1 = (f32[3,2,1024]{2,1,0:T(2,128)S(1)}, f32[1,8]{1,0:T(1,128)}) custom-call(s32[32]{0:T(128)S(1)} %copy-done.1, f32[32,16]{1,0:T(8,128)S(1)} %bitcast.30, f32[32,16]{1,0:T(8,128)S(1)} %bitcast.31, f32[640,128]{1,0:T(8,128)S(1)} %bitcast.24, f32[128,128]{1,0:T(8,128)S(1)} %bitcast.28, f32[128,128]{1,0:T(8,128)S(1)} %collective-permute-done.core_ref, ...), custom_call_target="tpu_custom_call" | custom-call | tf_op jit(solution)/shard_map/macro/pallas_call | solution.py:668
  50.9 0.1 reshape.46
  51.0 0.0 copy-done.2
  51.1 0.7 %add.14 = f32[3,2,32,32]{3,2,1,0:T(8,128)} add(f32[3,2,32,32]{3,2,1,0:T(8,128)S(1)} %copy-done.2, f32[3,2,32,32]{3,2,1,0:T(8,128)S(1)} %reshape.46) | non-fusion elementwise | flops 6144 | bytes 73728 | tf_op jit(solution)/shard_map/add | solution.py:685
  51.7 0.2 all-to-all-done.2
  51.9 0.2 reshape.47
  52.2 1.1 %bitcast_add_fusion = f32[6,8,4,1024]{3,2,1,0:T(4,128)} fusion(f32[8,6,4,1024]{3,2,1,0:T(4,128)S(1)} %reshape.47, f32[6,8]{1,0:T(8,128)S(1)} %copy.18), kind=kLoop, calls=%fused_computation | loop fusion | flops 196608 | bytes 1573056 | tf_op jit(solution)/shard_map/add | solution.py:667
  (2 shorter events, 0.0 us)
Async XLA Ops:
  2.8 42.6 %copy-start.1 = (s32[32]{0:T(128)S(1)}, s32[32]{0:T(128)}, u32[]{:S(2)}) copy-start(s32[32]{0:T(128)} %slots_ref.1) | copy-start | bytes 388
  20.5 18.9 %copy-start = (f32[8,80,128]{2,1,0:T(8,128)S(1)}, f32[8,80,128]{2,1,0:T(8,128)}, u32[]{:S(2)}) copy-start(f32[8,80,128]{2,1,0:T(8,128)} %all_to_all.15) | copy-start | bytes 983044
  20.5 30.5 %copy-start.2 = (f32[3,2,32,32]{3,2,1,0:T(8,128)S(1)}, f32[3,2,32,32]{3,2,1,0:T(8,128)}, u32[]{:S(2)}) copy-start(f32[3,2,32,32]{3,2,1,0:T(8,128)} %param.11) | copy-start | bytes 73732
  36.0 15.9 %all-to-all-start.2 = ((bf16[8,1,24,1024]{3,2,1,0:T(8,128)(2,1)}), bf16[8,1,24,1024]{3,2,1,0:T(8,128)(2,1)S(1)}, u32[]{:S(2)}, u32[]{:S(2)}) async-start(bf16[8,1,24,1024]{3,2,1,0:T(8,128)(2,1)} %bitcast.32), calls=%async_computation.2 | async-start | bytes 786432 | tf_op jit(solution)/shard_map/all_to_all | solution.py:663
  39.5 4.0 %collective-permute-start.2 = (f32[128,128]{1,0:T(8,128)S(1)}, f32[128,128]{1,0:T(8,128)S(1)}, u32[]{:S(2)}, u32[]{:S(2)}) collective-permute-start(f32[128,128]{1,0:T(8,128)S(1)} %bitcast.25), channel_id=1, source_target_pairs={{0,9},{1,8},{2,11},{3,10},{4,13},{5,12},{6,15},{7,14},{8,1},{9,0},... | collective-permute-start | bytes 196616 | tf_op jit(solution)/shard_map/ppermute | solution.py:626
  40.1 5.2 %collective-permute-start.1 = (f32[128,128]{1,0:T(8,128)S(1)}, f32[128,128]{1,0:T(8,128)S(1)}, u32[]{:S(2)}, u32[]{:S(2)}) collective-permute-start(f32[128,128]{1,0:T(8,128)S(1)} %bitcast.26), channel_id=1, source_target_pairs={{0,8},{8,0},{16,24},{24,16},{1,9},{9,1},{17,25},{25,17},{2,10},{10... | collective-permute-start | bytes 196616 | tf_op jit(solution)/shard_map/ppermute | solution.py:624
  41.6 3.8 %collective-permute-start = (f32[128,128]{1,0:T(8,128)S(1)}, f32[128,128]{1,0:T(8,128)S(1)}, u32[]{:S(2)}, u32[]{:S(2)}) collective-permute-start(f32[128,128]{1,0:T(8,128)S(1)} %bitcast.27), channel_id=1, source_target_pairs={{0,1},{1,0},{2,3},{3,2},{4,5},{5,4},{6,7},{7,6},{8,9},{9,8},{10,11... | collective-permute-start | bytes 196616 | tf_op jit(solution)/shard_map/ppermute | solution.py:623

commit v8 on v7

--- a/solution.py
+++ b/solution.py
@@ -214,11 +214,16 @@
 def remaining(shear, size, steps, most):
     stiff = (2.0 * shear) * (2.0 * shear) * size
 
-    def relax(count, left):
-        ratio = stiff * left * left
-        return left * ((1.0 - relax_rate) + relax_rate / (1.0 + ratio))
-
-    left = lax.fori_loop(0, steps, relax, jnp.ones_like(stiff))
+    rows = 8 if stiff.shape[0] % 8 == 0 else stiff.shape[0]
+    lefts = []
+    for top in range(0, stiff.shape[0], rows):
+        part = stiff[top : top + rows]
+
+        def relax(count, left, part=part):
+            return left * ((1.0 - relax_rate) + relax_rate / (1.0 + part * left * left))
+
+        lefts.append(lax.fori_loop(0, steps, relax, jnp.ones_like(part)))
+    left = jnp.concatenate(lefts, axis=0)
     return left, stiff * left * left
 
 

time: 53.6 us -> 53.7 us (level)
  no operation moved by 1% of the time
where the time goes in v8:
time: 53.7 us; the launch traced here: 53.3 us
  blocking collectives  28.3 us (53%)
  Pallas kernels  12.7 us (24%)
  starting transfers between devices  5.54 us (10%)
  waiting for transfers between devices  3.84 us (7%)
  other arithmetic  1.74 us (3%)
  between operations  0.7 us (1%)
    all_to_all x1, blocking collectives, shards(): lax.all_to_all(packet, 'dev', split_axis=0, concat_axis=0, tiled=True)  17.7 us
    all_to_all x1, blocking collectives, shards(): lax.all_to_all(jnp.stack(rows, axis=1), ('grp', 'dev'), split_axis=0, con...  10.6 us
    pallas_call x1, Pallas kernels, shards(): pl.pallas_call(functools.partial(macro_kernel, layers, base), name='macro...  5.56 us
    pallas_call x1, Pallas kernels, shards(): pl.pallas_call(functools.partial(micro_kernel, local, local_count, layers...  4.92 us
    all_to_all x1, starting transfers between devices, shards(): lax.all_to_all(jnp.stack(sents, axis=1), 'dev', split_axis=0, concat_axis...  3.45 us
    pallas_call x1, Pallas kernels, shards(): pl.pallas_call(functools.partial(pack_kernel, layers), name='pack', out_s...  2.18 us
    ppermute x1, waiting for transfers between devices, shards(): lax.ppermute(own_tail, 'grp', [(i, i ^ 1) for i in range(groups)])  1.88 us
    ppermute x1, waiting for transfers between devices, shards(): tails.append(lax.ppermute(own_tail, ('grp', 'dev'), flips))  1.76 us
  transfers between devices with their start and end apart: 4, of which 3 were waited for; matrix products, arithmetic and copies ran while one was open for 2% of the time, Pallas kernels for 10%

profile of v8, /device:TPU:0, one launch (start us, length us, event | category | flops | bytes accessed | tf_op | source)
XLA Modules:
  0.0 53.3 jit_solution(859260571485185142)
XLA Ops:
  0.6 2.2 %pack.1 = f32[8,80,128]{2,1,0:T(8,128)} custom-call(f32[192,32]{1,0:T(8,128)} %bitcast.33, s32[64,32]{1,0:T(8,128)} %bitcast.37, f32[192,32]{1,0:T(8,128)} %bitcast.34, bf16[8,1,4,1024]{3,2,1,0:T(4,128)(2,1)} %bitcast.35, bf16[8,1,4,1024]{3,2,1,0:T(4,128)(2,1)} %bitcast.36), custom_call_target="tpu_custom_call" | custom-call | tf_op jit(solution)/shard_map/pack/pallas_call | solution.py:612
  2.8 0.0 copy-start.1
  2.8 17.7 %all_to_all.15 = f32[8,80,128]{2,1,0:T(8,128)} all-to-all(f32[8,80,128]{2,1,0:T(8,128)} %pack.1), channel_id=1, replica_groups=mesh['grp'=4,'dev'=8] {'dev'}, dimensions={0} | all-to-all | bytes 655360 | tf_op jit(solution)/shard_map/all_to_all | solution.py:626
  20.5 0.0 copy-start
  20.5 0.0 copy-start.2
  20.5 4.9 %micro.1 = (bf16[8,24,1024]{2,1,0:T(8,128)(2,1)}, f32[32,16]{1,0:T(8,128)}) custom-call(s32[32]{0:T(128)} %steps_hbm.1, f32[640,128]{1,0:T(8,128)} %bitcast.23, f32[8,16,256]{2,1,0:T(8,128)} %constant.20.clone.mult_hbm, bf16[2,64,64]{2,1,0:T(8,128)(2,1)} %constant.21.clone.fwd_hbm, bf16[2,64,64]{2,1,0:T(8,128)(2,1)} %constant.22.clone.bwd_hbm, ...), custom_call_target="tpu_custom_call" | custom-call | tf_op jit(solution)/shard_map/micro/pallas_call | solution.py:636
  25.5 10.6 %all_to_all.16 = f32[32,1,16]{2,1,0:T(1,128)S(1)} all-to-all(f32[32,1,16]{2,1,0:T(1,128)} %bitcast.38), channel_id=1, replica_groups=mesh['grp'=4,'dev'=8] {'grp','dev'}, dimensions={0} | all-to-all | bytes 4096 | tf_op jit(solution)/shard_map/all_to_all | solution.py:665
  36.0 3.5 %all-to-all-start.2 = ((bf16[8,1,24,1024]{3,2,1,0:T(8,128)(2,1)}), bf16[8,1,24,1024]{3,2,1,0:T(8,128)(2,1)S(1)}, u32[]{:S(2)}, u32[]{:S(2)}) async-start(bf16[8,1,24,1024]{3,2,1,0:T(8,128)(2,1)} %bitcast.32), calls=%async_computation.2 | async-start | bytes 786432 | tf_op jit(solution)/shard_map/all_to_all | solution.py:668
  39.5 0.0 copy-done
  39.5 0.6 %collective-permute-start.2 = (f32[128,128]{1,0:T(8,128)S(1)}, f32[128,128]{1,0:T(8,128)S(1)}, u32[]{:S(2)}, u32[]{:S(2)}) collective-permute-start(f32[128,128]{1,0:T(8,128)S(1)} %bitcast.25), channel_id=1, source_target_pairs={{0,9},{1,8},{2,11},{3,10},{4,13},{5,12},{6,15},{7,14},{8,1},{9,0},... | collective-permute-start | bytes 196616 | tf_op jit(solution)/shard_map/ppermute | solution.py:631
  40.2 1.4 %collective-permute-start.1 = (f32[128,128]{1,0:T(8,128)S(1)}, f32[128,128]{1,0:T(8,128)S(1)}, u32[]{:S(2)}, u32[]{:S(2)}) collective-permute-start(f32[128,128]{1,0:T(8,128)S(1)} %bitcast.26), channel_id=1, source_target_pairs={{0,8},{8,0},{16,24},{24,16},{1,9},{9,1},{17,25},{25,17},{2,10},{10... | collective-permute-start | bytes 196616 | tf_op jit(solution)/shard_map/ppermute | solution.py:629
  41.6 0.0 collective-permute-start
  41.6 0.1 slice_bitcast_fusion
  41.7 0.1 copy.18
  41.8 1.8 %collective-permute-done.2.across_ref = f32[128,128]{1,0:T(8,128)S(1)} collective-permute-done((f32[128,128]{1,0:T(8,128)S(1)}, f32[128,128]{1,0:T(8,128)S(1)}, u32[]{:S(2)}, u32[]{:S(2)}) %collective-permute-start.2) | collective-permute-done | bytes 65568 | tf_op jit(solution)/shard_map/ppermute | solution.py:631
  43.5 1.9 %collective-permute-done.1.side_ref = f32[128,128]{1,0:T(8,128)S(1)} collective-permute-done((f32[128,128]{1,0:T(8,128)S(1)}, f32[128,128]{1,0:T(8,128)S(1)}, u32[]{:S(2)}, u32[]{:S(2)}) %collective-permute-start.1) | collective-permute-done | bytes 65568 | tf_op jit(solution)/shard_map/ppermute | solution.py:629
  45.4 0.0 collective-permute-done.core_ref
  45.4 0.0 copy-done.1
  45.4 5.6 %macro.1 = (f32[3,2,1024]{2,1,0:T(2,128)S(1)}, f32[1,8]{1,0:T(1,128)}) custom-call(s32[32]{0:T(128)S(1)} %copy-done.1, f32[32,16]{1,0:T(8,128)S(1)} %bitcast.30, f32[32,16]{1,0:T(8,128)S(1)} %bitcast.31, f32[640,128]{1,0:T(8,128)S(1)} %bitcast.24, f32[128,128]{1,0:T(8,128)S(1)} %bitcast.28, f32[128,128]{1,0:T(8,128)S(1)} %collective-permute-done.core_ref, ...), custom_call_target="tpu_custom_call" | custom-call | tf_op jit(solution)/shard_map/macro/pallas_call | solution.py:673
  51.0 0.1 reshape.46
  51.1 0.0 copy-done.2
  51.1 0.7 %add.14 = f32[3,2,32,32]{3,2,1,0:T(8,128)} add(f32[3,2,32,32]{3,2,1,0:T(8,128)S(1)} %copy-done.2, f32[3,2,32,32]{3,2,1,0:T(8,128)S(1)} %reshape.46) | non-fusion elementwise | flops 6144 | bytes 73728 | tf_op jit(solution)/shard_map/add | solution.py:690
  51.8 0.2 all-to-all-done.2
  52.0 0.2 reshape.47
  52.2 1.1 %bitcast_add_fusion = f32[6,8,4,1024]{3,2,1,0:T(4,128)} fusion(f32[8,6,4,1024]{3,2,1,0:T(4,128)S(1)} %reshape.47, f32[6,8]{1,0:T(8,128)S(1)} %copy.18), kind=kLoop, calls=%fused_computation | loop fusion | flops 196608 | bytes 1573056 | tf_op jit(solution)/shard_map/add | solution.py:672
  (2 shorter events, 0.0 us)
Async XLA Ops:
  2.8 42.6 %copy-start.1 = (s32[32]{0:T(128)S(1)}, s32[32]{0:T(128)}, u32[]{:S(2)}) copy-start(s32[32]{0:T(128)} %slots_ref.1) | copy-start | bytes 388
  20.5 19.0 %copy-start = (f32[8,80,128]{2,1,0:T(8,128)S(1)}, f32[8,80,128]{2,1,0:T(8,128)}, u32[]{:S(2)}) copy-start(f32[8,80,128]{2,1,0:T(8,128)} %all_to_all.15) | copy-start | bytes 983044
  20.5 30.6 %copy-start.2 = (f32[3,2,32,32]{3,2,1,0:T(8,128)S(1)}, f32[3,2,32,32]{3,2,1,0:T(8,128)}, u32[]{:S(2)}) copy-start(f32[3,2,32,32]{3,2,1,0:T(8,128)} %param.11) | copy-start | bytes 73732
  36.0 15.9 %all-to-all-start.2 = ((bf16[8,1,24,1024]{3,2,1,0:T(8,128)(2,1)}), bf16[8,1,24,1024]{3,2,1,0:T(8,128)(2,1)S(1)}, u32[]{:S(2)}, u32[]{:S(2)}) async-start(bf16[8,1,24,1024]{3,2,1,0:T(8,128)(2,1)} %bitcast.32), calls=%async_computation.2 | async-start | bytes 786432 | tf_op jit(solution)/shard_map/all_to_all | solution.py:668
  39.5 4.0 %collective-permute-start.2 = (f32[128,128]{1,0:T(8,128)S(1)}, f32[128,128]{1,0:T(8,128)S(1)}, u32[]{:S(2)}, u32[]{:S(2)}) collective-permute-start(f32[128,128]{1,0:T(8,128)S(1)} %bitcast.25), channel_id=1, source_target_pairs={{0,9},{1,8},{2,11},{3,10},{4,13},{5,12},{6,15},{7,14},{8,1},{9,0},... | collective-permute-start | bytes 196616 | tf_op jit(solution)/shard_map/ppermute | solution.py:631
  40.2 5.2 %collective-permute-start.1 = (f32[128,128]{1,0:T(8,128)S(1)}, f32[128,128]{1,0:T(8,128)S(1)}, u32[]{:S(2)}, u32[]{:S(2)}) collective-permute-start(f32[128,128]{1,0:T(8,128)S(1)} %bitcast.26), channel_id=1, source_target_pairs={{0,8},{8,0},{16,24},{24,16},{1,9},{9,1},{17,25},{25,17},{2,10},{10... | collective-permute-start | bytes 196616 | tf_op jit(solution)/shard_map/ppermute | solution.py:629
  41.6 3.8 %collective-permute-start = (f32[128,128]{1,0:T(8,128)S(1)}, f32[128,128]{1,0:T(8,128)S(1)}, u32[]{:S(2)}, u32[]{:S(2)}) collective-permute-start(f32[128,128]{1,0:T(8,128)S(1)} %bitcast.27), channel_id=1, source_target_pairs={{0,1},{1,0},{2,3},{3,2},{4,5},{5,4},{6,7},{7,6},{8,9},{9,8},{10,11... | collective-permute-start | bytes 196616 | tf_op jit(solution)/shard_map/ppermute | solution.py:628
